TPU v7x, 128 devices: a whole 4x4x4 slice. The times are simulated.
128 devices in a mesh: gx: 8 (over x, core), gy: 16 (over z, y).
Axes of the slice: x: 4, y: 4, z: 4, core: 2. Of those that a mesh axis runs over, the one named last changes fastest.
Arguments:
- subvoxel_location_share: float32 [3, 2097152], P(None, ('gx', 'gy')), may hold values from 0.5 to 1.5
- point_motion_vector: float32 [3, 2097152], P(None, ('gx', 'gy')), may hold values from -5 to 5
- linear_gradient_matrix: float32 [9, 2097152], P(None, ('gx', 'gy')), may hold values from -3 to 3
- kirchhoff_tension_matrix: float32 [9, 2097152], P(None, ('gx', 'gy')), may hold values from -5 to 5
- point_inertia_amounts: float32 [2097152], P(('gx', 'gy')), may hold values from 0.5 to 2
- point_thermal_state: float32 [2097152], P(('gx', 'gy')), may hold values from 0.5 to 2
- anchor_voxel_shift: int32 [2097152], P(('gx', 'gy')), may hold values from 0 to 63
- group_resting_volume: int32 [16384], P(('gx', 'gy')), may hold values from 0 to 127
- group_migration_label: int32 [16384], P(('gx', 'gy')), may hold values from 0 to 8, as said below
- cylinder_shell_flag: int32 [32, 64, 512], P('gx', 'gy'), may hold values 0 or 1
- rough_surface_flag: int32 [32, 64, 512], P('gx', 'gy'), may hold values 0 or 1
- voxel_facing_choice: int32 [32, 64, 512], P('gx', 'gy'), may hold values from 0 to 63
- facing_unit_vectors: float32 [3, 64], replicated, may hold values from -1 to 1, as said below
- rim_thermal_level: float32 [32, 64, 512], P('gx', 'gy'), may hold values from 1 to 3
Outputs:
- next_motion_vector: float32 [3, 4194304], P(None, ('gx', 'gy'))
- next_gradient_matrix: float32 [9, 4194304], P(None, ('gx', 'gy'))
- next_thermal_state: float32 [4194304], P(('gx', 'gy'))
- grid_velocity: float32 [3, 32, 64, 512], P(None, 'gx', 'gy')
- grid_temperature: float32 [32, 64, 512], P('gx', 'gy')
Inputs may be any that keep to these rules, and one draw needn't show every extreme that they name: `group_migration_label`: code 3*(dx+1)+(dy+1) sends a block to the tile offset by dx along x and dy along y, with wrap-around; code 4 keeps it. Among the 128 blocks of one tile at most 16 carry any one code other than 4, and in every draw some tile receives exactly 16 blocks from each of its eight neighbours. `anchor_voxel_shift`: the particle's base cell inside its block's brick is (o // 16, o // 4 % 4, o % 4). `facing_unit_vectors`: each column is a unit vector.
All inputs are finite; a program needn't handle non-finite values. No bound on the sum of `cylinder_shell_flag` or of `rough_surface_flag` on one device may be relied on, other than what follows from the above.
Results may differ from a plain program's by a relative error of at most 0.0003.
Values sent between devices are 32-bit elements; how exact they have to be, the bound alone decides.
No kernel may reach another device: no remote copies, remote signals or barrier semaphores. Data moves between devices by JAX's collectives and lax.ppermute only.
A program may use at most 128 MiB of HBM per device.

v0:
```python
import jax
import jax.numpy as jnp
from jax import lax
from jax.experimental import pallas as pl
from jax.experimental.pallas import tpu as pltpu
from jax.sharding import PartitionSpec as P

f32 = jnp.float32
bf16 = jnp.bfloat16
mass_floor = 0.25
slip_floor = 0.1
friction = 0.4
gravity_step = 0.5
conduct = 0.15
stress_coef = 0.25
mib = 1024 * 1024
pieces = 31
tiles = 9
msg_tiles = 13
msg_rows = msg_tiles * 16


def axis_tables(shift, inside, scale):
    near = 0.5 * (1.5 - inside) ** 2
    middle = 0.75 - (inside - 1.0) ** 2
    far = 0.5 * (inside - 0.5) ** 2
    at = [shift == step for step in range(4)]
    zero = jnp.zeros_like(inside)
    weight = [
        jnp.where(at[0], near, zero),
        jnp.where(at[0], middle, jnp.where(at[1], near, zero)),
        jnp.where(at[0], far, jnp.where(at[1], middle, jnp.where(at[2], near, zero))),
        jnp.where(at[1], far, jnp.where(at[2], middle, jnp.where(at[3], near, zero))),
        jnp.where(at[2], far, jnp.where(at[3], middle, zero)),
        jnp.where(at[3], far, zero),
    ]
    place = shift.astype(f32) + inside
    first = [weight[step] * (scale * (step - place)) for step in range(6)]
    return weight, first


def split_two(value):
    high = value.astype(bf16).astype(f32)
    return high, value - high


def deposit_kernel(
    code_s, brick_s, f_hbm, v_hbm, c_hbm, k_hbm, m_hbm, t_hbm, o_hbm,
    own_ref, frac_ref, xm_ref, ym_ref, yp_ref, xp_ref,
    f_ref, v_ref, c_ref, k_ref, m_ref, t_ref, o_ref, sems,
    raw, sa, sb, acc, cnt, out,
):
    pairs = (
        (f_hbm, f_ref), (v_hbm, v_ref), (c_hbm, c_ref), (k_hbm, k_ref),
        (m_hbm, m_ref), (t_hbm, t_ref), (o_hbm, o_ref),
    )
    copies = [pltpu.make_async_copy(a, b, sems.at[n]) for n, (a, b) in enumerate(pairs)]
    for copy in copies:
        copy.start()
    def clear(step, carry):
        acc[pl.ds(pl.multiple_of(step * 256, 256), 256), :] = jnp.zeros((256, 128), f32)
        return carry

    lax.fori_loop(0, 32, clear, 0)
    out[...] = jnp.zeros(out.shape, f32)
    sa[...] = jnp.zeros(sa.shape, f32)
    sb[...] = jnp.zeros(sb.shape, f32)
    for code in range(9):
        cnt[code] = 0
    for copy in copies:
        copy.wait()
    row_no = lax.broadcasted_iota(jnp.int32, (32, 1), 0)

    def group(g, carry):
        for j in range(8):
            lanes = pl.ds(pl.multiple_of((g * 8 + j) * 128, 128), 128)
            raw[j * 40 : j * 40 + 3, :] = f_ref[:, lanes]
            raw[j * 40 + 3 : j * 40 + 6, :] = v_ref[:, lanes]
            raw[j * 40 + 8 : j * 40 + 17, :] = c_ref[:, lanes]
            raw[j * 40 + 24 : j * 40 + 33, :] = k_ref[:, lanes]
        rows = pl.ds(pl.multiple_of(g * 8, 8), 8)
        mass = m_ref[rows, :]
        heat = mass * t_ref[rows, :]
        offset = o_ref[rows, :]

        def get(row):
            return raw[pl.ds(row, 8, stride=40), :]

        inside = [get(d) for d in range(3)]
        for d in range(3):
            frac_ref[d, rows, :] = inside[d]
        wx, rx = axis_tables(offset >> 4, inside[0], 1.0)
        for a in range(3):
            push = mass * get(3 + a)
            q = [
                mass * get(8 + a * 3 + k) - stress_coef * get(24 + a * 3 + k) for k in range(3)
            ]
            for j in range(6):
                sa[pl.ds((a * 6 + j) * 8, 8), :] = push * wx[j] + q[0] * rx[j]
                sa[pl.ds((32 + a * 6 + j) * 8, 8), :] = q[1] * wx[j]
                sa[pl.ds((64 + a * 6 + j) * 8, 8), :] = q[2] * wx[j]
        for j in range(6):
            sa[pl.ds((18 + j) * 8, 8), :] = mass * wx[j]
            sa[pl.ds((24 + j) * 8, 8), :] = heat * wx[j]
        wy, ry = axis_tables((offset >> 2) & 3, inside[1], 1.0)
        wz, rz = axis_tables(offset & 3, inside[2], 1.0)
        for jy in range(6):
            for jz in range(6):
                r = jy * 6 + jz
                sb[pl.ds(r * 8, 8), :] = wy[jy] * wz[jz]
                sb[pl.ds((40 + r) * 8, 8), :] = ry[jy] * wz[jz]
                sb[pl.ds((80 + r) * 8, 8), :] = wy[jy] * rz[jz]
        sums = []
        for j in range(8):
            left = jnp.concatenate(
                [sa[pl.ds(n * 256 + j, 32, stride=8), :] for n in range(3)], axis=1
            )
            right = jnp.concatenate(
                [sb[pl.ds(n * 320 + j, 40, stride=8), :] for n in range(3)], axis=1
            )
            left = jnp.concatenate(split_two(left), axis=0).astype(bf16)
            right = jnp.concatenate(split_two(right), axis=0).astype(bf16)
            both = lax.dot_general(
                left, right, (((1,), (1,)), ((), ())), preferred_element_type=f32
            )
            both = both[:32] + both[32:]
            sums.append(both[:, :40] + both[:, 40:])
        for j in range(8):
            b = g * 8 + j
            code = code_s[b]
            rank = cnt[code]
            cnt[code] = rank + 1
            stays = code == 4
            way = jnp.where(code > 4, code - 1, code)
            brick = brick_s[b]
            target = jnp.where(stays, brick, 128 + way * 16 + rank)
            mark = jnp.where(stays, 0, brick + 1).astype(f32)
            spot = pl.ds(pl.multiple_of(target * 32, 32), 32)
            acc[spot, 0:40] = acc[spot, 0:40] + (sums[j] + jnp.where(row_no == 30, mark, 0.0))
            at = jnp.where(stays, 8 * msg_rows, (way * msg_tiles + 9) * 16 + rank)
            for d in range(3):
                out[pl.ds(at + d * 16, 1), :] = raw[j * 40 + d : j * 40 + d + 1, :]
            out[pl.ds(at + 48, 1), :] = o_ref[pl.ds(b, 1), :].astype(f32)
        return carry

    lax.fori_loop(0, 16, group, 0)
    lane = lax.broadcasted_iota(jnp.int32, (8, 128), 1)

    def packed(chunk):
        total = [jnp.zeros((8, 128), f32) for _ in range(tiles)]
        for i in range(pieces):
            piece = acc[pl.ds(chunk * 256 + i, 8, stride=32), :]
            if i == 30:
                piece = jnp.where(lane < 36, piece, 0.0)
            tile, at = divmod(i * 36, 128)
            if at:
                piece = pltpu.roll(piece, at, 1)
            if at + 36 > 128:
                total[tile] = total[tile] + jnp.where(lane >= at, piece, 0.0)
                total[tile + 1] = total[tile + 1] + jnp.where(lane < at, piece, 0.0)
            else:
                total[tile] = total[tile] + piece
        return total

    def pack_own(chunk, carry):
        for tile, value in enumerate(packed(chunk)):
            own_ref[tile, pl.ds(pl.multiple_of(chunk * 8, 8), 8), :] = value
        return carry

    def pack_out(chunk, carry):
        base = (chunk // 2) * msg_rows + (chunk % 2) * 8
        for tile, value in enumerate(packed(chunk + 16)):
            out[pl.ds(pl.multiple_of(base + tile * 16, 8), 8), :] = value
        return carry

    lax.fori_loop(0, 16, pack_own, 0)
    lax.fori_loop(0, 16, pack_out, 0)
    xm_ref[...] = out[0 : 3 * msg_rows, :]
    ym_ref[...] = out[3 * msg_rows : 4 * msg_rows, :]
    yp_ref[...] = out[4 * msg_rows : 5 * msg_rows, :]
    xp_ref[...] = out[5 * msg_rows : 8 * msg_rows, :]


def runs_left():
    return (
        [(3, x, 0, 4) for x in range(2, 6)]
        + [(4, x, 0, 4) for x in range(2, 6)]
        + [(c, x, 0, 4) for c in range(3) for x in (4, 5)]
    )


def runs_below():
    return (
        [(3, x, 2, 4) for x in range(4)]
        + [(4, x, 2, 4) for x in range(4)]
        + [(c, x, 4, 2) for c in range(3) for x in range(4)]
    )


def runs_diagonal():
    return (
        [(3, x, 2, 4) for x in range(2, 6)]
        + [(4, x, 2, 4) for x in range(2, 6)]
        + [(c, x, 4, 2) for c in range(3) for x in (4, 5)]
    )


def runs_own():
    return [(c, x, 0, 4) for c in range(5) for x in range(4)]


def total_kernel(own_ref, rxp, rxm, ryp, rym, ml, mb, md, mo, brick_ref, wide, grid):
    places = [(ryp, 0), (rxp, 1), (rym, 0), (ryp, 1), (rym, 1), (ryp, 2), (rxm, 1), (rym, 2)]

    def arrived(tile):
        return jnp.concatenate(
            [ref[pl.ds((at * msg_tiles + tile) * 16, 16), :] for ref, at in places], axis=0
        )

    rows = lax.broadcasted_iota(jnp.int32, (128, 128), 0)
    lanes = lax.broadcasted_iota(jnp.int32, (128, 128), 1)
    column = arrived(8)[:, 56:57]
    row = jnp.sum(jnp.where(rows == lanes, column, 0.0), axis=0, keepdims=True)
    brick_ref[...] = row.astype(jnp.int32) - 1
    hits = (row == (rows + 1).astype(f32)).astype(f32).astype(bf16)
    hits = jnp.concatenate([hits, hits], axis=1)
    for tile in range(tiles):
        high, low = split_two(arrived(tile))
        stack = jnp.concatenate([high.astype(bf16), low.astype(bf16)], axis=0)
        value = own_ref[tile] + jnp.dot(hits, stack, preferred_element_type=f32)
        wide[tile * 128 : tile * 128 + 128, :] = jnp.transpose(value)
    lane = lax.broadcasted_iota(jnp.int32, (184, 128), 1)

    def layer(jz):
        return wide[pl.ds(jz, 184, stride=6), :]

    grid[0] = layer(1) + jnp.where(lane == 0, 0.0, pltpu.roll(layer(5), 1, 1))
    grid[1] = layer(2)
    grid[2] = layer(3)
    grid[3] = layer(4) + jnp.where(lane == 127, 0.0, pltpu.roll(layer(0), 127, 1))
    for ref, runs in ((ml, runs_left()), (mb, runs_below()), (md, runs_diagonal()), (mo, runs_own())):
        for kz in range(4):
            to = 0
            for c, x, y, count in runs:
                ref[kz, to : to + count, :] = grid[kz, c * 36 + x * 6 + y : c * 36 + x * 6 + y + count, :]
                to += count
            if to < ref.shape[1]:
                ref[kz, to:, :] = jnp.zeros((ref.shape[1] - to, 128), f32)


def static_kernel(
    table, solid_ref, rough_ref, choice_ref, rim_ref, own, ml, mb, md, cells
):
    for x in range(4):
        rows = slice(x * 4, x * 4 + 4)
        cells[rows, :] = solid_ref[x].astype(f32)
        cells[16 + x * 4 : 20 + x * 4, :] = rough_ref[x].astype(f32)
        cells[32 + x * 4 : 36 + x * 4, :] = choice_ref[x].astype(f32)
        cells[48 + x * 4 : 52 + x * 4, :] = rim_ref[x]
    value = cells[...]
    high, rest = split_two(value[48:64])
    middle, low = split_two(rest)
    value = jnp.concatenate([value[0:48], high, middle, low], axis=0).astype(bf16)
    source = lax.broadcasted_iota(jnp.int32, (512, 512), 0)
    wanted = (source % 4) * 128 + source // 4
    permute = (wanted == lax.broadcasted_iota(jnp.int32, (512, 512), 1)).astype(f32).astype(bf16)
    value = jnp.dot(value, permute, preferred_element_type=f32)
    rim = value[48:64] + value[64:80] + value[80:96]
    choice = value[32:48]
    normal = [jnp.zeros(choice.shape, f32) for _ in range(3)]
    for n in range(table.shape[1]):
        hit = choice == float(n)
        normal = [jnp.where(hit, table[d, n], normal[d]) for d in range(3)]
    for kz in range(4):
        lanes = slice(kz * 128, kz * 128 + 128)
        for field, part in enumerate((value[0:16], rim, value[16:32], *normal)):
            own[kz, field * 16 : field * 16 + 16, :] = part[:, lanes]
        ml[kz, 30:32, :] = jnp.zeros((2, 128), f32)
        mb[kz, 30:32, :] = jnp.zeros((2, 128), f32)
        md[kz, 22:24, :] = jnp.zeros((2, 128), f32)
        for field in range(2):
            for x in range(3):
                at = field * 9 + x * 3
                low_row, high_row = field * 16 + x * 4, field * 16 + x * 4 + 4
                ml[kz, at : at + 3, :] = own[kz, high_row : high_row + 3, :]
                mb[kz, at : at + 3, :] = own[kz, low_row + 1 : low_row + 4, :]
                md[kz, at : at + 3, :] = own[kz, high_row + 1 : high_row + 4, :]
        for field in range(4):
            row = field * 16 + 32
            ml[kz, 18 + field * 3 : 21 + field * 3, :] = own[kz, row + 12 : row + 15, :]
            for x in range(3):
                at = 18 + field * 3 + x
                mb[kz, at : at + 1, :] = own[kz, row + x * 4 + 3 : row + x * 4 + 4, :]
            md[kz, 18 + field : 19 + field, :] = own[kz, row + 15 : row + 16, :]


def update_kernel(
    mo, rl, rb, rd, own, sl, sb, sd, hl, hb, hd, ko, warm, push, region, rough, normal
):
    for kz in range(4):
        for field in range(2):
            to = 3 * field
            for x in range(3):
                at = field * 9 + x * 3
                inner, outer = x * 6, (x + 3) * 6
                row = field * 16 + x * 4
                region[to, kz, inner : inner + 3, :] = sd[kz, at : at + 3, :]
                region[to, kz, inner + 3 : inner + 6, :] = sl[kz, at : at + 3, :]
                region[to, kz, outer : outer + 3, :] = sb[kz, at : at + 3, :]
                region[to, kz, outer + 3 : outer + 6, :] = own[kz, row : row + 3, :]
        for field in range(4):
            ref = rough if field == 0 else normal.at[field - 1]
            at = 18 + field * 3
            row = 32 + field * 16
            ref[kz, 0:1, :] = sd[kz, 18 + field : 19 + field, :]
            ref[kz, 1:4, :] = sl[kz, at : at + 3, :]
            for x in range(3):
                to = (x + 1) * 4
                ref[kz, to : to + 1, :] = sb[kz, at + x : at + x + 1, :]
                ref[kz, to + 1 : to + 4, :] = own[kz, row + x * 4 : row + x * 4 + 3, :]
    warm[...] = jnp.zeros(warm.shape, f32)
    for kz in range(4):
        for ref, dx, dy in ((mo, 2, 2), (rl, 0, 2), (rb, 2, 0), (rd, 0, 0)):
            for c in range(2):
                for x in range(4):
                    at = (48 if ref is mo else 0) + c * 16 + x * 4
                    to = (x + dx) * 6 + dy
                    warm[c, kz, to : to + 4, :] = warm[c, kz, to : to + 4, :] + ref[kz, at : at + 4, :]
        for c in range(3):
            push[c, kz] = mo[kz, c * 16 : c * 16 + 16, :]
            push[c, kz, 0:8, :] = push[c, kz, 0:8, :] + rl[kz, 32 + c * 8 : 40 + c * 8, :]
            for x in range(4):
                at = 32 + c * 8 + x * 2
                push[c, kz, x * 4 : x * 4 + 2, :] = push[c, kz, x * 4 : x * 4 + 2, :] + rb[kz, at : at + 2, :]
            for x in range(2):
                at = 32 + c * 4 + x * 2
                push[c, kz, x * 4 : x * 4 + 2, :] = push[c, kz, x * 4 : x * 4 + 2, :] + rd[kz, at : at + 2, :]
        for x in range(4):
            for c in range(2):
                push[3 + c, kz, x * 4 : x * 4 + 4, :] = (
                    warm[0, kz, (x + 2) * 6 + 2 : (x + 2) * 6 + 6, :]
                    if c == 0
                    else region[0, kz, (x + 2) * 6 + 2 : (x + 2) * 6 + 6, :]
                )
    width_x = 4 * lax.axis_size("gx")
    height_z = 512
    spin = 2.0 / height_z
    shape = (16, 128)
    cell_x = lax.broadcasted_iota(jnp.int32, shape, 0) // 4 - 1 + 4 * lax.axis_index("gx")
    cell_x = jnp.where(cell_x < 0, cell_x + width_x, cell_x).astype(f32)
    wall_w = -spin * (cell_x + 0.5 - 0.5 * width_x)
    for kz in range(4):
        cell_z = (lax.broadcasted_iota(jnp.int32, shape, 1) * 4 + kz).astype(f32)
        wall = [spin * (cell_z + 0.5 - 0.5 * height_z), jnp.zeros(shape, f32), wall_w]
        inverse = 1.0 / jnp.maximum(push[3, kz], mass_floor)
        moving = [push[a, kz] * inverse for a in range(3)]
        moving[2] = moving[2] - gravity_step
        relative = [moving[a] - wall[a] for a in range(3)]
        facing = [normal[a, kz] for a in range(3)]
        normal_part = sum(relative[a] * facing[a] for a in range(3))
        tangent = [relative[a] - normal_part * facing[a] for a in range(3)]
        length = jnp.sqrt(sum(part * part for part in tangent))
        factor = jnp.maximum(
            0.0, 1.0 + friction * normal_part / jnp.maximum(length, slip_floor)
        )
        slips = (rough[kz] == 1.0) & (normal_part < 0.0)
        solid = push[4, kz] == 1.0
        for a in range(3):
            value = jnp.where(slips, wall[a] + tangent[a] * factor, moving[a])
            push[a, kz] = jnp.where(solid, wall[a], value)
        heat = warm[1, kz, 0:36, :] / jnp.maximum(warm[0, kz, 0:36, :], mass_floor)
        warm[1, kz, 0:36, :] = jnp.where(region[0, kz] == 1.0, region[3, kz], heat)
    for kz in range(4):
        ko[kz, 0:36, :] = warm[1, kz, 0:36, :]
        ko[kz, 36:40, :] = jnp.zeros((4, 128), f32)
        ko[kz, 88:124, :] = region[0, kz]
        ko[kz, 124:128, :] = jnp.zeros((4, 128), f32)
        hl[kz, 0:24, :] = warm[1, kz, 12:36, :]
        for c in range(3):
            ko[kz, 40 + c * 16 : 56 + c * 16, :] = push[c, kz]
            hl[kz, 24 + c * 8 : 32 + c * 8, :] = push[c, kz, 0:8, :]
            for x in range(4):
                at = 24 + c * 8 + x * 2
                hb[kz, at : at + 2, :] = push[c, kz, x * 4 : x * 4 + 2, :]
            for x in range(2):
                at = 16 + c * 4 + x * 2
                hd[kz, at : at + 2, :] = push[c, kz, x * 4 : x * 4 + 2, :]
        for x in range(6):
            hb[kz, x * 4 : x * 4 + 4, :] = warm[1, kz, x * 6 + 2 : x * 6 + 6, :]
        for x in range(4):
            hd[kz, x * 4 : x * 4 + 4, :] = warm[1, kz, (x + 2) * 6 + 2 : (x + 2) * 6 + 6, :]
        for x in range(3):
            row = (x + 2) * 6
            hl[kz, 48 + x * 5 : 53 + x * 5, :] = region[0, kz, row + 1 : row + 6, :]
            hd[kz, 28 + x * 3 : 31 + x * 3, :] = region[0, kz, row + 2 : row + 5, :]
        for x in range(5):
            row = (x + 1) * 6
            hb[kz, 48 + x * 3 : 51 + x * 3, :] = region[0, kz, row + 2 : row + 5, :]
        hl[kz, 63:64, :] = jnp.zeros((1, 128), f32)
        hb[kz, 63:64, :] = jnp.zeros((1, 128), f32)
        hd[kz, 37:40, :] = jnp.zeros((3, 128), f32)


def collect_kernel(
    code_s, brick_s, came_s, ko, rl, rb, rd, frac, o_ref, rxp, rxm, ryp, rym,
    move_ref, grad_ref, warm_ref, gvel_ref, gtemp_ref,
    heat, solid, speed, cells, fine, coarse, turn, lu, fo, sb, sw,
):
    lane = lax.broadcasted_iota(jnp.int32, (8, 128), 1)[0:1]
    heat[...] = jnp.zeros(heat.shape, f32)
    solid[...] = jnp.zeros(solid.shape, f32)
    for kz in range(4):
        for x in range(6):
            to = 16 + x * 10
            heat[0, kz, to : to + 6, :] = ko[kz, x * 6 : x * 6 + 6, :]
            heat[0, kz, to + 6 : to + 10, :] = rb[kz, x * 4 : x * 4 + 4, :]
            solid[kz, x * 10 : x * 10 + 6, :] = ko[kz, 88 + x * 6 : 94 + x * 6, :]
        for x in range(4):
            to = 16 + (x + 6) * 10
            heat[0, kz, to : to + 6, :] = rl[kz, x * 6 : x * 6 + 6, :]
            heat[0, kz, to + 6 : to + 10, :] = rd[kz, x * 4 : x * 4 + 4, :]
        for x in range(3):
            to = (x + 6) * 10
            solid[kz, to + 1 : to + 6, :] = rl[kz, 48 + x * 5 : 53 + x * 5, :]
            solid[kz, to + 6 : to + 9, :] = rd[kz, 28 + x * 3 : 31 + x * 3, :]
        for x in range(5):
            to = (x + 1) * 10
            solid[kz, to + 6 : to + 9, :] = rb[kz, 48 + x * 3 : 51 + x * 3, :]
        for c in range(3):
            for x in range(4):
                speed[c, kz, x * 6 : x * 6 + 4, :] = ko[kz, 40 + c * 16 + x * 4 : 44 + c * 16 + x * 4, :]
                at = 24 + c * 8 + x * 2
                speed[c, kz, x * 6 + 4 : x * 6 + 6, :] = rb[kz, at : at + 2, :]
            for x in range(2):
                at = 24 + c * 8 + x * 4
                speed[c, kz, 24 + x * 6 : 28 + x * 6, :] = rl[kz, at : at + 4, :]
                at = 16 + c * 4 + x * 2
                speed[c, kz, 28 + x * 6 : 30 + x * 6, :] = rd[kz, at : at + 2, :]
    for sweep in range(2):
        now, later = sweep, sweep + 1
        layers = [heat[now, kz, 16:120, :] for kz in range(4)]
        above = jnp.where(lane == 127, layers[3], pltpu.roll(layers[0], 127, 1))
        below = jnp.where(lane == 0, layers[0], pltpu.roll(layers[3], 1, 1))
        for kz in range(4):
            upper = layers[kz + 1] if kz < 3 else above
            lower = layers[kz - 1] if kz else below
            laplace = (
                heat[now, kz, 6:110, :]
                + heat[now, kz, 26:130, :]
                + heat[now, kz, 15:119, :]
                + heat[now, kz, 17:121, :]
                + upper
                + lower
                - 6.0 * layers[kz]
            )
            heat[later, kz, 16:120, :] = jnp.where(
                solid[kz] == 1.0, heat[0, kz, 16:120, :], layers[kz] + conduct * laplace
            )
    for kz in range(4):
        for x in range(6):
            to = 16 + (x + 2) * 10 + 2
            speed[3, kz, x * 6 : x * 6 + 6, :] = heat[2, kz, to : to + 6, :]
    for c in range(4):
        for kz in range(4):
            for x in range(4):
                at = (x + 1) * 6 + 1
                cells[c * 16 + x * 4 : c * 16 + x * 4 + 4, kz * 128 : kz * 128 + 128] = speed[c, kz, at : at + 4, :]
    source = lax.broadcasted_iota(jnp.int32, (512, 512), 0)
    wanted = (source % 128) * 4 + source // 128
    permute = (wanted == lax.broadcasted_iota(jnp.int32, (512, 512), 1)).astype(f32).astype(bf16)
    value = cells[...]
    high, rest = split_two(value)
    middle, low = split_two(rest)
    spread = jnp.concatenate([high, middle, low], axis=0).astype(bf16)
    spread = jnp.dot(spread, permute, preferred_element_type=f32)
    value = spread[0:64] + spread[64:128] + spread[128:192]
    for x in range(4):
        for c in range(3):
            gvel_ref[c, x] = value[c * 16 + x * 4 : c * 16 + x * 4 + 4]
        gtemp_ref[x] = value[48 + x * 4 : 52 + x * 4]
    for c in range(4):
        for jz in range(6):
            kz = (jz - 1) % 4
            layer = speed[c, kz]
            if jz == 0:
                layer = jnp.where(lane == 0, 0.0, pltpu.roll(layer, 1, 1))
            if jz == 5:
                layer = jnp.where(lane == 127, 0.0, pltpu.roll(layer, 127, 1))
            high, low = split_two(layer)
            coarse[c, jz] = high
            fine[c, jz] = low
    turn[...] = jnp.zeros(turn.shape, f32)
    for jx in range(6):
        for c in range(4):
            side = c % 2
            for jz in range(6):
                rows = slice(jx * 6, jx * 6 + 6)
                turn[side, jz * 6 : jz * 6 + 6, :] = coarse[c, jz, rows, :]
                turn[side, 40 + jz * 6 : 46 + jz * 6, :] = fine[c, jz, rows, :]
                turn[side, 80 + jz * 6 : 86 + jz * 6, :] = coarse[c, jz, rows, :]
            lu[pl.ds(jx * 4 + c, 128, stride=24), :] = jnp.transpose(turn[side])
    for d in range(3):
        fo[d, 0:128, :] = frac[d]
    fo[3, 0:128, :] = o_ref[...].astype(f32)
    places = [(ryp, 0), (rxp, 1), (rym, 0), (ryp, 1), (rym, 1), (ryp, 2), (rxm, 1), (rym, 2)]
    for g, (ref, at) in enumerate(places):
        for d in range(4):
            fo[d, 128 + g * 16 : 144 + g * 16, :] = ref[pl.ds((at * msg_tiles + 9 + d) * 16, 16), :]
    sb[...] = jnp.zeros(sb.shape, f32)

    def group(g, carry):
        rows = pl.ds(pl.multiple_of(g * 8, 8), 8)
        offset = fo[3, rows, :].astype(jnp.int32)
        wx, rx = axis_tables(offset >> 4, fo[0, rows, :], 4.0)
        for j in range(6):
            for copy in range(4):
                sw[pl.ds((j * 4 + copy) * 8, 8), :] = wx[j]
                sw[pl.ds((24 + j * 4 + copy) * 8, 8), :] = rx[j]
        wy, ry = axis_tables((offset >> 2) & 3, fo[1, rows, :], 4.0)
        wz, rz = axis_tables(offset & 3, fo[2, rows, :], 4.0)
        for jz in range(6):
            for jy in range(6):
                r = jz * 6 + jy
                sb[pl.ds(r * 8, 8), :] = wy[jy] * wz[jz]
                sb[pl.ds((40 + r) * 8, 8), :] = ry[jy] * wz[jz]
                sb[pl.ds((80 + r) * 8, 8), :] = wy[jy] * rz[jz]
        for j in range(8):
            slot = g * 8 + j
            home = jnp.minimum(slot, 127)
            stays = jnp.where(code_s[home] == 4, brick_s[home], -1)
            brick = jnp.where(slot < 128, stays, came_s[0, jnp.maximum(slot - 128, 0)])
            live = jnp.where(brick >= 0, 1.0, 0.0).astype(f32)
            spot = pl.ds(pl.multiple_of(jnp.maximum(brick, 0) * 24, 8), 24)
            left = lu[spot, :].astype(bf16)
            right = jnp.concatenate(
                [sb[pl.ds(n * 320 + j, 40, stride=8), :] for n in range(3)], axis=1
            )
            high, low = split_two(right)
            right = jnp.concatenate([high, high, low, jnp.zeros((8, 384), f32)], axis=0).astype(bf16)
            both = jnp.dot(left, right, preferred_element_type=f32)
            plain = sw[pl.ds(j, 24, stride=8), :]
            tilt = sw[pl.ds(192 + j, 24, stride=8), :]

            def over_x(weight, column):
                part = weight * both[:, column * 128 : column * 128 + 128]
                part = part[0:8] + part[8:16] + part[16:24]
                return (part[0:4] + part[4:8]) * live

            lanes = pl.ds(pl.multiple_of(slot * 128, 128), 128)
            moved = over_x(plain, 0)
            move_ref[:, lanes] = moved[0:3]
            warm_ref[pl.ds(slot, 1), :] = moved[3:4]
            for k, (weight, column) in enumerate(((tilt, 0), (plain, 1), (plain, 2))):
                part = over_x(weight, column)
                for a in range(3):
                    grad_ref[a * 3 + k : a * 3 + k + 1, lanes] = part[a : a + 1]
        return carry

    lax.fori_loop(0, 32, group, 0)


def neighbor(value, dx, dy):
    size_x, size_y = lax.axis_size("gx"), lax.axis_size("gy")
    if dy == 0:
        return lax.ppermute(value, "gx", [(i, (i + dx) % size_x) for i in range(size_x)])
    if dx == 0:
        return lax.ppermute(value, "gy", [(i, (i + dy) % size_y) for i in range(size_y)])
    pairs = [
        (i * size_y + j, (i + dx) % size_x * size_y + (j + dy) % size_y)
        for i in range(size_x)
        for j in range(size_y)
    ]
    return lax.ppermute(value, ("gx", "gy"), pairs)


def call(kernel, name, inputs, scalars, outputs, scratch, left_there=0, limit=50):
    in_specs = (
        [pl.BlockSpec(memory_space=pltpu.SMEM)] * scalars
        + [pl.BlockSpec(memory_space=pltpu.HBM)] * left_there
        + [pl.BlockSpec(memory_space=pltpu.VMEM)] * (len(inputs) - scalars - left_there)
    )
    return pl.pallas_call(
        kernel,
        name=name,
        out_shape=[jax.ShapeDtypeStruct(shape, dtype) for shape, dtype in outputs],
        in_specs=in_specs,
        out_specs=[pl.BlockSpec(memory_space=pltpu.VMEM)] * len(outputs),
        scratch_shapes=scratch,
        compiler_params=pltpu.CompilerParams(vmem_limit_bytes=limit * mib),
    )(*inputs)


def vmem(*shape):
    return pltpu.VMEM(shape, f32)


def on_device(
    subvoxel_location_share,
    point_motion_vector,
    linear_gradient_matrix,
    kirchhoff_tension_matrix,
    point_inertia_amounts,
    point_thermal_state,
    anchor_voxel_shift,
    group_resting_volume,
    group_migration_label,
    cylinder_shell_flag,
    rough_surface_flag,
    voxel_facing_choice,
    facing_unit_vectors,
    rim_thermal_level,
):
    offset = anchor_voxel_shift.reshape(128, 128)
    own, frac, xm, ym, yp, xp = call(
        deposit_kernel,
        "deposit",
        (
            group_migration_label,
            group_resting_volume,
            subvoxel_location_share,
            point_motion_vector,
            linear_gradient_matrix,
            kirchhoff_tension_matrix,
            point_inertia_amounts.reshape(128, 128),
            point_thermal_state.reshape(128, 128),
            offset,
        ),
        2,
        [
            ((tiles, 128, 128), f32),
            ((3, 128, 128), f32),
            ((3 * msg_rows, 128), f32),
            ((msg_rows, 128), f32),
            ((msg_rows, 128), f32),
            ((3 * msg_rows, 128), f32),
        ],
        [
            vmem(3, 16384),
            vmem(3, 16384),
            vmem(9, 16384),
            vmem(9, 16384),
            vmem(128, 128),
            vmem(128, 128),
            pltpu.VMEM((128, 128), jnp.int32),
            pltpu.SemaphoreType.DMA((7,)),
            vmem(320, 128),
            vmem(96 * 8, 128),
            vmem(120 * 8, 128),
            vmem(256 * 32, 128),
            pltpu.SMEM((16,), jnp.int32),
            vmem(8 * msg_rows + 64, 128),
        ],
        7,
        64,
    )
    rxp = neighbor(xp, 1, 0)
    rxm = neighbor(xm, -1, 0)
    ryp = neighbor(
        jnp.concatenate([rxp[2 * msg_rows :], yp, rxm[2 * msg_rows :]], axis=0), 0, 1
    )
    rym = neighbor(jnp.concatenate([rxp[:msg_rows], ym, rxm[:msg_rows]], axis=0), 0, -1)

    static, sl, sb, sd = call(
        static_kernel,
        "static",
        (
            facing_unit_vectors,
            cylinder_shell_flag,
            rough_surface_flag,
            voxel_facing_choice,
            rim_thermal_level,
        ),
        1,
        [
            ((4, 96, 128), f32),
            ((4, 32, 128), f32),
            ((4, 32, 128), f32),
            ((4, 24, 128), f32),
        ],
        [vmem(64, 512)],
    )
    sl, sb, sd = neighbor(sl, 1, 0), neighbor(sb, 0, 1), neighbor(sd, 1, 1)

    ml, mb, md, mo, came = call(
        total_kernel,
        "total",
        (own, rxp, rxm, ryp, rym),
        0,
        [
            ((4, 56, 128), f32),
            ((4, 56, 128), f32),
            ((4, 48, 128), f32),
            ((4, 80, 128), f32),
            ((1, 128), jnp.int32),
        ],
        [vmem(tiles * 128, 128), vmem(4, 184, 128)],
    )
    hl, hb, hd, ko = call(
        update_kernel,
        "update",
        (mo, neighbor(ml, 1, 0), neighbor(mb, 0, 1), neighbor(md, 1, 1), static, sl, sb, sd),
        0,
        [
            ((4, 64, 128), f32),
            ((4, 64, 128), f32),
            ((4, 40, 128), f32),
            ((4, 128, 128), f32),
        ],
        [
            vmem(2, 4, 40, 128),
            vmem(5, 4, 16, 128),
            vmem(4, 4, 36, 128),
            vmem(4, 16, 128),
            vmem(3, 4, 16, 128),
        ],
    )
    move, grad, warm, gvel, gtemp = call(
        collect_kernel,
        "collect",
        (
            group_migration_label,
            group_resting_volume,
            came,
            ko,
            neighbor(hl, -1, 0),
            neighbor(hb, 0, -1),
            neighbor(hd, -1, -1),
            frac,
            offset,
            rxp,
            rxm,
            ryp,
            rym,
        ),
        3,
        [
            ((3, 32768), f32),
            ((9, 32768), f32),
            ((256, 128), f32),
            ((3, 4, 4, 512), f32),
            ((4, 4, 512), f32),
        ],
        [
            vmem(3, 4, 136, 128),
            vmem(4, 104, 128),
            vmem(4, 4, 40, 128),
            vmem(64, 512),
            vmem(4, 6, 40, 128),
            vmem(4, 6, 40, 128),
            vmem(2, 128, 128),
            vmem(128 * 24, 128),
            vmem(4, 256, 128),
            vmem(120 * 8, 128),
            vmem(48 * 8, 128),
        ],
    )
    return move, grad, warm.reshape(-1), gvel, gtemp


def solution(mesh):
    in_specs = (
        P(None, ("gx", "gy")),
        P(None, ("gx", "gy")),
        P(None, ("gx", "gy")),
        P(None, ("gx", "gy")),
        P(("gx", "gy")),
        P(("gx", "gy")),
        P(("gx", "gy")),
        P(("gx", "gy")),
        P(("gx", "gy")),
        P("gx", "gy", None),
        P("gx", "gy", None),
        P("gx", "gy", None),
        P(),
        P("gx", "gy", None),
    )
    out_specs = (
        P(None, ("gx", "gy")),
        P(None, ("gx", "gy")),
        P(("gx", "gy")),
        P(None, "gx", "gy", None),
        P("gx", "gy", None),
    )
    return jax.shard_map(
        on_device, mesh=mesh, in_specs=in_specs, out_specs=out_specs, check_vma=False
    )
```

profile of v0, /device:TPU:0, one launch (start us, length us, event | category | flops | bytes accessed | tf_op | source)
XLA Modules:
  0.0 76.1 jit_solution(17249231915652940440)
XLA Ops:
  0.6 15.6 %deposit.1 = (f32[9,128,128]{2,1,0:T(8,128)}, f32[3,128,128]{2,1,0:T(8,128)}, f32[624,128]{1,0:T(8,128)}, f32[208,128]{1,0:T(8,128)}, f32[208,128]{1,0:T(8,128)}, /*index=5*/f32[624,128]{1,0:T(8,128)}) custom-call(s32[128]{0:T(128)} %code_s.3, s32[128]{0:T(128)} %brick_s.3, f32[3,16384]{1,0:T(4,128)} %f_hbm.1, f32[3,16384]{1,0:T(4,128)} %v_hbm.1, ...), custom_call_target="tpu_custom_call" | custom-call | tf_op jit(solution)/shard_map/deposit/pallas_call | solution.py:582
  16.2 0.0 copy-start.3
  16.2 0.0 copy-start.4
  16.2 0.0 copy-start.5
  16.2 0.0 copy-start.6
  16.3 0.0 collective-permute-start
  16.3 2.9 %collective-permute-start.1 = (f32[624,128]{1,0:T(8,128)}, f32[624,128]{1,0:T(8,128)S(1)}, u32[]{:S(2)}, u32[]{:S(2)}) collective-permute-start(f32[624,128]{1,0:T(8,128)} %get-tuple-element.31), channel_id=1, source_target_pairs={{0,112},{16,0},{32,16},{48,32},{64,48},{80,64},{96,80},{112,96},{1... | collective-permute-start | bytes 958472 | tf_op jit(solution)/shard_map/ppermute | solution.py:565
  19.2 4.9 %collective-permute-done.rxp = f32[624,128]{1,0:T(8,128)S(1)} collective-permute-done((f32[624,128]{1,0:T(8,128)}, f32[624,128]{1,0:T(8,128)S(1)}, u32[]{:S(2)}, u32[]{:S(2)}) %collective-permute-start) | collective-permute-done | bytes 319520 | tf_op jit(solution)/shard_map/ppermute | solution.py:565
  24.2 0.0 copy-start.9
  24.2 1.0 %pad_maximum_fusion = f32[624,128]{1,0:T(8,128)S(1)} fusion(f32[208,128]{1,0:T(8,128)S(1)} %get-tuple-element.56, f32[208,128]{1,0:T(8,128)} %get-tuple-element.32, f32[208,128]{1,0:T(8,128)S(1)} %get-tuple-element.54), kind=kLoop, calls=%fused_computation | loop fusion | flops 159744 | bytes 638976 | tf_op jit(solution)/shard_map/concatenate | solution.py:659
  25.2 1.7 %collective-permute-start.2 = (f32[624,128]{1,0:T(8,128)S(1)}, f32[624,128]{1,0:T(8,128)S(1)}, u32[]{:S(2)}, u32[]{:S(2)}) collective-permute-start(f32[624,128]{1,0:T(8,128)S(1)} %pad_maximum_fusion), channel_id=1, source_target_pairs={{0,1},{1,2},{2,3},{3,4},{4,5},{5,6},{6,7},{7,8},{8,9},{9,10},{10,1... | collective-permute-start | bytes 958472 | tf_op jit(solution)/shard_map/ppermute | solution.py:567
  26.9 0.9 %pad_maximum_fusion.1 = f32[624,128]{1,0:T(8,128)S(1)} fusion(f32[208,128]{1,0:T(8,128)S(1)} %get-tuple-element.55, f32[208,128]{1,0:T(8,128)} %get-tuple-element.33, f32[208,128]{1,0:T(8,128)S(1)} %get-tuple-element.53), kind=kLoop, calls=%fused_computation.1 | loop fusion | flops 159744 | bytes 638976 | tf_op jit(solution)/shard_map/concatenate | solution.py:661
  27.9 5.0 %collective-permute-start.3 = (f32[624,128]{1,0:T(8,128)S(1)}, f32[624,128]{1,0:T(8,128)S(1)}, u32[]{:S(2)}, u32[]{:S(2)}) collective-permute-start(f32[624,128]{1,0:T(8,128)S(1)} %pad_maximum_fusion.1), channel_id=1, source_target_pairs={{0,15},{1,0},{2,1},{3,2},{4,3},{5,4},{6,5},{7,6},{8,7},{9,8},{10,9... | collective-permute-start | bytes 958472 | tf_op jit(solution)/shard_map/ppermute | solution.py:567
  32.9 1.1 %static.1 = (f32[4,96,128]{2,1,0:T(8,128)S(1)}, f32[4,32,128]{2,1,0:T(8,128)S(1)}, f32[4,32,128]{2,1,0:T(8,128)S(1)}, f32[4,24,128]{2,1,0:T(8,128)S(1)}) custom-call(f32[3,64]{1,0:T(4,128)S(1)} %copy-done.7, s32[4,4,512]{2,1,0:T(4,128)S(1)} %copy-done.3, s32[4,4,512]{2,1,0:T(4,128)S(1)} %copy-done.4, s32[4,4,512]{2,1,0:T(4,128)S(1)} %copy-done.5, ...), custom_call_target="tpu_custom_call" | custom-call | tf_op jit(solution)/shard_map/static/pallas_call | solution.py:582
  34.0 0.1 collective-permute-start.9
  34.1 5.8 %collective-permute-done.2.ryp = f32[624,128]{1,0:T(8,128)S(1)} collective-permute-done((f32[624,128]{1,0:T(8,128)S(1)}, f32[624,128]{1,0:T(8,128)S(1)}, u32[]{:S(2)}, u32[]{:S(2)}) %collective-permute-start.2) | collective-permute-done | bytes 319520 | tf_op jit(solution)/shard_map/ppermute | solution.py:567
  39.9 0.3 collective-permute-done.3.rym
  40.2 0.7 total.1
  40.9 0.0 collective-permute-start.4
  40.9 0.1 collective-permute-start.5
  41.0 0.3 collective-permute-start.6
  41.3 0.3 collective-permute-start.7
  41.6 1.4 %collective-permute-done.9.sd = f32[4,24,128]{2,1,0:T(8,128)S(1)} collective-permute-done((f32[4,24,128]{2,1,0:T(8,128)S(1)}, f32[4,24,128]{2,1,0:T(8,128)S(1)}, u32[]{:S(2)}, u32[]{:S(2)}) %collective-permute-start.9) | collective-permute-done | bytes 49184 | tf_op jit(solution)/shard_map/ppermute | solution.py:573
  43.0 2.2 %collective-permute-start.8 = (f32[4,32,128]{2,1,0:T(8,128)S(1)}, f32[4,32,128]{2,1,0:T(8,128)S(1)}, u32[]{:S(2)}, u32[]{:S(2)}) collective-permute-start(f32[4,32,128]{2,1,0:T(8,128)S(1)} %get-tuple-element.41), channel_id=1, source_target_pairs={{0,1},{1,2},{2,3},{3,4},{4,5},{5,6},{6,7},{7,8},{8,9},{9,10},{10,1... | collective-permute-start | bytes 196616 | tf_op jit(solution)/shard_map/ppermute | solution.py:567
  45.3 2.8 %collective-permute-done.7.sl = f32[4,32,128]{2,1,0:T(8,128)S(1)} collective-permute-done((f32[4,32,128]{2,1,0:T(8,128)S(1)}, f32[4,32,128]{2,1,0:T(8,128)S(1)}, u32[]{:S(2)}, u32[]{:S(2)}) %collective-permute-start.7) | collective-permute-done | bytes 65568 | tf_op jit(solution)/shard_map/ppermute | solution.py:565
  48.1 5.9 %collective-permute-done.8.sb = f32[4,32,128]{2,1,0:T(8,128)S(1)} collective-permute-done((f32[4,32,128]{2,1,0:T(8,128)S(1)}, f32[4,32,128]{2,1,0:T(8,128)S(1)}, u32[]{:S(2)}, u32[]{:S(2)}) %collective-permute-start.8) | collective-permute-done | bytes 65568 | tf_op jit(solution)/shard_map/ppermute | solution.py:567
  54.0 0.4 update.1
  54.4 1.5 %collective-permute-start.10 = (f32[4,64,128]{2,1,0:T(8,128)S(1)}, f32[4,64,128]{2,1,0:T(8,128)S(1)}, u32[]{:S(2)}, u32[]{:S(2)}) collective-permute-start(f32[4,64,128]{2,1,0:T(8,128)S(1)} %get-tuple-element.44), channel_id=1, source_target_pairs={{0,112},{16,0},{32,16},{48,32},{64,48},{80,64},{96,80},{112,96},{1... | collective-permute-start | bytes 393224 | tf_op jit(solution)/shard_map/ppermute | solution.py:565
  55.9 1.4 %collective-permute-start.11 = (f32[4,64,128]{2,1,0:T(8,128)S(1)}, f32[4,64,128]{2,1,0:T(8,128)S(1)}, u32[]{:S(2)}, u32[]{:S(2)}) collective-permute-start(f32[4,64,128]{2,1,0:T(8,128)S(1)} %get-tuple-element.45), channel_id=1, source_target_pairs={{0,15},{1,0},{2,1},{3,2},{4,3},{5,4},{6,5},{7,6},{8,7},{9,8},{10,9... | collective-permute-start | bytes 393224 | tf_op jit(solution)/shard_map/ppermute | solution.py:567
  57.3 0.8 %collective-permute-start.12 = (f32[4,40,128]{2,1,0:T(8,128)S(1)}, f32[4,40,128]{2,1,0:T(8,128)S(1)}, u32[]{:S(2)}, u32[]{:S(2)}) collective-permute-start(f32[4,40,128]{2,1,0:T(8,128)S(1)} %get-tuple-element.46), channel_id=1, source_target_pairs={{0,127},{1,112},{2,113},{3,114},{4,115},{5,116},{6,117},{7,118},{8... | collective-permute-start | bytes 245768 | tf_op jit(solution)/shard_map/ppermute | solution.py:573
  58.2 4.4 %collective-permute-done.12.rd = f32[4,40,128]{2,1,0:T(8,128)S(1)} collective-permute-done((f32[4,40,128]{2,1,0:T(8,128)S(1)}, f32[4,40,128]{2,1,0:T(8,128)S(1)}, u32[]{:S(2)}, u32[]{:S(2)}) %collective-permute-start.12) | collective-permute-done | bytes 81952 | tf_op jit(solution)/shard_map/ppermute | solution.py:573
  62.6 13.5 %collect.1 = (f32[3,32768]{1,0:T(4,128)}, f32[9,32768]{1,0:T(8,128)}, f32[256,128]{1,0:T(8,128)}, f32[3,4,4,512]{3,2,1,0:T(4,128)}, f32[4,4,512]{2,1,0:T(4,128)}) custom-call(s32[128]{0:T(128)S(1)} %copy-done.8, s32[128]{0:T(128)S(1)} %copy-done.9, s32[1,128]{1,0:T(1,128)S(1)} %get-tuple-element.34.came_s, f32[4,128,128]{2,1,0:T(8,128)S(1)} %get-tuple-element.43.ko, ...), custom_call_target="tpu_custom_call" | custom-call | tf_op jit(solution)/shard_map/collect/pallas_call | solution.py:582
  (23 shorter events, 0.1 us)
Async XLA Ops:
  16.2 16.7 %copy-start.3 = (s32[4,4,512]{2,1,0:T(4,128)S(1)}, s32[4,4,512]{2,1,0:T(4,128)}, u32[]{:S(2)}) copy-start(s32[4,4,512]{2,1,0:T(4,128)} %solid_ref.1) | copy-start | bytes 98308
  16.2 16.7 %copy-start.4 = (s32[4,4,512]{2,1,0:T(4,128)S(1)}, s32[4,4,512]{2,1,0:T(4,128)}, u32[]{:S(2)}) copy-start(s32[4,4,512]{2,1,0:T(4,128)} %rough_ref.1) | copy-start | bytes 98308
  16.2 16.6 %copy-start.5 = (s32[4,4,512]{2,1,0:T(4,128)S(1)}, s32[4,4,512]{2,1,0:T(4,128)}, u32[]{:S(2)}) copy-start(s32[4,4,512]{2,1,0:T(4,128)} %choice_ref.1) | copy-start | bytes 98308
  16.2 16.6 %copy-start.6 = (f32[4,4,512]{2,1,0:T(4,128)S(1)}, f32[4,4,512]{2,1,0:T(4,128)}, u32[]{:S(2)}) copy-start(f32[4,4,512]{2,1,0:T(4,128)} %rim_ref.1) | copy-start | bytes 98308
  16.2 16.6 %copy-start.7 = (f32[3,64]{1,0:T(4,128)S(1)}, f32[3,64]{1,0:T(4,128)}, u32[]{:S(2)}) copy-start(f32[3,64]{1,0:T(4,128)} %table.1) | copy-start | bytes 2308
  16.3 23.9 %copy-start = (f32[9,128,128]{2,1,0:T(8,128)S(1)}, f32[9,128,128]{2,1,0:T(8,128)}, u32[]{:S(2)}) copy-start(f32[9,128,128]{2,1,0:T(8,128)} %get-tuple-element.29.own_ref) | copy-start | bytes 1769476
  16.3 7.8 %collective-permute-start = (f32[624,128]{1,0:T(8,128)}, f32[624,128]{1,0:T(8,128)S(1)}, u32[]{:S(2)}, u32[]{:S(2)}) collective-permute-start(f32[624,128]{1,0:T(8,128)} %get-tuple-element.30), channel_id=1, source_target_pairs={{0,16},{16,32},{32,48},{48,64},{64,80},{80,96},{96,112},{112,0},{1... | collective-permute-start | bytes 958472 | tf_op jit(solution)/shard_map/ppermute | solution.py:565
  16.3 7.8 %collective-permute-start.1 = (f32[624,128]{1,0:T(8,128)}, f32[624,128]{1,0:T(8,128)S(1)}, u32[]{:S(2)}, u32[]{:S(2)}) collective-permute-start(f32[624,128]{1,0:T(8,128)} %get-tuple-element.31), channel_id=1, source_target_pairs={{0,112},{16,0},{32,16},{48,32},{64,48},{80,64},{96,80},{112,96},{1... | collective-permute-start | bytes 958472 | tf_op jit(solution)/shard_map/ppermute | solution.py:565
  24.2 38.4 %copy-start.1 = (s32[16384]{0:T(1024)S(1)}, s32[16384]{0:T(1024)}, u32[]{:S(2)}) copy-start(s32[16384]{0:T(1024)} %param.20) | copy-start | bytes 196612
  24.2 38.4 %copy-start.2 = (f32[3,128,128]{2,1,0:T(8,128)S(1)}, f32[3,128,128]{2,1,0:T(8,128)}, u32[]{:S(2)}) copy-start(f32[3,128,128]{2,1,0:T(8,128)} %get-tuple-element.47.frac) | copy-start | bytes 589828
  24.2 38.4 %copy-start.8 = (s32[128]{0:T(128)S(1)}, s32[128]{0:T(128)}, u32[]{:S(2)}) copy-start(s32[128]{0:T(128)} %code_s.3) | copy-start | bytes 1540
  24.2 38.4 %copy-start.9 = (s32[128]{0:T(128)S(1)}, s32[128]{0:T(128)}, u32[]{:S(2)}) copy-start(s32[128]{0:T(128)} %brick_s.3) | copy-start | bytes 1540
  25.2 14.7 %collective-permute-start.2 = (f32[624,128]{1,0:T(8,128)S(1)}, f32[624,128]{1,0:T(8,128)S(1)}, u32[]{:S(2)}, u32[]{:S(2)}) collective-permute-start(f32[624,128]{1,0:T(8,128)S(1)} %pad_maximum_fusion), channel_id=1, source_target_pairs={{0,1},{1,2},{2,3},{3,4},{4,5},{5,6},{6,7},{7,8},{8,9},{9,10},{10,1... | collective-permute-start | bytes 958472 | tf_op jit(solution)/shard_map/ppermute | solution.py:567
  27.9 12.3 %collective-permute-start.3 = (f32[624,128]{1,0:T(8,128)S(1)}, f32[624,128]{1,0:T(8,128)S(1)}, u32[]{:S(2)}, u32[]{:S(2)}) collective-permute-start(f32[624,128]{1,0:T(8,128)S(1)} %pad_maximum_fusion.1), channel_id=1, source_target_pairs={{0,15},{1,0},{2,1},{3,2},{4,3},{5,4},{6,5},{7,6},{8,7},{9,8},{10,9... | collective-permute-start | bytes 958472 | tf_op jit(solution)/shard_map/ppermute | solution.py:567
  34.0 9.0 %collective-permute-start.9 = (f32[4,24,128]{2,1,0:T(8,128)S(1)}, f32[4,24,128]{2,1,0:T(8,128)S(1)}, u32[]{:S(2)}, u32[]{:S(2)}) collective-permute-start(f32[4,24,128]{2,1,0:T(8,128)S(1)} %get-tuple-element.42), channel_id=1, source_target_pairs={{0,17},{1,18},{2,19},{3,20},{4,21},{5,22},{6,23},{7,24},{8,25},{9,... | collective-permute-start | bytes 147464 | tf_op jit(solution)/shard_map/ppermute | solution.py:573
  40.9 13.1 %collective-permute-start.4 = (f32[4,56,128]{2,1,0:T(8,128)S(1)}, f32[4,56,128]{2,1,0:T(8,128)S(1)}, u32[]{:S(2)}, u32[]{:S(2)}) collective-permute-start(f32[4,56,128]{2,1,0:T(8,128)S(1)} %get-tuple-element.36), channel_id=1, source_target_pairs={{0,16},{16,32},{32,48},{48,64},{64,80},{80,96},{96,112},{112,0},{1... | collective-permute-start | bytes 344072 | tf_op jit(solution)/shard_map/ppermute | solution.py:565
  40.9 13.1 %collective-permute-start.5 = (f32[4,56,128]{2,1,0:T(8,128)S(1)}, f32[4,56,128]{2,1,0:T(8,128)S(1)}, u32[]{:S(2)}, u32[]{:S(2)}) collective-permute-start(f32[4,56,128]{2,1,0:T(8,128)S(1)} %get-tuple-element.37), channel_id=1, source_target_pairs={{0,1},{1,2},{2,3},{3,4},{4,5},{5,6},{6,7},{7,8},{8,9},{9,10},{10,1... | collective-permute-start | bytes 344072 | tf_op jit(solution)/shard_map/ppermute | solution.py:567
  41.0 13.0 %collective-permute-start.6 = (f32[4,48,128]{2,1,0:T(8,128)S(1)}, f32[4,48,128]{2,1,0:T(8,128)S(1)}, u32[]{:S(2)}, u32[]{:S(2)}) collective-permute-start(f32[4,48,128]{2,1,0:T(8,128)S(1)} %get-tuple-element.38), channel_id=1, source_target_pairs={{0,17},{1,18},{2,19},{3,20},{4,21},{5,22},{6,23},{7,24},{8,25},{9,... | collective-permute-start | bytes 294920 | tf_op jit(solution)/shard_map/ppermute | solution.py:573
  41.3 6.8 %collective-permute-start.7 = (f32[4,32,128]{2,1,0:T(8,128)S(1)}, f32[4,32,128]{2,1,0:T(8,128)S(1)}, u32[]{:S(2)}, u32[]{:S(2)}) collective-permute-start(f32[4,32,128]{2,1,0:T(8,128)S(1)} %get-tuple-element.40), channel_id=1, source_target_pairs={{0,16},{16,32},{32,48},{48,64},{64,80},{80,96},{96,112},{112,0},{1... | collective-permute-start | bytes 196616 | tf_op jit(solution)/shard_map/ppermute | solution.py:565
  43.0 11.0 %collective-permute-start.8 = (f32[4,32,128]{2,1,0:T(8,128)S(1)}, f32[4,32,128]{2,1,0:T(8,128)S(1)}, u32[]{:S(2)}, u32[]{:S(2)}) collective-permute-start(f32[4,32,128]{2,1,0:T(8,128)S(1)} %get-tuple-element.41), channel_id=1, source_target_pairs={{0,1},{1,2},{2,3},{3,4},{4,5},{5,6},{6,7},{7,8},{8,9},{9,10},{10,1... | collective-permute-start | bytes 196616 | tf_op jit(solution)/shard_map/ppermute | solution.py:567
  54.4 8.2 %collective-permute-start.10 = (f32[4,64,128]{2,1,0:T(8,128)S(1)}, f32[4,64,128]{2,1,0:T(8,128)S(1)}, u32[]{:S(2)}, u32[]{:S(2)}) collective-permute-start(f32[4,64,128]{2,1,0:T(8,128)S(1)} %get-tuple-element.44), channel_id=1, source_target_pairs={{0,112},{16,0},{32,16},{48,32},{64,48},{80,64},{96,80},{112,96},{1... | collective-permute-start | bytes 393224 | tf_op jit(solution)/shard_map/ppermute | solution.py:565
  55.9 6.7 %collective-permute-start.11 = (f32[4,64,128]{2,1,0:T(8,128)S(1)}, f32[4,64,128]{2,1,0:T(8,128)S(1)}, u32[]{:S(2)}, u32[]{:S(2)}) collective-permute-start(f32[4,64,128]{2,1,0:T(8,128)S(1)} %get-tuple-element.45), channel_id=1, source_target_pairs={{0,15},{1,0},{2,1},{3,2},{4,3},{5,4},{6,5},{7,6},{8,7},{9,8},{10,9... | collective-permute-start | bytes 393224 | tf_op jit(solution)/shard_map/ppermute | solution.py:567
  57.3 5.3 %collective-permute-start.12 = (f32[4,40,128]{2,1,0:T(8,128)S(1)}, f32[4,40,128]{2,1,0:T(8,128)S(1)}, u32[]{:S(2)}, u32[]{:S(2)}) collective-permute-start(f32[4,40,128]{2,1,0:T(8,128)S(1)} %get-tuple-element.46), channel_id=1, source_target_pairs={{0,127},{1,112},{2,113},{3,114},{4,115},{5,116},{6,117},{7,118},{8... | collective-permute-start | bytes 245768 | tf_op jit(solution)/shard_map/ppermute | solution.py:573
where the time goes:
time: 76.3 us; the launch traced here: 76.1 us
  Pallas kernels  31.2 us (41%)
  waiting for transfers between devices  25.6 us (34%)
  starting transfers between devices  16.5 us (22%)
  other arithmetic  1.9 us (2%)
  between operations  0.84 us (1%)
    pallas_call x5, Pallas kernels, call(): pl.pallas_call(kernel, name=name, out_shape=[jax.ShapeDtypeStruct(shape,...  31.2 us
    ppermute x5, waiting for transfers between devices, neighbor(): lax.ppermute(value, 'gy', [(i, (i + dy) % size_y) for i in range(size_y)])  12 us
    ppermute x5, starting transfers between devices, neighbor(): lax.ppermute(value, 'gy', [(i, (i + dy) % size_y) for i in range(size_y)])  10.5 us
    ppermute x5, waiting for transfers between devices, neighbor(): lax.ppermute(value, 'gx', [(i, (i + dx) % size_x) for i in range(size_x)])  7.7 us
    ppermute x3, waiting for transfers between devices, neighbor(): return lax.ppermute(value, ('gx', 'gy'), pairs)  5.9 us
    ppermute x5, starting transfers between devices, neighbor(): lax.ppermute(value, 'gx', [(i, (i + dx) % size_x) for i in range(size_x)])  4.75 us
  transfers between devices with their start and end apart: 13, of which 7 were waited for; matrix products, arithmetic and copies ran while one was open for 1% of the time, Pallas kernels for 2%

commit v1 on v0

--- a/solution.py
+++ b/solution.py
@@ -16,8 +16,8 @@
 mib = 1024 * 1024
 pieces = 31
 tiles = 9
-msg_tiles = 13
-msg_rows = msg_tiles * 16
+msg_rows = tiles * 16
+way_rows = 64
 
 
 def axis_tables(shift, inside, scale):
@@ -44,51 +44,50 @@
     return high, value - high
 
 
-def deposit_kernel(
-    code_s, brick_s, f_hbm, v_hbm, c_hbm, k_hbm, m_hbm, t_hbm, o_hbm,
-    own_ref, frac_ref, xm_ref, ym_ref, yp_ref, xp_ref,
-    f_ref, v_ref, c_ref, k_ref, m_ref, t_ref, o_ref, sems,
-    raw, sa, sb, acc, cnt, out,
+def clear_rows(ref, rows):
+    def step(n, carry):
+        ref[pl.ds(pl.multiple_of(n * 128, 128), 128), :] = jnp.zeros((128, 128), f32)
+        return carry
+
+    lax.fori_loop(0, rows // 128, step, 0)
+
+
+def deposit_blocks(
+    base, count, info_s, brick_s, target_of, hbm_refs, vmem_refs, sems, first, second, acc, after
 ):
-    pairs = (
-        (f_hbm, f_ref), (v_hbm, v_ref), (c_hbm, c_ref), (k_hbm, k_ref),
-        (m_hbm, m_ref), (t_hbm, t_ref), (o_hbm, o_ref),
-    )
-    copies = [pltpu.make_async_copy(a, b, sems.at[n]) for n, (a, b) in enumerate(pairs)]
+    copies = [
+        pltpu.make_async_copy(a, b, sems.at[n]) for n, (a, b) in enumerate(zip(hbm_refs, vmem_refs))
+    ]
     for copy in copies:
         copy.start()
-    def clear(step, carry):
-        acc[pl.ds(pl.multiple_of(step * 256, 256), 256), :] = jnp.zeros((256, 128), f32)
-        return carry
-
-    lax.fori_loop(0, 32, clear, 0)
-    out[...] = jnp.zeros(out.shape, f32)
-    sa[...] = jnp.zeros(sa.shape, f32)
-    sb[...] = jnp.zeros(sb.shape, f32)
-    for code in range(9):
-        cnt[code] = 0
+    f_ref, v_ref, c_ref, k_ref, m_ref, t_ref, o_ref = vmem_refs
+    clear_rows(acc, 128 * 32)
+    for _, sa, sb in (first, second):
+        sa[...] = jnp.zeros(sa.shape, f32)
+        sb[...] = jnp.zeros(sb.shape, f32)
     for copy in copies:
         copy.wait()
     row_no = lax.broadcasted_iota(jnp.int32, (32, 1), 0)
 
-    def group(g, carry):
+    def build(g, raw, sa, sb):
+        blocks = [info_s[base + g * 8 + j] for j in range(8)]
         for j in range(8):
-            lanes = pl.ds(pl.multiple_of((g * 8 + j) * 128, 128), 128)
+            lanes = pl.ds(pl.multiple_of(blocks[j] * 128, 128), 128)
             raw[j * 40 : j * 40 + 3, :] = f_ref[:, lanes]
             raw[j * 40 + 3 : j * 40 + 6, :] = v_ref[:, lanes]
+            raw[j * 40 + 6 : j * 40 + 7, :] = m_ref[pl.ds(blocks[j], 1), :]
+            raw[j * 40 + 7 : j * 40 + 8, :] = t_ref[pl.ds(blocks[j], 1), :]
             raw[j * 40 + 8 : j * 40 + 17, :] = c_ref[:, lanes]
             raw[j * 40 + 24 : j * 40 + 33, :] = k_ref[:, lanes]
-        rows = pl.ds(pl.multiple_of(g * 8, 8), 8)
-        mass = m_ref[rows, :]
-        heat = mass * t_ref[rows, :]
-        offset = o_ref[rows, :]
+            raw[j * 40 + 33 : j * 40 + 34, :] = o_ref[pl.ds(blocks[j], 1), :].astype(f32)
 
         def get(row):
             return raw[pl.ds(row, 8, stride=40), :]
 
+        mass = get(6)
+        heat = mass * get(7)
+        offset = get(33).astype(jnp.int32)
         inside = [get(d) for d in range(3)]
-        for d in range(3):
-            frac_ref[d, rows, :] = inside[d]
         wx, rx = axis_tables(offset >> 4, inside[0], 1.0)
         for a in range(3):
             push = mass * get(3 + a)
@@ -110,6 +109,9 @@
                 sb[pl.ds(r * 8, 8), :] = wy[jy] * wz[jz]
                 sb[pl.ds((40 + r) * 8, 8), :] = ry[jy] * wz[jz]
                 sb[pl.ds((80 + r) * 8, 8), :] = wy[jy] * rz[jz]
+
+    def work(g, raw, sa, sb):
+        blocks = [info_s[base + g * 8 + j] for j in range(8)]
         sums = []
         for j in range(8):
             left = jnp.concatenate(
@@ -126,59 +128,98 @@
             both = both[:32] + both[32:]
             sums.append(both[:, :40] + both[:, 40:])
         for j in range(8):
-            b = g * 8 + j
-            code = code_s[b]
-            rank = cnt[code]
-            cnt[code] = rank + 1
-            stays = code == 4
-            way = jnp.where(code > 4, code - 1, code)
-            brick = brick_s[b]
-            target = jnp.where(stays, brick, 128 + way * 16 + rank)
-            mark = jnp.where(stays, 0, brick + 1).astype(f32)
+            target, mark = target_of(g * 8 + j, blocks[j])
             spot = pl.ds(pl.multiple_of(target * 32, 32), 32)
             acc[spot, 0:40] = acc[spot, 0:40] + (sums[j] + jnp.where(row_no == 30, mark, 0.0))
-            at = jnp.where(stays, 8 * msg_rows, (way * msg_tiles + 9) * 16 + rank)
-            for d in range(3):
-                out[pl.ds(at + d * 16, 1), :] = raw[j * 40 + d : j * 40 + d + 1, :]
-            out[pl.ds(at + 48, 1), :] = o_ref[pl.ds(b, 1), :].astype(f32)
+            after(j, blocks[j], raw)
+
+    def pair(i, carry):
+        build(2 * i + 1, *second)
+        work(2 * i, *first)
+        build(2 * i + 2, *first)
+        work(2 * i + 1, *second)
         return carry
 
-    lax.fori_loop(0, 16, group, 0)
+    build(0, *first)
+    lax.fori_loop(0, (count + 15) // 16, pair, 0)
+
+
+def packed(acc, chunk):
     lane = lax.broadcasted_iota(jnp.int32, (8, 128), 1)
-
-    def packed(chunk):
-        total = [jnp.zeros((8, 128), f32) for _ in range(tiles)]
-        for i in range(pieces):
-            piece = acc[pl.ds(chunk * 256 + i, 8, stride=32), :]
-            if i == 30:
-                piece = jnp.where(lane < 36, piece, 0.0)
-            tile, at = divmod(i * 36, 128)
-            if at:
-                piece = pltpu.roll(piece, at, 1)
-            if at + 36 > 128:
-                total[tile] = total[tile] + jnp.where(lane >= at, piece, 0.0)
-                total[tile + 1] = total[tile + 1] + jnp.where(lane < at, piece, 0.0)
-            else:
-                total[tile] = total[tile] + piece
-        return total
+    total = [jnp.zeros((8, 128), f32) for _ in range(tiles)]
+    for i in range(pieces):
+        piece = acc[pl.ds(chunk * 256 + i, 8, stride=32), :]
+        if i == 30:
+            piece = jnp.where(lane < 36, piece, 0.0)
+        tile, at = divmod(i * 36, 128)
+        if at:
+            piece = pltpu.roll(piece, at, 1)
+        if at + 36 > 128:
+            total[tile] = total[tile] + jnp.where(lane >= at, piece, 0.0)
+            total[tile + 1] = total[tile + 1] + jnp.where(lane < at, piece, 0.0)
+        else:
+            total[tile] = total[tile] + piece
+    return total
+
+
+def outgoing_kernel(
+    info_s, brick_s, f_hbm, v_hbm, c_hbm, k_hbm, m_hbm, t_hbm, o_hbm,
+    xm_ref, ym_ref, yp_ref, xp_ref,
+    f_ref, v_ref, c_ref, k_ref, m_ref, t_ref, o_ref, sems, raw, sa, sb, raw2, sa2, sb2, acc,
+):
+    def target_of(entry, block):
+        return info_s[160 + entry], (brick_s[block] + 1).astype(f32)
+
+    deposit_blocks(
+        0, info_s[544], info_s, brick_s, target_of,
+        (f_hbm, v_hbm, c_hbm, k_hbm, m_hbm, t_hbm, o_hbm),
+        (f_ref, v_ref, c_ref, k_ref, m_ref, t_ref, o_ref),
+        sems, (raw, sa, sb), (raw2, sa2, sb2), acc, lambda j, block, raw: None,
+    )
+    for first, count, ref in ((0, 3, xm_ref), (3, 1, ym_ref), (4, 1, yp_ref), (5, 3, xp_ref)):
+        for n in range(count):
+            for half in range(2):
+
+                def some(n=n, half=half, first=first, ref=ref):
+                    for tile, value in enumerate(packed(acc, (first + n) * 2 + half)):
+                        at = n * msg_rows + tile * 16 + half * 8
+                        ref[at : at + 8, :] = value
+
+                def none(n=n, half=half, ref=ref):
+                    for tile in range(tiles):
+                        at = n * msg_rows + tile * 16 + half * 8
+                        ref[at : at + 8, :] = jnp.zeros((8, 128), f32)
+
+                lax.cond(info_s[552 + first + n] > half * 8, some, none)
+
+
+def staying_kernel(
+    info_s, brick_s, f_hbm, v_hbm, c_hbm, k_hbm, m_hbm, t_hbm, o_hbm,
+    own_ref, frac_ref,
+    f_ref, v_ref, c_ref, k_ref, m_ref, t_ref, o_ref, sems, raw, sa, sb, raw2, sa2, sb2, acc,
+):
+    frac_ref[...] = jnp.zeros(frac_ref.shape, f32)
+
+    def target_of(entry, block):
+        return jnp.where(entry < info_s[545], brick_s[block], 128), jnp.float32(0.0)
+
+    def after(j, block, raw):
+        for d in range(3):
+            frac_ref[d, pl.ds(block, 1), :] = raw[j * 40 + d : j * 40 + d + 1, :]
+
+    deposit_blocks(
+        320, info_s[545], info_s, brick_s, target_of,
+        (f_hbm, v_hbm, c_hbm, k_hbm, m_hbm, t_hbm, o_hbm),
+        (f_ref, v_ref, c_ref, k_ref, m_ref, t_ref, o_ref),
+        sems, (raw, sa, sb), (raw2, sa2, sb2), acc, after,
+    )
 
     def pack_own(chunk, carry):
-        for tile, value in enumerate(packed(chunk)):
+        for tile, value in enumerate(packed(acc, chunk)):
             own_ref[tile, pl.ds(pl.multiple_of(chunk * 8, 8), 8), :] = value
         return carry
 
-    def pack_out(chunk, carry):
-        base = (chunk // 2) * msg_rows + (chunk % 2) * 8
-        for tile, value in enumerate(packed(chunk + 16)):
-            out[pl.ds(pl.multiple_of(base + tile * 16, 8), 8), :] = value
-        return carry
-
     lax.fori_loop(0, 16, pack_own, 0)
-    lax.fori_loop(0, 16, pack_out, 0)
-    xm_ref[...] = out[0 : 3 * msg_rows, :]
-    ym_ref[...] = out[3 * msg_rows : 4 * msg_rows, :]
-    yp_ref[...] = out[4 * msg_rows : 5 * msg_rows, :]
-    xp_ref[...] = out[5 * msg_rows : 8 * msg_rows, :]
 
 
 def runs_left():
@@ -214,7 +255,7 @@
 
     def arrived(tile):
         return jnp.concatenate(
-            [ref[pl.ds((at * msg_tiles + tile) * 16, 16), :] for ref, at in places], axis=0
+            [ref[pl.ds(at * msg_rows + tile * 16, 16), :] for ref, at in places], axis=0
         )
 
     rows = lax.broadcasted_iota(jnp.int32, (128, 128), 0)
@@ -248,9 +289,41 @@
                 ref[kz, to:, :] = jnp.zeros((ref.shape[1] - to, 128), f32)
 
 
-def static_kernel(
-    table, solid_ref, rough_ref, choice_ref, rim_ref, own, ml, mb, md, cells
+def prepare_kernel(
+    table, code_s, solid_ref, rough_ref, choice_ref, rim_ref, f_ref, o_ref,
+    info, own, xp, xm, cells, fo, cnt,
 ):
+    fo[...] = jnp.zeros(fo.shape, f32)
+    for n in range(10):
+        cnt[n] = 0
+
+    def sort(b, carry):
+        code = code_s[b]
+        rank = cnt[code]
+        cnt[code] = rank + 1
+        leaves = code != 4
+        way = jnp.where(code > 4, code - 1, code)
+        gone = cnt[9]
+        slot = way * 16 + rank
+        info[jnp.where(leaves, gone, 320 + b - gone)] = b
+        info[jnp.where(leaves, 160 + gone, 639)] = slot
+        cnt[9] = gone + jnp.where(leaves, 1, 0)
+        at = pl.multiple_of(jnp.where(leaves, slot, 128) * 4, 4)
+        lanes = pl.ds(pl.multiple_of(b * 128, 128), 128)
+        fo[pl.ds(at, 3), :] = f_ref[:, lanes]
+        fo[pl.ds(at + 3, 1), :] = o_ref[pl.ds(b, 1), :].astype(f32)
+        return carry
+
+    lax.fori_loop(0, 128, sort, 0, unroll=4)
+    gone = cnt[9]
+    for n in range(24):
+        info[gone + n] = 0
+        info[160 + gone + n] = 128
+        info[320 + 128 - gone + n] = 0
+    for n in range(8):
+        info[552 + n] = cnt[n if n < 4 else n + 1]
+    info[544] = gone
+    info[545] = 128 - gone
     for x in range(4):
         rows = slice(x * 4, x * 4 + 4)
         cells[rows, :] = solid_ref[x].astype(f32)
@@ -275,49 +348,100 @@
         lanes = slice(kz * 128, kz * 128 + 128)
         for field, part in enumerate((value[0:16], rim, value[16:32], *normal)):
             own[kz, field * 16 : field * 16 + 16, :] = part[:, lanes]
-        ml[kz, 30:32, :] = jnp.zeros((2, 128), f32)
-        mb[kz, 30:32, :] = jnp.zeros((2, 128), f32)
-        md[kz, 22:24, :] = jnp.zeros((2, 128), f32)
-        for field in range(2):
-            for x in range(3):
-                at = field * 9 + x * 3
-                low_row, high_row = field * 16 + x * 4, field * 16 + x * 4 + 4
-                ml[kz, at : at + 3, :] = own[kz, high_row : high_row + 3, :]
-                mb[kz, at : at + 3, :] = own[kz, low_row + 1 : low_row + 4, :]
-                md[kz, at : at + 3, :] = own[kz, high_row + 1 : high_row + 4, :]
+        at = 192 + kz * 40
+        xp[at : at + 12, :] = own[kz, 4:16, :]
+        xp[at + 12 : at + 24, :] = own[kz, 20:32, :]
         for field in range(4):
-            row = field * 16 + 32
-            ml[kz, 18 + field * 3 : 21 + field * 3, :] = own[kz, row + 12 : row + 15, :]
-            for x in range(3):
-                at = 18 + field * 3 + x
-                mb[kz, at : at + 1, :] = own[kz, row + x * 4 + 3 : row + x * 4 + 4, :]
-            md[kz, 18 + field : 19 + field, :] = own[kz, row + 15 : row + 16, :]
-
-
-def update_kernel(
-    mo, rl, rb, rd, own, sl, sb, sd, hl, hb, hd, ko, warm, push, region, rough, normal
-):
+            row = 32 + field * 16
+            xp[at + 24 + field * 4 : at + 28 + field * 4, :] = own[kz, row + 12 : row + 16, :]
+        xm[192 + kz * 8 : 200 + kz * 8, :] = own[kz, 0:8, :]
+    xm[0:192, :] = fo[0:192, :]
+    for way in range(2):
+        own[4 + way, 0:64, :] = fo[192 + way * 64 : 256 + way * 64, :]
+        own[4 + way, 64:96, :] = jnp.zeros((32, 128), f32)
+    xp[0:192, :] = fo[320:512, :]
+
+
+def relay_kernel(left, right, own, up, down):
+    for way, ref in ((0, down), (1, up)):
+        at = 128 * way
+        ref[0:64, :] = left[at : at + 64, :]
+        ref[64:128, :] = own[4 + way, 0:64, :]
+        ref[128:192, :] = right[at : at + 64, :]
     for kz in range(4):
-        for field in range(2):
-            to = 3 * field
-            for x in range(3):
-                at = field * 9 + x * 3
+        lrow, rrow = 192 + kz * 40, 192 + kz * 8
+        to = 192 + kz * 64
+        for x in range(4):
+            up[to + x * 3 : to + x * 3 + 3, :] = own[kz, x * 4 + 1 : x * 4 + 4, :]
+        for x in range(3):
+            row = 16 + x * 4
+            up[to + 12 + x * 3 : to + 15 + x * 3, :] = own[kz, row + 1 : row + 4, :]
+            up[to + 33 + x * 3 : to + 36 + x * 3, :] = left[lrow + x * 4 + 1 : lrow + x * 4 + 4, :]
+            row = lrow + 12 + x * 4
+            up[to + 42 + x * 3 : to + 45 + x * 3, :] = left[row + 1 : row + 4, :]
+            for field in range(4):
+                row = 32 + field * 16 + x * 4 + 3
+                at = to + 21 + field * 3 + x
+                up[at : at + 1, :] = own[kz, row : row + 1, :]
+        for field in range(4):
+            row = lrow + 24 + field * 4 + 3
+            up[to + 51 + field : to + 52 + field, :] = left[row : row + 1, :]
+        for x in range(2):
+            up[to + 55 + x * 3 : to + 58 + x * 3, :] = right[rrow + x * 4 + 1 : rrow + x * 4 + 4, :]
+        up[to + 61 : to + 64, :] = jnp.zeros((3, 128), f32)
+        to = 192 + kz * 24
+        for x in range(4):
+            down[to + x * 2 : to + x * 2 + 2, :] = own[kz, x * 4 : x * 4 + 2, :]
+        for x in range(3):
+            down[to + 8 + x * 2 : to + 10 + x * 2, :] = left[lrow + x * 4 : lrow + x * 4 + 2, :]
+        for x in range(2):
+            down[to + 14 + x * 2 : to + 16 + x * 2, :] = right[rrow + x * 4 : rrow + x * 4 + 2, :]
+        down[to + 18 : to + 24, :] = jnp.zeros((6, 128), f32)
+
+
+def assemble_kernel(own, left, right, below, above, region, rough, normal, solid):
+    solid[...] = jnp.zeros(solid.shape, f32)
+    for kz in range(4):
+        lrow, rrow, brow, arow = 192 + kz * 40, 192 + kz * 8, 192 + kz * 64, 192 + kz * 24
+        for x in range(3):
+            for field in range(2):
                 inner, outer = x * 6, (x + 3) * 6
+                diagonal = brow + 33 + field * 9 + x * 3
+                region[field, kz, inner : inner + 3, :] = below[diagonal : diagonal + 3, :]
+                row = lrow + field * 12 + x * 4
+                region[field, kz, inner + 3 : inner + 6, :] = left[row : row + 3, :]
+                row = brow + field * 12 + x * 3
+                region[field, kz, outer : outer + 3, :] = below[row : row + 3, :]
                 row = field * 16 + x * 4
-                region[to, kz, inner : inner + 3, :] = sd[kz, at : at + 3, :]
-                region[to, kz, inner + 3 : inner + 6, :] = sl[kz, at : at + 3, :]
-                region[to, kz, outer : outer + 3, :] = sb[kz, at : at + 3, :]
-                region[to, kz, outer + 3 : outer + 6, :] = own[kz, row : row + 3, :]
+                region[field, kz, outer + 3 : outer + 6, :] = own[kz, row : row + 3, :]
+            to = x * 10
+            solid[kz, to : to + 3, :] = below[brow + 33 + x * 3 : brow + 36 + x * 3, :]
+            solid[kz, to + 3 : to + 7, :] = left[lrow + x * 4 : lrow + x * 4 + 4, :]
+            solid[kz, to + 7 : to + 9, :] = above[arow + 8 + x * 2 : arow + 10 + x * 2, :]
+        for x in range(4):
+            to = (x + 3) * 10
+            solid[kz, to : to + 3, :] = below[brow + x * 3 : brow + x * 3 + 3, :]
+            solid[kz, to + 3 : to + 7, :] = own[kz, x * 4 : x * 4 + 4, :]
+            solid[kz, to + 7 : to + 9, :] = above[arow + x * 2 : arow + x * 2 + 2, :]
+        for x in range(2):
+            to = (x + 7) * 10
+            solid[kz, to : to + 3, :] = below[brow + 55 + x * 3 : brow + 58 + x * 3, :]
+            solid[kz, to + 3 : to + 7, :] = right[rrow + x * 4 : rrow + x * 4 + 4, :]
+            solid[kz, to + 7 : to + 9, :] = above[arow + 14 + x * 2 : arow + 16 + x * 2, :]
         for field in range(4):
             ref = rough if field == 0 else normal.at[field - 1]
-            at = 18 + field * 3
-            row = 32 + field * 16
-            ref[kz, 0:1, :] = sd[kz, 18 + field : 19 + field, :]
-            ref[kz, 1:4, :] = sl[kz, at : at + 3, :]
+            ref[kz, 0:1, :] = below[brow + 51 + field : brow + 52 + field, :]
+            row = lrow + 24 + field * 4
+            ref[kz, 1:4, :] = left[row : row + 3, :]
             for x in range(3):
                 to = (x + 1) * 4
-                ref[kz, to : to + 1, :] = sb[kz, at + x : at + x + 1, :]
-                ref[kz, to + 1 : to + 4, :] = own[kz, row + x * 4 : row + x * 4 + 3, :]
+                row = brow + 21 + field * 3 + x
+                ref[kz, to : to + 1, :] = below[row : row + 1, :]
+                row = 32 + field * 16 + x * 4
+                ref[kz, to + 1 : to + 4, :] = own[kz, row : row + 3, :]
+
+
+def update_kernel(mo, rl, rb, rd, region, rough, normal, hl, hb, hd, ko, warm, push):
     warm[...] = jnp.zeros(warm.shape, f32)
     for kz in range(4):
         for ref, dx, dy in ((mo, 2, 2), (rl, 0, 2), (rb, 2, 0), (rd, 0, 0)):
@@ -369,12 +493,10 @@
             value = jnp.where(slips, wall[a] + tangent[a] * factor, moving[a])
             push[a, kz] = jnp.where(solid, wall[a], value)
         heat = warm[1, kz, 0:36, :] / jnp.maximum(warm[0, kz, 0:36, :], mass_floor)
-        warm[1, kz, 0:36, :] = jnp.where(region[0, kz] == 1.0, region[3, kz], heat)
+        warm[1, kz, 0:36, :] = jnp.where(region[0, kz] == 1.0, region[1, kz], heat)
     for kz in range(4):
         ko[kz, 0:36, :] = warm[1, kz, 0:36, :]
         ko[kz, 36:40, :] = jnp.zeros((4, 128), f32)
-        ko[kz, 88:124, :] = region[0, kz]
-        ko[kz, 124:128, :] = jnp.zeros((4, 128), f32)
         hl[kz, 0:24, :] = warm[1, kz, 12:36, :]
         for c in range(3):
             ko[kz, 40 + c * 16 : 56 + c * 16, :] = push[c, kz]
@@ -389,43 +511,25 @@
             hb[kz, x * 4 : x * 4 + 4, :] = warm[1, kz, x * 6 + 2 : x * 6 + 6, :]
         for x in range(4):
             hd[kz, x * 4 : x * 4 + 4, :] = warm[1, kz, (x + 2) * 6 + 2 : (x + 2) * 6 + 6, :]
-        for x in range(3):
-            row = (x + 2) * 6
-            hl[kz, 48 + x * 5 : 53 + x * 5, :] = region[0, kz, row + 1 : row + 6, :]
-            hd[kz, 28 + x * 3 : 31 + x * 3, :] = region[0, kz, row + 2 : row + 5, :]
-        for x in range(5):
-            row = (x + 1) * 6
-            hb[kz, 48 + x * 3 : 51 + x * 3, :] = region[0, kz, row + 2 : row + 5, :]
-        hl[kz, 63:64, :] = jnp.zeros((1, 128), f32)
-        hb[kz, 63:64, :] = jnp.zeros((1, 128), f32)
-        hd[kz, 37:40, :] = jnp.zeros((3, 128), f32)
+        hd[kz, 28:32, :] = jnp.zeros((4, 128), f32)
 
 
 def collect_kernel(
-    code_s, brick_s, came_s, ko, rl, rb, rd, frac, o_ref, rxp, rxm, ryp, rym,
+    code_s, brick_s, came_s, ko, rl, rb, rd, solid, frac, o_ref, rxp, rxm, ryp, rym,
     move_ref, grad_ref, warm_ref, gvel_ref, gtemp_ref,
-    heat, solid, speed, cells, fine, coarse, turn, lu, fo, sb, sw,
+    heat, speed, cells, fine, coarse, turn, lu, fo, sb, sw, sb2, sw2,
 ):
     lane = lax.broadcasted_iota(jnp.int32, (8, 128), 1)[0:1]
     heat[...] = jnp.zeros(heat.shape, f32)
-    solid[...] = jnp.zeros(solid.shape, f32)
     for kz in range(4):
         for x in range(6):
             to = 16 + x * 10
             heat[0, kz, to : to + 6, :] = ko[kz, x * 6 : x * 6 + 6, :]
             heat[0, kz, to + 6 : to + 10, :] = rb[kz, x * 4 : x * 4 + 4, :]
-            solid[kz, x * 10 : x * 10 + 6, :] = ko[kz, 88 + x * 6 : 94 + x * 6, :]
         for x in range(4):
             to = 16 + (x + 6) * 10
             heat[0, kz, to : to + 6, :] = rl[kz, x * 6 : x * 6 + 6, :]
             heat[0, kz, to + 6 : to + 10, :] = rd[kz, x * 4 : x * 4 + 4, :]
-        for x in range(3):
-            to = (x + 6) * 10
-            solid[kz, to + 1 : to + 6, :] = rl[kz, 48 + x * 5 : 53 + x * 5, :]
-            solid[kz, to + 6 : to + 9, :] = rd[kz, 28 + x * 3 : 31 + x * 3, :]
-        for x in range(5):
-            to = (x + 1) * 10
-            solid[kz, to + 6 : to + 9, :] = rb[kz, 48 + x * 3 : 51 + x * 3, :]
         for c in range(3):
             for x in range(4):
                 speed[c, kz, x * 6 : x * 6 + 4, :] = ko[kz, 40 + c * 16 + x * 4 : 44 + c * 16 + x * 4, :]
@@ -505,10 +609,11 @@
     places = [(ryp, 0), (rxp, 1), (rym, 0), (ryp, 1), (rym, 1), (ryp, 2), (rxm, 1), (rym, 2)]
     for g, (ref, at) in enumerate(places):
         for d in range(4):
-            fo[d, 128 + g * 16 : 144 + g * 16, :] = ref[pl.ds((at * msg_tiles + 9 + d) * 16, 16), :]
+            fo[d, 128 + g * 16 : 144 + g * 16, :] = ref[pl.ds(at * way_rows + d, 16, stride=4), :]
     sb[...] = jnp.zeros(sb.shape, f32)
-
-    def group(g, carry):
+    sb2[...] = jnp.zeros(sb2.shape, f32)
+
+    def build(g, sb, sw):
         rows = pl.ds(pl.multiple_of(g * 8, 8), 8)
         offset = fo[3, rows, :].astype(jnp.int32)
         wx, rx = axis_tables(offset >> 4, fo[0, rows, :], 4.0)
@@ -524,6 +629,8 @@
                 sb[pl.ds(r * 8, 8), :] = wy[jy] * wz[jz]
                 sb[pl.ds((40 + r) * 8, 8), :] = ry[jy] * wz[jz]
                 sb[pl.ds((80 + r) * 8, 8), :] = wy[jy] * rz[jz]
+
+    def work(g, sb, sw):
         for j in range(8):
             slot = g * 8 + j
             home = jnp.minimum(slot, 127)
@@ -554,9 +661,16 @@
                 part = over_x(weight, column)
                 for a in range(3):
                     grad_ref[a * 3 + k : a * 3 + k + 1, lanes] = part[a : a + 1]
+
+    def pair(i, carry):
+        build(2 * i + 1, sb2, sw2)
+        work(2 * i, sb, sw)
+        build(jnp.minimum(2 * i + 2, 31), sb, sw)
+        work(2 * i + 1, sb2, sw2)
         return carry
 
-    lax.fori_loop(0, 32, group, 0)
+    build(0, sb, sw)
+    lax.fori_loop(0, 16, pair, 0)
 
 
 def neighbor(value, dx, dy):
@@ -573,7 +687,9 @@
     return lax.ppermute(value, ("gx", "gy"), pairs)
 
 
-def call(kernel, name, inputs, scalars, outputs, scratch, left_there=0, limit=50):
+def call(
+    kernel, name, inputs, scalars, outputs, scratch, left_there=0, limit=50, flops=1e8, listed=0
+):
     in_specs = (
         [pl.BlockSpec(memory_space=pltpu.SMEM)] * scalars
         + [pl.BlockSpec(memory_space=pltpu.HBM)] * left_there
@@ -584,7 +700,11 @@
         name=name,
         out_shape=[jax.ShapeDtypeStruct(shape, dtype) for shape, dtype in outputs],
         in_specs=in_specs,
-        out_specs=[pl.BlockSpec(memory_space=pltpu.VMEM)] * len(outputs),
+        out_specs=[pl.BlockSpec(memory_space=pltpu.SMEM)] * listed
+        + [pl.BlockSpec(memory_space=pltpu.VMEM)] * (len(outputs) - listed),
+        cost_estimate=pl.CostEstimate(
+            flops=int(flops), bytes_accessed=int(flops / 300), transcendentals=0
+        ),
         scratch_shapes=scratch,
         compiler_params=pltpu.CompilerParams(vmem_limit_bytes=limit * mib),
     )(*inputs)
@@ -611,75 +731,120 @@
     rim_thermal_level,
 ):
     offset = anchor_voxel_shift.reshape(128, 128)
-    own, frac, xm, ym, yp, xp = call(
-        deposit_kernel,
-        "deposit",
+    info, static, sxp, sxm = call(
+        prepare_kernel,
+        "prepare",
         (
+            facing_unit_vectors,
             group_migration_label,
-            group_resting_volume,
+            cylinder_shell_flag,
+            rough_surface_flag,
+            voxel_facing_choice,
+            rim_thermal_level,
             subvoxel_location_share,
-            point_motion_vector,
-            linear_gradient_matrix,
-            kirchhoff_tension_matrix,
-            point_inertia_amounts.reshape(128, 128),
-            point_thermal_state.reshape(128, 128),
             offset,
         ),
         2,
         [
-            ((tiles, 128, 128), f32),
-            ((3, 128, 128), f32),
+            ((640,), jnp.int32),
+            ((6, 96, 128), f32),
+            ((352, 128), f32),
+            ((224, 128), f32),
+        ],
+        [vmem(64, 512), vmem(520, 128), pltpu.SMEM((16,), jnp.int32)],
+        limit=64,
+        flops=2e9,
+        listed=1,
+    )
+    rsxp = neighbor(sxp, 1, 0)
+    rsxm = neighbor(sxm, -1, 0)
+    block_args = (
+        group_resting_volume,
+        subvoxel_location_share,
+        point_motion_vector,
+        linear_gradient_matrix,
+        kirchhoff_tension_matrix,
+        point_inertia_amounts.reshape(128, 128),
+        point_thermal_state.reshape(128, 128),
+        offset,
+    )
+    block_scratch = [
+        vmem(3, 16384),
+        vmem(3, 16384),
+        vmem(9, 16384),
+        vmem(9, 16384),
+        vmem(128, 128),
+        vmem(128, 128),
+        pltpu.VMEM((128, 128), jnp.int32),
+        pltpu.SemaphoreType.DMA((7,)),
+        vmem(320, 128),
+        vmem(96 * 8, 128),
+        vmem(120 * 8, 128),
+        vmem(320, 128),
+        vmem(96 * 8, 128),
+        vmem(120 * 8, 128),
+        vmem(129 * 32, 128),
+    ]
+    xm, ym, yp, xp = call(
+        outgoing_kernel,
+        "outgoing",
+        (info,) + block_args,
+        2,
+        [
             ((3 * msg_rows, 128), f32),
             ((msg_rows, 128), f32),
             ((msg_rows, 128), f32),
             ((3 * msg_rows, 128), f32),
         ],
-        [
-            vmem(3, 16384),
-            vmem(3, 16384),
-            vmem(9, 16384),
-            vmem(9, 16384),
-            vmem(128, 128),
-            vmem(128, 128),
-            pltpu.VMEM((128, 128), jnp.int32),
-            pltpu.SemaphoreType.DMA((7,)),
-            vmem(320, 128),
-            vmem(96 * 8, 128),
-            vmem(120 * 8, 128),
-            vmem(256 * 32, 128),
-            pltpu.SMEM((16,), jnp.int32),
-            vmem(8 * msg_rows + 64, 128),
-        ],
+        block_scratch,
         7,
         64,
-    )
+        flops=6e9,
+    )
+    xm, xp, rsxp, rsxm = lax.optimization_barrier((xm, xp, rsxp, rsxm))
     rxp = neighbor(xp, 1, 0)
     rxm = neighbor(xm, -1, 0)
-    ryp = neighbor(
-        jnp.concatenate([rxp[2 * msg_rows :], yp, rxm[2 * msg_rows :]], axis=0), 0, 1
-    )
-    rym = neighbor(jnp.concatenate([rxp[:msg_rows], ym, rxm[:msg_rows]], axis=0), 0, -1)
-
-    static, sl, sb, sd = call(
-        static_kernel,
-        "static",
-        (
-            facing_unit_vectors,
-            cylinder_shell_flag,
-            rough_surface_flag,
-            voxel_facing_choice,
-            rim_thermal_level,
-        ),
-        1,
+    up, down = call(
+        relay_kernel,
+        "relay",
+        (rsxp, rsxm, static),
+        0,
+        [((448, 128), f32), ((288, 128), f32)],
+        [],
+        flops=5e8,
+    )
+    rsyp = neighbor(up, 0, 1)
+    rsym = neighbor(down, 0, -1)
+    up = jnp.concatenate([rxp[2 * msg_rows :], yp, rxm[2 * msg_rows :]], axis=0)
+    down = jnp.concatenate([rxp[:msg_rows], ym, rxm[:msg_rows]], axis=0)
+    up, down, info = lax.optimization_barrier((up, down, info))
+    ryp = neighbor(up, 0, 1)
+    rym = neighbor(down, 0, -1)
+    own, frac = call(
+        staying_kernel,
+        "staying",
+        (info,) + block_args,
+        2,
+        [((tiles, 128, 128), f32), ((3, 128, 128), f32)],
+        block_scratch,
+        7,
+        50,
+        flops=1e10,
+    )
+    region, rough, normal, solid = call(
+        assemble_kernel,
+        "assemble",
+        (static, rsxp, rsxm, rsyp, rsym),
+        0,
         [
-            ((4, 96, 128), f32),
-            ((4, 32, 128), f32),
-            ((4, 32, 128), f32),
-            ((4, 24, 128), f32),
+            ((2, 4, 36, 128), f32),
+            ((4, 16, 128), f32),
+            ((3, 4, 16, 128), f32),
+            ((4, 104, 128), f32),
         ],
-        [vmem(64, 512)],
-    )
-    sl, sb, sd = neighbor(sl, 1, 0), neighbor(sb, 0, 1), neighbor(sd, 1, 1)
+        [],
+        flops=5e8,
+    )
 
     ml, mb, md, mo, came = call(
         total_kernel,
@@ -698,21 +863,15 @@
     hl, hb, hd, ko = call(
         update_kernel,
         "update",
-        (mo, neighbor(ml, 1, 0), neighbor(mb, 0, 1), neighbor(md, 1, 1), static, sl, sb, sd),
+        (mo, neighbor(ml, 1, 0), neighbor(mb, 0, 1), neighbor(md, 1, 1), region, rough, normal),
         0,
         [
-            ((4, 64, 128), f32),
-            ((4, 64, 128), f32),
-            ((4, 40, 128), f32),
-            ((4, 128, 128), f32),
+            ((4, 48, 128), f32),
+            ((4, 48, 128), f32),
+            ((4, 32, 128), f32),
+            ((4, 88, 128), f32),
         ],
-        [
-            vmem(2, 4, 40, 128),
-            vmem(5, 4, 16, 128),
-            vmem(4, 4, 36, 128),
-            vmem(4, 16, 128),
-            vmem(3, 4, 16, 128),
-        ],
+        [vmem(2, 4, 40, 128), vmem(5, 4, 16, 128)],
     )
     move, grad, warm, gvel, gtemp = call(
         collect_kernel,
@@ -725,12 +884,13 @@
             neighbor(hl, -1, 0),
             neighbor(hb, 0, -1),
             neighbor(hd, -1, -1),
+            solid,
             frac,
             offset,
-            rxp,
-            rxm,
-            ryp,
-            rym,
+            rsxp,
+            rsxm,
+            rsyp,
+            rsym,
         ),
         3,
         [
@@ -742,7 +902,6 @@
         ],
         [
             vmem(3, 4, 136, 128),
-            vmem(4, 104, 128),
             vmem(4, 4, 40, 128),
             vmem(64, 512),
             vmem(4, 6, 40, 128),
@@ -750,6 +909,8 @@
             vmem(2, 128, 128),
             vmem(128 * 24, 128),
             vmem(4, 256, 128),
+            vmem(120 * 8, 128),
+            vmem(48 * 8, 128),
             vmem(120 * 8, 128),
             vmem(48 * 8, 128),
         ],

time: 76.3 us -> 71.7 us (0.940)
  waiting for transfers between devices: 25.6 us -> 13.9 us
  starting transfers between devices: 16.5 us -> 19.7 us
  Pallas kernels: 31.2 us -> 34.3 us
  local copies, waits for them, and re-layouts: 0.09 us -> 1.04 us
  other arithmetic: 1.9 us -> 0.95 us
    ppermute x5 -> x6, waiting for transfers between devices: 12 us -> 0.1 us  [neighbor(): lax.ppermute(value, 'gy', [(i, (i + dy) % size_y) for i in range(size_y)])]
    ppermute x3 -> x2, waiting for transfers between devices: 5.9 us -> 13.6 us  [neighbor(): return lax.ppermute(value, ('gx', 'gy'), pairs)]
    ppermute x5 -> x6, waiting for transfers between devices: 7.7 us -> 0.18 us  [neighbor(): lax.ppermute(value, 'gx', [(i, (i + dx) % size_x) for i in range(size_x)])]
    pallas_call x5 -> x8, Pallas kernels: 31.2 us -> 34.3 us  [call(): pl.pallas_call(kernel, name=name, out_shape=[jax.ShapeDtypeStruct(shape,...]
    ppermute x5 -> x6, starting transfers between devices: 10.5 us -> 13 us  [neighbor(): lax.ppermute(value, 'gy', [(i, (i + dy) % size_y) for i in range(size_y)])]
    ppermute x5 -> x6, starting transfers between devices: 4.75 us -> 6.65 us  [neighbor(): lax.ppermute(value, 'gx', [(i, (i + dx) % size_x) for i in range(size_x)])]
    ppermute x3 -> x2, starting transfers between devices: 1.24 us -> 0.08 us  [neighbor(): return lax.ppermute(value, ('gx', 'gy'), pairs)]
    unnamed x20 -> x22, local copies, waits for them, and re-layouts: 0.06 us -> 1.02 us
  transfers between devices with their start and end apart: 13 -> 14, of which waited for: 7 -> 4; matrix products, arithmetic and copies ran while one was open for 1% -> 1% of each run, Pallas kernels for 2% -> 26%
where the time goes in v1:
time: 71.7 us; the launch traced here: 70.8 us
  Pallas kernels  34.3 us (48%)
  starting transfers between devices  19.7 us (27%)
  waiting for transfers between devices  13.9 us (19%)
  local copies, waits for them, and re-layouts  1.04 us (1%)
  other arithmetic  0.95 us (1%)
  between operations  0.89 us (1%)
    pallas_call x8, Pallas kernels, call(): pl.pallas_call(kernel, name=name, out_shape=[jax.ShapeDtypeStruct(shape,...  34.3 us
    ppermute x2, waiting for transfers between devices, neighbor(): return lax.ppermute(value, ('gx', 'gy'), pairs)  13.6 us
    ppermute x6, starting transfers between devices, neighbor(): lax.ppermute(value, 'gy', [(i, (i + dy) % size_y) for i in range(size_y)])  13 us
    ppermute x6, starting transfers between devices, neighbor(): lax.ppermute(value, 'gx', [(i, (i + dx) % size_x) for i in range(size_x)])  6.65 us
  transfers between devices with their start and end apart: 14, of which 4 were waited for; matrix products, arithmetic and copies ran while one was open for 1% of the time, Pallas kernels for 26%

profile of v1, /device:TPU:0, one launch (start us, length us, event | category | flops | bytes accessed | tf_op | source)
XLA Modules:
  0.0 70.8 jit_solution(968888960321901119)
XLA Ops:
  0.6 3.8 %prepare.1 = (s32[640]{0:T(1024)}, f32[6,96,128]{2,1,0:T(8,128)}, f32[352,128]{1,0:T(8,128)}, f32[224,128]{1,0:T(8,128)}) custom-call(f32[3,64]{1,0:T(4,128)} %table.1, s32[128]{0:T(128)} %code_s.3, s32[4,4,512]{2,1,0:T(4,128)} %solid_ref.1, s32[4,4,512]{2,1,0:T(4,128)} %rough_ref.1, s32[4,4,512]{2,1,0:T(4,128)} %choice_ref.1, f32[4,4,512]{2,1,0:T(4,128)} %rim_ref.1, ...), custom_call_target="tpu_custom_call" | custom-call | flops 2000000000 | bytes 6666666 | tf_op jit(solution)/shard_map/prepare/pallas_call | solution.py:698
  4.5 2.3 %collective-permute-start.1 = (f32[224,128]{1,0:T(8,128)}, f32[224,128]{1,0:T(8,128)}, u32[]{:S(2)}, u32[]{:S(2)}) collective-permute-start(f32[224,128]{1,0:T(8,128)} %get-tuple-element.46), channel_id=1, source_target_pairs={{0,112},{16,0},{32,16},{48,32},{64,48},{80,64},{96,80},{112,96},{1... | collective-permute-start | bytes 344072 | tf_op jit(solution)/shard_map/ppermute | solution.py:679
  6.8 6.2 %outgoing.1 = (f32[432,128]{1,0:T(8,128)}, f32[144,128]{1,0:T(8,128)}, f32[144,128]{1,0:T(8,128)}, f32[432,128]{1,0:T(8,128)}) custom-call(s32[640]{0:T(1024)} %get-tuple-element.51.info_s, s32[128]{0:T(128)} %brick_s.5, f32[3,16384]{1,0:T(4,128)} %f_hbm.3, f32[3,16384]{1,0:T(4,128)} %v_hbm.3, f32[9,16384]{1,0:T(8,128)} %c_hbm.3, f32[9,16384]{1,0:T(8,128)} %k_hbm.3, ...), custom_call_target="tpu_custom_call" | custom-call | flops 6000000000 | bytes 20000000 | tf_op jit(solution)/shard_map/outgoing/pallas_call | solution.py:698
  13.0 0.0 copy-start
  13.0 0.0 copy-start.2
  13.0 0.0 copy-start.3
  13.0 0.0 copy-start.4
  13.0 0.0 copy-start.5
  13.0 0.0 copy-start.6
  13.0 0.0 copy-start.7
  13.0 0.0 copy-start.8
  13.1 0.2 collective-permute-done.left.rxp
  13.2 3.0 %collective-permute-start.3 = (f32[432,128]{1,0:T(8,128)}, f32[432,128]{1,0:T(8,128)S(1)}, u32[]{:S(2)}, u32[]{:S(2)}) collective-permute-start(f32[432,128]{1,0:T(8,128)} %get-tuple-element.49), channel_id=1, source_target_pairs={{0,112},{16,0},{32,16},{48,32},{64,48},{80,64},{96,80},{112,96},{1... | collective-permute-start | bytes 663560 | tf_op jit(solution)/shard_map/ppermute | solution.py:679
  16.2 1.0 %copy-done.9 = f32[6,96,128]{2,1,0:T(8,128)S(1)} copy-done((f32[6,96,128]{2,1,0:T(8,128)S(1)}, f32[6,96,128]{2,1,0:T(8,128)}, u32[]{:S(2)}) %copy-start.9) | copy-done | bytes 294936
  17.1 1.1 %relay.1 = (f32[448,128]{1,0:T(8,128)S(1)}, f32[288,128]{1,0:T(8,128)S(1)}) custom-call(f32[352,128]{1,0:T(8,128)} %collective-permute-done.left.rxp, f32[224,128]{1,0:T(8,128)} %collective-permute-done.1.right.rxm, f32[6,96,128]{2,1,0:T(8,128)S(1)} %copy-done.9), custom_call_target="tpu_custom_call" | custom-call | flops 500000000 | bytes 1666666 | tf_op jit(solution)/shard_map/relay/pallas_call | solution.py:698
  18.2 6.6 %collective-permute-start.10 = (f32[288,128]{1,0:T(8,128)S(1)}, f32[288,128]{1,0:T(8,128)S(1)}, u32[]{:S(2)}, u32[]{:S(2)}) collective-permute-start(f32[288,128]{1,0:T(8,128)S(1)} %get-tuple-element.64), channel_id=1, source_target_pairs={{0,15},{1,0},{2,1},{3,2},{4,3},{5,4},{6,5},{7,6},{8,7},{9,8},{10,9... | collective-permute-start | bytes 442376 | tf_op jit(solution)/shard_map/ppermute | solution.py:681
  24.8 1.0 %pad_maximum_fusion = (f32[432,128]{1,0:T(8,128)S(1)}, f32[432,128]{1,0:T(8,128)S(1)}) fusion(f32[144,128]{1,0:T(8,128)S(1)} %get-tuple-element.82, f32[144,128]{1,0:T(8,128)} %get-tuple-element.48, f32[144,128]{1,0:T(8,128)S(1)} %get-tuple-element.80, f32[144,128]{1,0:T(8,128)S(1)} %get-tuple-element.81, f32[144,128]{1,0:T(8,128)} %get-tuple-element.50, ...), kind=kLoop, calls=%fused_computation | loop fusion | flops 221184 | bytes 884736 | tf_op jit(solution)/shard_map/concatenate | solution.py:818
  25.8 0.1 collective-permute-start.4
  25.9 5.4 %collective-permute-start.5 = (f32[432,128]{1,0:T(8,128)S(1)}, f32[432,128]{1,0:T(8,128)S(1)}, u32[]{:S(2)}, u32[]{:S(2)}) collective-permute-start(f32[432,128]{1,0:T(8,128)S(1)} %get-tuple-element.54), channel_id=1, source_target_pairs={{0,15},{1,0},{2,1},{3,2},{4,3},{5,4},{6,5},{7,6},{8,7},{9,8},{10,9... | collective-permute-start | bytes 663560 | tf_op jit(solution)/shard_map/ppermute | solution.py:681
  31.3 9.2 %staying.1 = (f32[9,128,128]{2,1,0:T(8,128)S(1)}, f32[3,128,128]{2,1,0:T(8,128)S(1)}) custom-call(s32[640]{0:T(1024)S(1)} %copy-done.10, s32[128]{0:T(128)S(1)} %copy-done.2, f32[3,16384]{1,0:T(4,128)S(1)} %copy-done.5, f32[3,16384]{1,0:T(4,128)S(1)} %copy-done.6, f32[9,16384]{1,0:T(8,128)S(1)} %copy-done.3, f32[9,16384]{1,0:T(8,128)S(1)} %copy-done.4, ...), custom_call_target="tpu_custom_call" | custom-call | flops 10000000000 | bytes 33333332 | tf_op jit(solution)/shard_map/staying/pallas_call | solution.py:698
  40.6 0.7 %total.1 = (f32[4,56,128]{2,1,0:T(8,128)S(1)}, f32[4,56,128]{2,1,0:T(8,128)S(1)}, f32[4,48,128]{2,1,0:T(8,128)S(1)}, f32[4,80,128]{2,1,0:T(8,128)S(1)}, s32[1,128]{1,0:T(1,128)S(1)}) custom-call(f32[9,128,128]{2,1,0:T(8,128)S(1)} %get-tuple-element.52.own_ref, f32[432,128]{1,0:T(8,128)S(1)} %collective-permute-done.2.rxp, ...), custom_call_target="tpu_custom_call" | custom-call | flops 100000000 | bytes 333333 | tf_op jit(solution)/shard_map/total/pallas_call | solution.py:698
  41.3 0.0 collective-permute-start.6
  41.4 0.1 collective-permute-start.7
  41.4 0.1 collective-permute-start.8
  41.6 1.1 %assemble.1 = (f32[2,4,36,128]{3,2,1,0:T(8,128)S(1)}, f32[4,16,128]{2,1,0:T(8,128)S(1)}, f32[3,4,16,128]{3,2,1,0:T(8,128)S(1)}, f32[4,104,128]{2,1,0:T(8,128)S(1)}) custom-call(f32[6,96,128]{2,1,0:T(8,128)S(1)} %copy-done.9, f32[352,128]{1,0:T(8,128)} %collective-permute-done.left.rxp, f32[224,128]{1,0:T(8,128)} %collective-permute-done.1.right.rxm, ...), custom_call_target="tpu_custom_call" | custom-call | flops 500000000 | bytes 1666666 | tf_op jit(solution)/shard_map/assemble/pallas_call | solution.py:698
  42.7 8.5 %collective-permute-done.8.rd = f32[4,48,128]{2,1,0:T(8,128)S(1)} collective-permute-done((f32[4,48,128]{2,1,0:T(8,128)S(1)}, f32[4,48,128]{2,1,0:T(8,128)S(1)}, u32[]{:S(2)}, u32[]{:S(2)}) %collective-permute-start.8) | collective-permute-done | bytes 98336 | tf_op jit(solution)/shard_map/ppermute | solution.py:687
  51.2 0.3 update.1
  51.5 1.4 %collective-permute-start.11 = (f32[4,48,128]{2,1,0:T(8,128)S(1)}, f32[4,48,128]{2,1,0:T(8,128)S(1)}, u32[]{:S(2)}, u32[]{:S(2)}) collective-permute-start(f32[4,48,128]{2,1,0:T(8,128)S(1)} %get-tuple-element.69), channel_id=1, source_target_pairs={{0,112},{16,0},{32,16},{48,32},{64,48},{80,64},{96,80},{112,96},{1... | collective-permute-start | bytes 294920 | tf_op jit(solution)/shard_map/ppermute | solution.py:679
  52.9 0.8 %collective-permute-start.12 = (f32[4,48,128]{2,1,0:T(8,128)S(1)}, f32[4,48,128]{2,1,0:T(8,128)S(1)}, u32[]{:S(2)}, u32[]{:S(2)}) collective-permute-start(f32[4,48,128]{2,1,0:T(8,128)S(1)} %get-tuple-element.70), channel_id=1, source_target_pairs={{0,15},{1,0},{2,1},{3,2},{4,3},{5,4},{6,5},{7,6},{8,7},{9,8},{10,9... | collective-permute-start | bytes 294920 | tf_op jit(solution)/shard_map/ppermute | solution.py:681
  53.7 5.1 %collective-permute-done.13.rd = f32[4,32,128]{2,1,0:T(8,128)S(1)} collective-permute-done((f32[4,32,128]{2,1,0:T(8,128)S(1)}, f32[4,32,128]{2,1,0:T(8,128)S(1)}, u32[]{:S(2)}, u32[]{:S(2)}) %collective-permute-start.13) | collective-permute-done | bytes 65568 | tf_op jit(solution)/shard_map/ppermute | solution.py:687
  58.8 0.1 collective-permute-done.12.rb
  58.9 11.9 %collect.1 = (f32[3,32768]{1,0:T(4,128)}, f32[9,32768]{1,0:T(8,128)}, f32[256,128]{1,0:T(8,128)}, f32[3,4,4,512]{3,2,1,0:T(4,128)}, f32[4,4,512]{2,1,0:T(4,128)}) custom-call(s32[128]{0:T(128)S(1)} %copy-done.1, s32[128]{0:T(128)S(1)} %copy-done.2, s32[1,128]{1,0:T(1,128)S(1)} %get-tuple-element.55.came_s, f32[4,88,128]{2,1,0:T(8,128)S(1)} %get-tuple-element.68.ko, ...), custom_call_target="tpu_custom_call" | custom-call | flops 100000000 | bytes 333333 | tf_op jit(solution)/shard_map/collect/pallas_call | solution.py:698
  (29 shorter events, 0.1 us)
Async XLA Ops:
  4.5 8.6 %collective-permute-start.1 = (f32[224,128]{1,0:T(8,128)}, f32[224,128]{1,0:T(8,128)}, u32[]{:S(2)}, u32[]{:S(2)}) collective-permute-start(f32[224,128]{1,0:T(8,128)} %get-tuple-element.46), channel_id=1, source_target_pairs={{0,112},{16,0},{32,16},{48,32},{64,48},{80,64},{96,80},{112,96},{1... | collective-permute-start | bytes 344072 | tf_op jit(solution)/shard_map/ppermute | solution.py:679
  6.8 6.4 %collective-permute-start = (f32[352,128]{1,0:T(8,128)}, f32[352,128]{1,0:T(8,128)}, u32[]{:S(2)}, u32[]{:S(2)}) collective-permute-start(f32[352,128]{1,0:T(8,128)} %get-tuple-element.45), channel_id=1, source_target_pairs={{0,16},{16,32},{32,48},{48,64},{64,80},{80,96},{96,112},{112,0},{1... | collective-permute-start | bytes 540680 | tf_op jit(solution)/shard_map/ppermute | solution.py:679
  13.0 18.3 %copy-start = (s32[16384]{0:T(1024)S(1)}, s32[16384]{0:T(1024)}, u32[]{:S(2)}) copy-start(s32[16384]{0:T(1024)} %param.20) | copy-start | bytes 196612
  13.0 18.3 %copy-start.2 = (s32[128]{0:T(128)S(1)}, s32[128]{0:T(128)}, u32[]{:S(2)}) copy-start(s32[128]{0:T(128)} %brick_s.5) | copy-start | bytes 1540
  13.0 18.3 %copy-start.3 = (f32[9,16384]{1,0:T(8,128)S(1)}, f32[9,16384]{1,0:T(8,128)}, u32[]{:S(2)}) copy-start(f32[9,16384]{1,0:T(8,128)} %c_hbm.3) | copy-start | bytes 1769476
  13.0 18.3 %copy-start.4 = (f32[9,16384]{1,0:T(8,128)S(1)}, f32[9,16384]{1,0:T(8,128)}, u32[]{:S(2)}) copy-start(f32[9,16384]{1,0:T(8,128)} %k_hbm.3) | copy-start | bytes 1769476
  13.0 18.3 %copy-start.5 = (f32[3,16384]{1,0:T(4,128)S(1)}, f32[3,16384]{1,0:T(4,128)}, u32[]{:S(2)}) copy-start(f32[3,16384]{1,0:T(4,128)} %f_hbm.3) | copy-start | bytes 589828
  13.0 18.3 %copy-start.6 = (f32[3,16384]{1,0:T(4,128)S(1)}, f32[3,16384]{1,0:T(4,128)}, u32[]{:S(2)}) copy-start(f32[3,16384]{1,0:T(4,128)} %v_hbm.3) | copy-start | bytes 589828
  13.0 18.3 %copy-start.7 = (f32[16384]{0:T(1024)S(1)}, f32[16384]{0:T(1024)}, u32[]{:S(2)}) copy-start(f32[16384]{0:T(1024)} %param.18) | copy-start | bytes 196612
  13.0 18.3 %copy-start.8 = (f32[16384]{0:T(1024)S(1)}, f32[16384]{0:T(1024)}, u32[]{:S(2)}) copy-start(f32[16384]{0:T(1024)} %param.19) | copy-start | bytes 196612
  13.2 11.6 %collective-permute-start.2 = (f32[432,128]{1,0:T(8,128)}, f32[432,128]{1,0:T(8,128)S(1)}, u32[]{:S(2)}, u32[]{:S(2)}) collective-permute-start(f32[432,128]{1,0:T(8,128)} %get-tuple-element.47), channel_id=1, source_target_pairs={{0,16},{16,32},{32,48},{48,64},{64,80},{80,96},{96,112},{112,0},{1... | collective-permute-start | bytes 663560 | tf_op jit(solution)/shard_map/ppermute | solution.py:679
  13.2 11.6 %collective-permute-start.3 = (f32[432,128]{1,0:T(8,128)}, f32[432,128]{1,0:T(8,128)S(1)}, u32[]{:S(2)}, u32[]{:S(2)}) collective-permute-start(f32[432,128]{1,0:T(8,128)} %get-tuple-element.49), channel_id=1, source_target_pairs={{0,112},{16,0},{32,16},{48,32},{64,48},{80,64},{96,80},{112,96},{1... | collective-permute-start | bytes 663560 | tf_op jit(solution)/shard_map/ppermute | solution.py:679
  16.2 1.0 %copy-start.9 = (f32[6,96,128]{2,1,0:T(8,128)S(1)}, f32[6,96,128]{2,1,0:T(8,128)}, u32[]{:S(2)}) copy-start(f32[6,96,128]{2,1,0:T(8,128)} %get-tuple-element.60.own) | copy-start | bytes 884740
  17.1 14.2 %copy-start.10 = (s32[640]{0:T(1024)S(1)}, s32[640]{0:T(1024)}, u32[]{:S(2)}) copy-start(s32[640]{0:T(1024)} %get-tuple-element.51.info_s) | copy-start | bytes 7684
  18.2 23.3 %collective-permute-start.10 = (f32[288,128]{1,0:T(8,128)S(1)}, f32[288,128]{1,0:T(8,128)S(1)}, u32[]{:S(2)}, u32[]{:S(2)}) collective-permute-start(f32[288,128]{1,0:T(8,128)S(1)} %get-tuple-element.64), channel_id=1, source_target_pairs={{0,15},{1,0},{2,1},{3,2},{4,3},{5,4},{6,5},{7,6},{8,7},{9,8},{10,9... | collective-permute-start | bytes 442376 | tf_op jit(solution)/shard_map/ppermute | solution.py:681
  24.8 16.8 %collective-permute-start.9 = (f32[448,128]{1,0:T(8,128)S(1)}, f32[448,128]{1,0:T(8,128)S(1)}, u32[]{:S(2)}, u32[]{:S(2)}) collective-permute-start(f32[448,128]{1,0:T(8,128)S(1)} %get-tuple-element.63), channel_id=1, source_target_pairs={{0,1},{1,2},{2,3},{3,4},{4,5},{5,6},{6,7},{7,8},{8,9},{9,10},{10,1... | collective-permute-start | bytes 688136 | tf_op jit(solution)/shard_map/ppermute | solution.py:681
  25.8 14.8 %collective-permute-start.4 = (f32[432,128]{1,0:T(8,128)S(1)}, f32[432,128]{1,0:T(8,128)S(1)}, u32[]{:S(2)}, u32[]{:S(2)}) collective-permute-start(f32[432,128]{1,0:T(8,128)S(1)} %get-tuple-element.53), channel_id=1, source_target_pairs={{0,1},{1,2},{2,3},{3,4},{4,5},{5,6},{6,7},{7,8},{8,9},{9,10},{10,1... | collective-permute-start | bytes 663560 | tf_op jit(solution)/shard_map/ppermute | solution.py:681
  25.9 14.7 %collective-permute-start.5 = (f32[432,128]{1,0:T(8,128)S(1)}, f32[432,128]{1,0:T(8,128)S(1)}, u32[]{:S(2)}, u32[]{:S(2)}) collective-permute-start(f32[432,128]{1,0:T(8,128)S(1)} %get-tuple-element.54), channel_id=1, source_target_pairs={{0,15},{1,0},{2,1},{3,2},{4,3},{5,4},{6,5},{7,6},{8,7},{9,8},{10,9... | collective-permute-start | bytes 663560 | tf_op jit(solution)/shard_map/ppermute | solution.py:681
  40.6 18.3 %copy-start.1 = (s32[128]{0:T(128)S(1)}, s32[128]{0:T(128)}, u32[]{:S(2)}) copy-start(s32[128]{0:T(128)} %code_s.3) | copy-start | bytes 1540
  41.3 9.9 %collective-permute-start.6 = (f32[4,56,128]{2,1,0:T(8,128)S(1)}, f32[4,56,128]{2,1,0:T(8,128)S(1)}, u32[]{:S(2)}, u32[]{:S(2)}) collective-permute-start(f32[4,56,128]{2,1,0:T(8,128)S(1)} %get-tuple-element.57), channel_id=1, source_target_pairs={{0,16},{16,32},{32,48},{48,64},{64,80},{80,96},{96,112},{112,0},{1... | collective-permute-start | bytes 344072 | tf_op jit(solution)/shard_map/ppermute | solution.py:679
  41.4 9.8 %collective-permute-start.7 = (f32[4,56,128]{2,1,0:T(8,128)S(1)}, f32[4,56,128]{2,1,0:T(8,128)S(1)}, u32[]{:S(2)}, u32[]{:S(2)}) collective-permute-start(f32[4,56,128]{2,1,0:T(8,128)S(1)} %get-tuple-element.58), channel_id=1, source_target_pairs={{0,1},{1,2},{2,3},{3,4},{4,5},{5,6},{6,7},{7,8},{8,9},{9,10},{10,1... | collective-permute-start | bytes 344072 | tf_op jit(solution)/shard_map/ppermute | solution.py:681
  41.4 9.8 %collective-permute-start.8 = (f32[4,48,128]{2,1,0:T(8,128)S(1)}, f32[4,48,128]{2,1,0:T(8,128)S(1)}, u32[]{:S(2)}, u32[]{:S(2)}) collective-permute-start(f32[4,48,128]{2,1,0:T(8,128)S(1)} %get-tuple-element.59), channel_id=1, source_target_pairs={{0,17},{1,18},{2,19},{3,20},{4,21},{5,22},{6,23},{7,24},{8,25},{9,... | collective-permute-start | bytes 294920 | tf_op jit(solution)/shard_map/ppermute | solution.py:687
  51.5 7.3 %collective-permute-start.11 = (f32[4,48,128]{2,1,0:T(8,128)S(1)}, f32[4,48,128]{2,1,0:T(8,128)S(1)}, u32[]{:S(2)}, u32[]{:S(2)}) collective-permute-start(f32[4,48,128]{2,1,0:T(8,128)S(1)} %get-tuple-element.69), channel_id=1, source_target_pairs={{0,112},{16,0},{32,16},{48,32},{64,48},{80,64},{96,80},{112,96},{1... | collective-permute-start | bytes 294920 | tf_op jit(solution)/shard_map/ppermute | solution.py:679
  52.9 6.0 %collective-permute-start.12 = (f32[4,48,128]{2,1,0:T(8,128)S(1)}, f32[4,48,128]{2,1,0:T(8,128)S(1)}, u32[]{:S(2)}, u32[]{:S(2)}) collective-permute-start(f32[4,48,128]{2,1,0:T(8,128)S(1)} %get-tuple-element.70), channel_id=1, source_target_pairs={{0,15},{1,0},{2,1},{3,2},{4,3},{5,4},{6,5},{7,6},{8,7},{9,8},{10,9... | collective-permute-start | bytes 294920 | tf_op jit(solution)/shard_map/ppermute | solution.py:681
  53.7 5.1 %collective-permute-start.13 = (f32[4,32,128]{2,1,0:T(8,128)S(1)}, f32[4,32,128]{2,1,0:T(8,128)S(1)}, u32[]{:S(2)}, u32[]{:S(2)}) collective-permute-start(f32[4,32,128]{2,1,0:T(8,128)S(1)} %get-tuple-element.71), channel_id=1, source_target_pairs={{0,127},{1,112},{2,113},{3,114},{4,115},{5,116},{6,117},{7,118},{8... | collective-permute-start | bytes 196616 | tf_op jit(solution)/shard_map/ppermute | solution.py:687

commit v2 on v1

--- a/solution.py
+++ b/solution.py
@@ -53,20 +53,13 @@
 
 
 def deposit_blocks(
-    base, count, info_s, brick_s, target_of, hbm_refs, vmem_refs, sems, first, second, acc, after
+    base, count, info_s, target_of, refs, first, second, acc, after
 ):
-    copies = [
-        pltpu.make_async_copy(a, b, sems.at[n]) for n, (a, b) in enumerate(zip(hbm_refs, vmem_refs))
-    ]
-    for copy in copies:
-        copy.start()
-    f_ref, v_ref, c_ref, k_ref, m_ref, t_ref, o_ref = vmem_refs
-    clear_rows(acc, 128 * 32)
+    f_ref, v_ref, c_ref, k_ref, m_ref, t_ref, o_ref = refs
+    clear_rows(acc, 128 * 40)
     for _, sa, sb in (first, second):
         sa[...] = jnp.zeros(sa.shape, f32)
         sb[...] = jnp.zeros(sb.shape, f32)
-    for copy in copies:
-        copy.wait()
     row_no = lax.broadcasted_iota(jnp.int32, (32, 1), 0)
 
     def build(g, raw, sa, sb):
@@ -129,7 +122,7 @@
             sums.append(both[:, :40] + both[:, 40:])
         for j in range(8):
             target, mark = target_of(g * 8 + j, blocks[j])
-            spot = pl.ds(pl.multiple_of(target * 32, 32), 32)
+            spot = pl.ds(pl.multiple_of(target * 40, 8), 32)
             acc[spot, 0:40] = acc[spot, 0:40] + (sums[j] + jnp.where(row_no == 30, mark, 0.0))
             after(j, blocks[j], raw)
 
@@ -148,7 +141,7 @@
     lane = lax.broadcasted_iota(jnp.int32, (8, 128), 1)
     total = [jnp.zeros((8, 128), f32) for _ in range(tiles)]
     for i in range(pieces):
-        piece = acc[pl.ds(chunk * 256 + i, 8, stride=32), :]
+        piece = acc[pl.ds(chunk * 320 + i, 8, stride=40), :]
         if i == 30:
             piece = jnp.where(lane < 36, piece, 0.0)
         tile, at = divmod(i * 36, 128)
@@ -163,18 +156,17 @@
 
 
 def outgoing_kernel(
-    info_s, brick_s, f_hbm, v_hbm, c_hbm, k_hbm, m_hbm, t_hbm, o_hbm,
+    info_s, f_ref, v_ref, c_ref, k_ref, m_ref, t_ref, o_ref,
     xm_ref, ym_ref, yp_ref, xp_ref,
-    f_ref, v_ref, c_ref, k_ref, m_ref, t_ref, o_ref, sems, raw, sa, sb, raw2, sa2, sb2, acc,
+    raw, sa, sb, raw2, sa2, sb2, acc,
 ):
     def target_of(entry, block):
-        return info_s[160 + entry], (brick_s[block] + 1).astype(f32)
+        return info_s[160 + entry], (info_s[640 + block] + 1).astype(f32)
 
     deposit_blocks(
-        0, info_s[544], info_s, brick_s, target_of,
-        (f_hbm, v_hbm, c_hbm, k_hbm, m_hbm, t_hbm, o_hbm),
+        0, info_s[544], info_s, target_of,
         (f_ref, v_ref, c_ref, k_ref, m_ref, t_ref, o_ref),
-        sems, (raw, sa, sb), (raw2, sa2, sb2), acc, lambda j, block, raw: None,
+        (raw, sa, sb), (raw2, sa2, sb2), acc, lambda j, block, raw: None,
     )
     for first, count, ref in ((0, 3, xm_ref), (3, 1, ym_ref), (4, 1, yp_ref), (5, 3, xp_ref)):
         for n in range(count):
@@ -194,24 +186,23 @@
 
 
 def staying_kernel(
-    info_s, brick_s, f_hbm, v_hbm, c_hbm, k_hbm, m_hbm, t_hbm, o_hbm,
+    info_s, f_ref, v_ref, c_ref, k_ref, m_ref, t_ref, o_ref,
     own_ref, frac_ref,
-    f_ref, v_ref, c_ref, k_ref, m_ref, t_ref, o_ref, sems, raw, sa, sb, raw2, sa2, sb2, acc,
+    raw, sa, sb, raw2, sa2, sb2, acc,
 ):
     frac_ref[...] = jnp.zeros(frac_ref.shape, f32)
 
     def target_of(entry, block):
-        return jnp.where(entry < info_s[545], brick_s[block], 128), jnp.float32(0.0)
+        return jnp.where(entry < info_s[545], info_s[640 + block], 128), jnp.float32(0.0)
 
     def after(j, block, raw):
         for d in range(3):
             frac_ref[d, pl.ds(block, 1), :] = raw[j * 40 + d : j * 40 + d + 1, :]
 
     deposit_blocks(
-        320, info_s[545], info_s, brick_s, target_of,
-        (f_hbm, v_hbm, c_hbm, k_hbm, m_hbm, t_hbm, o_hbm),
+        320, info_s[545], info_s, target_of,
         (f_ref, v_ref, c_ref, k_ref, m_ref, t_ref, o_ref),
-        sems, (raw, sa, sb), (raw2, sa2, sb2), acc, after,
+        (raw, sa, sb), (raw2, sa2, sb2), acc, after,
     )
 
     def pack_own(chunk, carry):
@@ -290,10 +281,24 @@
 
 
 def prepare_kernel(
-    table, code_s, solid_ref, rough_ref, choice_ref, rim_ref, f_ref, o_ref,
-    info, own, xp, xm, cells, fo, cnt,
+    table_hbm, code_hbm, solid_hbm, rough_hbm, choice_hbm, rim_hbm,
+    brick_hbm, f_hbm, v_hbm, c_hbm, k_hbm, m_hbm, t_hbm, o_hbm,
+    info, own, xp, xm, f_ref, v_ref, c_ref, k_ref, m_ref, t_ref, o_ref,
+    table, code_s, brick_s, solid_ref, rough_ref, choice_ref, rim_ref, sems,
+    cells, fo, cnt,
 ):
+    pairs = (
+        (code_hbm, code_s), (f_hbm, f_ref), (o_hbm, o_ref), (table_hbm, table),
+        (solid_hbm, solid_ref), (rough_hbm, rough_ref), (choice_hbm, choice_ref), (rim_hbm, rim_ref),
+        (brick_hbm, brick_s), (v_hbm, v_ref), (c_hbm, c_ref), (k_hbm, k_ref), (m_hbm, m_ref),
+        (t_hbm, t_ref),
+    )
+    copies = [pltpu.make_async_copy(a, b, sems.at[n]) for n, (a, b) in enumerate(pairs)]
+    for copy in copies:
+        copy.start()
     fo[...] = jnp.zeros(fo.shape, f32)
+    for copy in copies[:9]:
+        copy.wait()
     for n in range(10):
         cnt[n] = 0
 
@@ -306,6 +311,7 @@
         gone = cnt[9]
         slot = way * 16 + rank
         info[jnp.where(leaves, gone, 320 + b - gone)] = b
+        info[640 + b] = brick_s[b]
         info[jnp.where(leaves, 160 + gone, 639)] = slot
         cnt[9] = gone + jnp.where(leaves, 1, 0)
         at = pl.multiple_of(jnp.where(leaves, slot, 128) * 4, 4)
@@ -355,6 +361,8 @@
             row = 32 + field * 16
             xp[at + 24 + field * 4 : at + 28 + field * 4, :] = own[kz, row + 12 : row + 16, :]
         xm[192 + kz * 8 : 200 + kz * 8, :] = own[kz, 0:8, :]
+    for copy in copies[9:]:
+        copy.wait()
     xm[0:192, :] = fo[0:192, :]
     for way in range(2):
         own[4 + way, 0:64, :] = fo[192 + way * 64 : 256 + way * 64, :]
@@ -707,7 +715,11 @@
         ),
         scratch_shapes=scratch,
         compiler_params=pltpu.CompilerParams(vmem_limit_bytes=limit * mib),
-    )(*inputs)
+    )(
+        *inputs[:scalars],
+        *[pltpu.with_memory_space_constraint(x, pltpu.HBM) for x in inputs[scalars : scalars + left_there]],
+        *inputs[scalars + left_there :],
+    )
 
 
 def vmem(*shape):
@@ -731,7 +743,7 @@
     rim_thermal_level,
 ):
     offset = anchor_voxel_shift.reshape(128, 128)
-    info, static, sxp, sxm = call(
+    info, static, sxp, sxm, *block_args = call(
         prepare_kernel,
         "prepare",
         (
@@ -741,55 +753,63 @@
             rough_surface_flag,
             voxel_facing_choice,
             rim_thermal_level,
+            group_resting_volume,
             subvoxel_location_share,
+            point_motion_vector,
+            linear_gradient_matrix,
+            kirchhoff_tension_matrix,
+            point_inertia_amounts.reshape(128, 128),
+            point_thermal_state.reshape(128, 128),
             offset,
         ),
-        2,
+        0,
         [
-            ((640,), jnp.int32),
+            ((768,), jnp.int32),
             ((6, 96, 128), f32),
             ((352, 128), f32),
             ((224, 128), f32),
+            ((3, 16384), f32),
+            ((3, 16384), f32),
+            ((9, 16384), f32),
+            ((9, 16384), f32),
+            ((128, 128), f32),
+            ((128, 128), f32),
+            ((128, 128), jnp.int32),
         ],
-        [vmem(64, 512), vmem(520, 128), pltpu.SMEM((16,), jnp.int32)],
-        limit=64,
+        [
+            pltpu.SMEM((3, 64), f32),
+            pltpu.SMEM((128,), jnp.int32),
+            pltpu.SMEM((128,), jnp.int32),
+            pltpu.VMEM((4, 4, 512), jnp.int32),
+            pltpu.VMEM((4, 4, 512), jnp.int32),
+            pltpu.VMEM((4, 4, 512), jnp.int32),
+            vmem(4, 4, 512),
+            pltpu.SemaphoreType.DMA((14,)),
+            vmem(64, 512),
+            vmem(520, 128),
+            pltpu.SMEM((16,), jnp.int32),
+        ],
+        14,
+        24,
         flops=2e9,
         listed=1,
     )
     rsxp = neighbor(sxp, 1, 0)
     rsxm = neighbor(sxm, -1, 0)
-    block_args = (
-        group_resting_volume,
-        subvoxel_location_share,
-        point_motion_vector,
-        linear_gradient_matrix,
-        kirchhoff_tension_matrix,
-        point_inertia_amounts.reshape(128, 128),
-        point_thermal_state.reshape(128, 128),
-        offset,
-    )
     block_scratch = [
-        vmem(3, 16384),
-        vmem(3, 16384),
-        vmem(9, 16384),
-        vmem(9, 16384),
-        vmem(128, 128),
-        vmem(128, 128),
-        pltpu.VMEM((128, 128), jnp.int32),
-        pltpu.SemaphoreType.DMA((7,)),
         vmem(320, 128),
         vmem(96 * 8, 128),
         vmem(120 * 8, 128),
         vmem(320, 128),
         vmem(96 * 8, 128),
         vmem(120 * 8, 128),
-        vmem(129 * 32, 128),
+        vmem(130 * 40, 128),
     ]
     xm, ym, yp, xp = call(
         outgoing_kernel,
         "outgoing",
-        (info,) + block_args,
-        2,
+        (info, *block_args),
+        1,
         [
             ((3 * msg_rows, 128), f32),
             ((msg_rows, 128), f32),
@@ -797,8 +817,7 @@
             ((3 * msg_rows, 128), f32),
         ],
         block_scratch,
-        7,
-        64,
+        limit=24,
         flops=6e9,
     )
     xm, xp, rsxp, rsxm = lax.optimization_barrier((xm, xp, rsxp, rsxm))
@@ -823,12 +842,11 @@
     own, frac = call(
         staying_kernel,
         "staying",
-        (info,) + block_args,
-        2,
+        (info, *block_args),
+        1,
         [((tiles, 128, 128), f32), ((3, 128, 128), f32)],
         block_scratch,
-        7,
-        50,
+        limit=24,
         flops=1e10,
     )
     region, rough, normal, solid = call(

time: 71.7 us -> 67 us (0.934)
  Pallas kernels: 34.3 us -> 28.1 us
  waiting for transfers between devices: 13.9 us -> 17.7 us
  local copies, waits for them, and re-layouts: 1.04 us -> 0.04 us
  other arithmetic: 0.95 us -> 0.03 us
    pallas_call x8, Pallas kernels: 34.3 us -> 28.1 us  [call(): pl.pallas_call(kernel, name=name, out_shape=[jax.ShapeDtypeStruct(shape,...]
    ppermute x6, waiting for transfers between devices: 0.18 us -> 2.66 us  [neighbor(): lax.ppermute(value, 'gx', [(i, (i + dx) % size_x) for i in range(size_x)])]
    ppermute x6, starting transfers between devices: 6.65 us -> 7.74 us  [neighbor(): lax.ppermute(value, 'gx', [(i, (i + dx) % size_x) for i in range(size_x)])]
    unnamed x22 -> x6, local copies, waits for them, and re-layouts: 1.02 us -> 0.02 us
    concatenate x1, other arithmetic: 0.95 us -> 0.03 us  [on_device(): up = jnp.concatenate([rxp[2 * msg_rows:], yp, rxm[2 * msg_rows:]], axis=0)]
    ppermute x6, starting transfers between devices: 13 us -> 12.1 us  [neighbor(): lax.ppermute(value, 'gy', [(i, (i + dy) % size_y) for i in range(size_y)])]
    ppermute x6, waiting for transfers between devices: 0.1 us -> 0.83 us  [neighbor(): lax.ppermute(value, 'gy', [(i, (i + dy) % size_y) for i in range(size_y)])]
  transfers between devices with their start and end apart: 14 -> 14, of which waited for: 4 -> 4; matrix products, arithmetic and copies ran while one was open for 1% -> 0% of each run, Pallas kernels for 26% -> 19%
where the time goes in v2:
time: 67 us; the launch traced here: 66.6 us
  Pallas kernels  28.1 us (42%)
  starting transfers between devices  19.9 us (30%)
  waiting for transfers between devices  17.7 us (26%)
  between operations  0.81 us (1%)
    pallas_call x8, Pallas kernels, call(): pl.pallas_call(kernel, name=name, out_shape=[jax.ShapeDtypeStruct(shape,...  28.1 us
    ppermute x2, waiting for transfers between devices, neighbor(): return lax.ppermute(value, ('gx', 'gy'), pairs)  14.2 us
    ppermute x6, starting transfers between devices, neighbor(): lax.ppermute(value, 'gy', [(i, (i + dy) % size_y) for i in range(size_y)])  12.1 us
    ppermute x6, starting transfers between devices, neighbor(): lax.ppermute(value, 'gx', [(i, (i + dx) % size_x) for i in range(size_x)])  7.74 us
    ppermute x6, waiting for transfers between devices, neighbor(): lax.ppermute(value, 'gx', [(i, (i + dx) % size_x) for i in range(size_x)])  2.66 us
  transfers between devices with their start and end apart: 14, of which 4 were waited for; matrix products, arithmetic and copies ran while one was open for 0% of the time, Pallas kernels for 19%

profile of v2, /device:TPU:0, one launch (start us, length us, event | category | flops | bytes accessed | tf_op | source)
XLA Modules:
  0.0 66.6 jit_solution(9415081711760826735)
XLA Ops:
  0.6 3.9 %prepare.1 = (s32[768]{0:T(1024)S(1)}, f32[6,96,128]{2,1,0:T(8,128)S(1)}, f32[352,128]{1,0:T(8,128)S(1)}, f32[224,128]{1,0:T(8,128)S(1)}, f32[3,16384]{1,0:T(4,1...) custom-call(f32[3,64]{1,0:T(4,128)} %table_hbm.1, ...), custom_call_target="tpu_custom_call" | custom-call | flops 2000000000 | bytes 6666666 | tf_op jit(solution)/shard_map/prepare/pallas_call | solution.py:706
  4.6 2.3 %collective-permute-start.1 = (f32[224,128]{1,0:T(8,128)S(1)}, f32[224,128]{1,0:T(8,128)S(1)}, u32[]{:S(2)}, u32[]{:S(2)}) collective-permute-start(f32[224,128]{1,0:T(8,128)S(1)} %get-tuple-element.60), channel_id=1, source_target_pairs={{0,112},{16,0},{32,16},{48,32},{64,48},{80,64},{96,80},{112,96},{1... | collective-permute-start | bytes 344072 | tf_op jit(solution)/shard_map/ppermute | solution.py:687
  6.8 0.0 collective-permute-start
  6.8 3.5 %outgoing.1 = (f32[432,128]{1,0:T(8,128)S(1)}, f32[144,128]{1,0:T(8,128)S(1)}, f32[144,128]{1,0:T(8,128)S(1)}, f32[432,128]{1,0:T(8,128)S(1)}) custom-call(s32[768]{0:T(1024)S(1)} %get-tuple-element.65.info_s, f32[3,16384]{1,0:T(4,128)S(1)} %get-tuple-element.50.f_ref, f32[3,16384]{1,0:T(4,128)S(1)} %get-tuple-element.51.v_ref, ...), custom_call_target="tpu_custom_call" | custom-call | flops 6000000000 | bytes 20000000 | tf_op jit(solution)/shard_map/outgoing/pallas_call | solution.py:706
  10.3 0.0 collective-permute-done.1.right.rxm
  10.3 2.6 %collective-permute-done.left.rxp = f32[352,128]{1,0:T(8,128)S(1)} collective-permute-done((f32[352,128]{1,0:T(8,128)S(1)}, f32[352,128]{1,0:T(8,128)S(1)}, u32[]{:S(2)}, u32[]{:S(2)}) %collective-permute-start) | collective-permute-done | bytes 180256 | tf_op jit(solution)/shard_map/ppermute | solution.py:687
  13.0 0.0 collective-permute-start.2
  13.0 3.0 %collective-permute-start.3 = (f32[432,128]{1,0:T(8,128)S(1)}, f32[432,128]{1,0:T(8,128)S(1)}, u32[]{:S(2)}, u32[]{:S(2)}) collective-permute-start(f32[432,128]{1,0:T(8,128)S(1)} %get-tuple-element.63), channel_id=1, source_target_pairs={{0,112},{16,0},{32,16},{48,32},{64,48},{80,64},{96,80},{112,96},{1... | collective-permute-start | bytes 663560 | tf_op jit(solution)/shard_map/ppermute | solution.py:687
  15.9 0.1 relay.1
  16.0 6.6 %collective-permute-start.10 = (f32[288,128]{1,0:T(8,128)S(1)}, f32[288,128]{1,0:T(8,128)S(1)}, u32[]{:S(2)}, u32[]{:S(2)}) collective-permute-start(f32[288,128]{1,0:T(8,128)S(1)} %get-tuple-element.78), channel_id=1, source_target_pairs={{0,15},{1,0},{2,1},{3,2},{4,3},{5,4},{6,5},{7,6},{8,7},{9,8},{10,9... | collective-permute-start | bytes 442376 | tf_op jit(solution)/shard_map/ppermute | solution.py:689
  22.6 0.0 collective-permute-start.9
  22.6 0.0 collective-permute-done.2.rxp
  22.7 0.1 collective-permute-start.4
  22.7 5.4 %collective-permute-start.5 = (f32[432,128]{1,0:T(8,128)S(1)}, f32[432,128]{1,0:T(8,128)S(1)}, u32[]{:S(2)}, u32[]{:S(2)}) collective-permute-start(f32[432,128]{1,0:T(8,128)S(1)} %get-tuple-element.68), channel_id=1, source_target_pairs={{0,15},{1,0},{2,1},{3,2},{4,3},{5,4},{6,5},{7,6},{8,7},{9,8},{10,9... | collective-permute-start | bytes 663560 | tf_op jit(solution)/shard_map/ppermute | solution.py:689
  28.2 8.2 %staying.1 = (f32[9,128,128]{2,1,0:T(8,128)S(1)}, f32[3,128,128]{2,1,0:T(8,128)S(1)}) custom-call(s32[768]{0:T(1024)S(1)} %get-tuple-element.65.info_s, f32[3,16384]{1,0:T(4,128)S(1)} %get-tuple-element.50.f_ref, f32[3,16384]{1,0:T(4,128)S(1)} %get-tuple-element.51.v_ref, f32[9,16384]{1,0:T(8,128)S(1)} %get-tuple-element.52.c_ref, ...), custom_call_target="tpu_custom_call" | custom-call | flops 10000000000 | bytes 33333332 | tf_op jit(solution)/shard_map/staying/pallas_call | solution.py:706
  36.3 0.0 copy-start
  36.3 0.0 copy-start.1
  36.3 0.0 copy-start.2
  36.4 0.7 %total.1 = (f32[4,56,128]{2,1,0:T(8,128)S(1)}, f32[4,56,128]{2,1,0:T(8,128)S(1)}, f32[4,48,128]{2,1,0:T(8,128)S(1)}, f32[4,80,128]{2,1,0:T(8,128)S(1)}, s32[1,128]{1,0:T(1,128)S(1)}) custom-call(f32[9,128,128]{2,1,0:T(8,128)S(1)} %get-tuple-element.66.own_ref, f32[432,128]{1,0:T(8,128)S(1)} %collective-permute-done.2.rxp, ...), custom_call_target="tpu_custom_call" | custom-call | flops 100000000 | bytes 333333 | tf_op jit(solution)/shard_map/total/pallas_call | solution.py:706
  37.1 0.0 collective-permute-start.6
  37.1 0.1 collective-permute-start.7
  37.2 0.1 collective-permute-start.8
  37.3 0.0 collective-permute-done.10.above.rym
  37.3 0.0 collective-permute-done.9.below.ryp
  37.3 0.1 assemble.1
  37.4 9.5 %collective-permute-done.8.rd = f32[4,48,128]{2,1,0:T(8,128)S(1)} collective-permute-done((f32[4,48,128]{2,1,0:T(8,128)S(1)}, f32[4,48,128]{2,1,0:T(8,128)S(1)}, u32[]{:S(2)}, u32[]{:S(2)}) %collective-permute-start.8) | collective-permute-done | bytes 98336 | tf_op jit(solution)/shard_map/ppermute | solution.py:695
  47.0 0.0 collective-permute-done.6.rl
  47.0 0.3 update.1
  47.3 2.5 %collective-permute-start.11 = (f32[4,48,128]{2,1,0:T(8,128)S(1)}, f32[4,48,128]{2,1,0:T(8,128)S(1)}, u32[]{:S(2)}, u32[]{:S(2)}) collective-permute-start(f32[4,48,128]{2,1,0:T(8,128)S(1)} %get-tuple-element.83), channel_id=1, source_target_pairs={{0,112},{16,0},{32,16},{48,32},{64,48},{80,64},{96,80},{112,96},{1... | collective-permute-start | bytes 294920 | tf_op jit(solution)/shard_map/ppermute | solution.py:687
  49.7 4.7 %collective-permute-done.13.rd = f32[4,32,128]{2,1,0:T(8,128)S(1)} collective-permute-done((f32[4,32,128]{2,1,0:T(8,128)S(1)}, f32[4,32,128]{2,1,0:T(8,128)S(1)}, u32[]{:S(2)}, u32[]{:S(2)}) %collective-permute-start.13) | collective-permute-done | bytes 65568 | tf_op jit(solution)/shard_map/ppermute | solution.py:695
  54.4 0.8 %collective-permute-done.12.rb = f32[4,48,128]{2,1,0:T(8,128)S(1)} collective-permute-done((f32[4,48,128]{2,1,0:T(8,128)S(1)}, f32[4,48,128]{2,1,0:T(8,128)S(1)}, u32[]{:S(2)}, u32[]{:S(2)}) %collective-permute-start.12) | collective-permute-done | bytes 98336 | tf_op jit(solution)/shard_map/ppermute | solution.py:689
  55.2 11.4 %collect.1 = (f32[3,32768]{1,0:T(4,128)}, f32[9,32768]{1,0:T(8,128)}, f32[256,128]{1,0:T(8,128)}, f32[3,4,4,512]{3,2,1,0:T(4,128)}, f32[4,4,512]{2,1,0:T(4,128)}) custom-call(s32[128]{0:T(128)S(1)} %copy-done.1, s32[128]{0:T(128)S(1)} %copy-done.2, s32[1,128]{1,0:T(1,128)S(1)} %get-tuple-element.69.came_s, f32[4,88,128]{2,1,0:T(8,128)S(1)} %get-tuple-element.82.ko, ...), custom_call_target="tpu_custom_call" | custom-call | flops 100000000 | bytes 333333 | tf_op jit(solution)/shard_map/collect/pallas_call | solution.py:706
  (13 shorter events, 0.1 us)
Async XLA Ops:
  4.6 5.8 %collective-permute-start.1 = (f32[224,128]{1,0:T(8,128)S(1)}, f32[224,128]{1,0:T(8,128)S(1)}, u32[]{:S(2)}, u32[]{:S(2)}) collective-permute-start(f32[224,128]{1,0:T(8,128)S(1)} %get-tuple-element.60), channel_id=1, source_target_pairs={{0,112},{16,0},{32,16},{48,32},{64,48},{80,64},{96,80},{112,96},{1... | collective-permute-start | bytes 344072 | tf_op jit(solution)/shard_map/ppermute | solution.py:687
  6.8 6.1 %collective-permute-start = (f32[352,128]{1,0:T(8,128)S(1)}, f32[352,128]{1,0:T(8,128)S(1)}, u32[]{:S(2)}, u32[]{:S(2)}) collective-permute-start(f32[352,128]{1,0:T(8,128)S(1)} %get-tuple-element.59), channel_id=1, source_target_pairs={{0,16},{16,32},{32,48},{48,64},{64,80},{80,96},{96,112},{112,0},{1... | collective-permute-start | bytes 540680 | tf_op jit(solution)/shard_map/ppermute | solution.py:687
  13.0 9.6 %collective-permute-start.2 = (f32[432,128]{1,0:T(8,128)S(1)}, f32[432,128]{1,0:T(8,128)S(1)}, u32[]{:S(2)}, u32[]{:S(2)}) collective-permute-start(f32[432,128]{1,0:T(8,128)S(1)} %get-tuple-element.61), channel_id=1, source_target_pairs={{0,16},{16,32},{32,48},{48,64},{64,80},{80,96},{96,112},{112,0},{1... | collective-permute-start | bytes 663560 | tf_op jit(solution)/shard_map/ppermute | solution.py:687
  13.0 9.6 %collective-permute-start.3 = (f32[432,128]{1,0:T(8,128)S(1)}, f32[432,128]{1,0:T(8,128)S(1)}, u32[]{:S(2)}, u32[]{:S(2)}) collective-permute-start(f32[432,128]{1,0:T(8,128)S(1)} %get-tuple-element.63), channel_id=1, source_target_pairs={{0,112},{16,0},{32,16},{48,32},{64,48},{80,64},{96,80},{112,96},{1... | collective-permute-start | bytes 663560 | tf_op jit(solution)/shard_map/ppermute | solution.py:687
  16.0 21.3 %collective-permute-start.10 = (f32[288,128]{1,0:T(8,128)S(1)}, f32[288,128]{1,0:T(8,128)S(1)}, u32[]{:S(2)}, u32[]{:S(2)}) collective-permute-start(f32[288,128]{1,0:T(8,128)S(1)} %get-tuple-element.78), channel_id=1, source_target_pairs={{0,15},{1,0},{2,1},{3,2},{4,3},{5,4},{6,5},{7,6},{8,7},{9,8},{10,9... | collective-permute-start | bytes 442376 | tf_op jit(solution)/shard_map/ppermute | solution.py:689
  22.6 14.7 %collective-permute-start.9 = (f32[448,128]{1,0:T(8,128)S(1)}, f32[448,128]{1,0:T(8,128)S(1)}, u32[]{:S(2)}, u32[]{:S(2)}) collective-permute-start(f32[448,128]{1,0:T(8,128)S(1)} %get-tuple-element.77), channel_id=1, source_target_pairs={{0,1},{1,2},{2,3},{3,4},{4,5},{5,6},{6,7},{7,8},{8,9},{9,10},{10,1... | collective-permute-start | bytes 688136 | tf_op jit(solution)/shard_map/ppermute | solution.py:689
  22.7 13.7 %collective-permute-start.4 = (f32[432,128]{1,0:T(8,128)S(1)}, f32[432,128]{1,0:T(8,128)S(1)}, u32[]{:S(2)}, u32[]{:S(2)}) collective-permute-start(f32[432,128]{1,0:T(8,128)S(1)} %get-tuple-element.67), channel_id=1, source_target_pairs={{0,1},{1,2},{2,3},{3,4},{4,5},{5,6},{6,7},{7,8},{8,9},{9,10},{10,1... | collective-permute-start | bytes 663560 | tf_op jit(solution)/shard_map/ppermute | solution.py:689
  22.7 13.6 %collective-permute-start.5 = (f32[432,128]{1,0:T(8,128)S(1)}, f32[432,128]{1,0:T(8,128)S(1)}, u32[]{:S(2)}, u32[]{:S(2)}) collective-permute-start(f32[432,128]{1,0:T(8,128)S(1)} %get-tuple-element.68), channel_id=1, source_target_pairs={{0,15},{1,0},{2,1},{3,2},{4,3},{5,4},{6,5},{7,6},{8,7},{9,8},{10,9... | collective-permute-start | bytes 663560 | tf_op jit(solution)/shard_map/ppermute | solution.py:689
  36.3 18.9 %copy-start = (s32[16384]{0:T(1024)S(1)}, s32[16384]{0:T(1024)}, u32[]{:S(2)}) copy-start(s32[16384]{0:T(1024)} %param.20) | copy-start | bytes 196612
  36.3 18.9 %copy-start.1 = (s32[128]{0:T(128)S(1)}, s32[128]{0:T(128)}, u32[]{:S(2)}) copy-start(s32[128]{0:T(128)} %code_s.1) | copy-start | bytes 1540
  36.3 18.9 %copy-start.2 = (s32[128]{0:T(128)S(1)}, s32[128]{0:T(128)}, u32[]{:S(2)}) copy-start(s32[128]{0:T(128)} %brick_s.1) | copy-start | bytes 1540
  37.1 9.9 %collective-permute-start.6 = (f32[4,56,128]{2,1,0:T(8,128)S(1)}, f32[4,56,128]{2,1,0:T(8,128)S(1)}, u32[]{:S(2)}, u32[]{:S(2)}) collective-permute-start(f32[4,56,128]{2,1,0:T(8,128)S(1)} %get-tuple-element.71), channel_id=1, source_target_pairs={{0,16},{16,32},{32,48},{48,64},{64,80},{80,96},{96,112},{112,0},{1... | collective-permute-start | bytes 344072 | tf_op jit(solution)/shard_map/ppermute | solution.py:687
  37.1 9.8 %collective-permute-start.7 = (f32[4,56,128]{2,1,0:T(8,128)S(1)}, f32[4,56,128]{2,1,0:T(8,128)S(1)}, u32[]{:S(2)}, u32[]{:S(2)}) collective-permute-start(f32[4,56,128]{2,1,0:T(8,128)S(1)} %get-tuple-element.72), channel_id=1, source_target_pairs={{0,1},{1,2},{2,3},{3,4},{4,5},{5,6},{6,7},{7,8},{8,9},{9,10},{10,1... | collective-permute-start | bytes 344072 | tf_op jit(solution)/shard_map/ppermute | solution.py:689
  37.2 9.8 %collective-permute-start.8 = (f32[4,48,128]{2,1,0:T(8,128)S(1)}, f32[4,48,128]{2,1,0:T(8,128)S(1)}, u32[]{:S(2)}, u32[]{:S(2)}) collective-permute-start(f32[4,48,128]{2,1,0:T(8,128)S(1)} %get-tuple-element.73), channel_id=1, source_target_pairs={{0,17},{1,18},{2,19},{3,20},{4,21},{5,22},{6,23},{7,24},{8,25},{9,... | collective-permute-start | bytes 294920 | tf_op jit(solution)/shard_map/ppermute | solution.py:695
  47.3 7.1 %collective-permute-start.11 = (f32[4,48,128]{2,1,0:T(8,128)S(1)}, f32[4,48,128]{2,1,0:T(8,128)S(1)}, u32[]{:S(2)}, u32[]{:S(2)}) collective-permute-start(f32[4,48,128]{2,1,0:T(8,128)S(1)} %get-tuple-element.83), channel_id=1, source_target_pairs={{0,112},{16,0},{32,16},{48,32},{64,48},{80,64},{96,80},{112,96},{1... | collective-permute-start | bytes 294920 | tf_op jit(solution)/shard_map/ppermute | solution.py:687
  49.7 5.5 %collective-permute-start.12 = (f32[4,48,128]{2,1,0:T(8,128)S(1)}, f32[4,48,128]{2,1,0:T(8,128)S(1)}, u32[]{:S(2)}, u32[]{:S(2)}) collective-permute-start(f32[4,48,128]{2,1,0:T(8,128)S(1)} %get-tuple-element.84), channel_id=1, source_target_pairs={{0,15},{1,0},{2,1},{3,2},{4,3},{5,4},{6,5},{7,6},{8,7},{9,8},{10,9... | collective-permute-start | bytes 294920 | tf_op jit(solution)/shard_map/ppermute | solution.py:689
  49.7 4.7 %collective-permute-start.13 = (f32[4,32,128]{2,1,0:T(8,128)S(1)}, f32[4,32,128]{2,1,0:T(8,128)S(1)}, u32[]{:S(2)}, u32[]{:S(2)}) collective-permute-start(f32[4,32,128]{2,1,0:T(8,128)S(1)} %get-tuple-element.85), channel_id=1, source_target_pairs={{0,127},{1,112},{2,113},{3,114},{4,115},{5,116},{6,117},{7,118},{8... | collective-permute-start | bytes 196616 | tf_op jit(solution)/shard_map/ppermute | solution.py:695

commit v3 on v2

--- a/solution.py
+++ b/solution.py
@@ -522,10 +522,61 @@
         hd[kz, 28:32, :] = jnp.zeros((4, 128), f32)
 
 
+def shape_slots(fo, out, sb, sb2):
+    sb[...] = jnp.zeros(sb.shape, f32)
+    sb2[...] = jnp.zeros(sb2.shape, f32)
+
+    def build(g, sb):
+        rows = pl.ds(pl.multiple_of(g * 8, 8), 8)
+        offset = fo[2, rows, :].astype(jnp.int32)
+        wy, ry = axis_tables((offset >> 2) & 3, fo[0, rows, :], 4.0)
+        wz, rz = axis_tables(offset & 3, fo[1, rows, :], 4.0)
+        for jz in range(6):
+            for jy in range(6):
+                r = jz * 6 + jy
+                sb[pl.ds(r * 8, 8), :] = wy[jy] * wz[jz]
+                sb[pl.ds((40 + r) * 8, 8), :] = ry[jy] * wz[jz]
+                sb[pl.ds((80 + r) * 8, 8), :] = wy[jy] * rz[jz]
+
+    def work(g, sb):
+        for j in range(8):
+            right = jnp.concatenate(
+                [sb[pl.ds(n * 320 + j, 40, stride=8), :] for n in range(3)], axis=1
+            )
+            high, low = split_two(right)
+            right = jnp.concatenate([high, high, low, jnp.zeros((8, 384), f32)], axis=0).astype(bf16)
+            out[pl.ds(pl.multiple_of((g * 8 + j) * 128, 128), 128), :] = right
+
+    def pair(i, carry):
+        build(2 * i + 1, sb2)
+        work(2 * i, sb)
+        build(jnp.minimum(2 * i + 2, 15), sb)
+        work(2 * i + 1, sb2)
+        return carry
+
+    build(0, sb)
+    lax.fori_loop(0, 8, pair, 0)
+
+
+def shape_own_kernel(frac, o_ref, out, fo, sb, sb2):
+    fo[0] = frac[1]
+    fo[1] = frac[2]
+    fo[2] = o_ref[...].astype(f32)
+    shape_slots(fo, out, sb, sb2)
+
+
+def shape_new_kernel(rxp, rxm, ryp, rym, out, fo, sb, sb2):
+    places = [(ryp, 0), (rxp, 1), (rym, 0), (ryp, 1), (rym, 1), (ryp, 2), (rxm, 1), (rym, 2)]
+    for g, (ref, at) in enumerate(places):
+        for d in range(3):
+            fo[d, g * 16 : g * 16 + 16, :] = ref[pl.ds(at * way_rows + 1 + d, 16, stride=4), :]
+    shape_slots(fo, out, sb, sb2)
+
+
 def collect_kernel(
-    code_s, brick_s, came_s, ko, rl, rb, rd, solid, frac, o_ref, rxp, rxm, ryp, rym,
+    code_s, brick_s, came_s, ko, rl, rb, rd, solid, frac, o_ref, rxp, rxm, ryp, rym, own_shape, new_shape,
     move_ref, grad_ref, warm_ref, gvel_ref, gtemp_ref,
-    heat, speed, cells, fine, coarse, turn, lu, fo, sb, sw, sb2, sw2,
+    heat, speed, cells, fine, coarse, turn, lu, fo, sw, sw2,
 ):
     lane = lax.broadcasted_iota(jnp.int32, (8, 128), 1)[0:1]
     heat[...] = jnp.zeros(heat.shape, f32)
@@ -611,34 +662,23 @@
                 turn[side, 40 + jz * 6 : 46 + jz * 6, :] = fine[c, jz, rows, :]
                 turn[side, 80 + jz * 6 : 86 + jz * 6, :] = coarse[c, jz, rows, :]
             lu[pl.ds(jx * 4 + c, 128, stride=24), :] = jnp.transpose(turn[side])
-    for d in range(3):
-        fo[d, 0:128, :] = frac[d]
-    fo[3, 0:128, :] = o_ref[...].astype(f32)
+    fo[0, 0:128, :] = frac[0]
+    fo[1, 0:128, :] = o_ref[...].astype(f32)
     places = [(ryp, 0), (rxp, 1), (rym, 0), (ryp, 1), (rym, 1), (ryp, 2), (rxm, 1), (rym, 2)]
     for g, (ref, at) in enumerate(places):
-        for d in range(4):
-            fo[d, 128 + g * 16 : 144 + g * 16, :] = ref[pl.ds(at * way_rows + d, 16, stride=4), :]
-    sb[...] = jnp.zeros(sb.shape, f32)
-    sb2[...] = jnp.zeros(sb2.shape, f32)
-
-    def build(g, sb, sw):
+        for d in range(2):
+            fo[d, 128 + g * 16 : 144 + g * 16, :] = ref[pl.ds(at * way_rows + 3 * d, 16, stride=4), :]
+
+    def build(g, sw):
         rows = pl.ds(pl.multiple_of(g * 8, 8), 8)
-        offset = fo[3, rows, :].astype(jnp.int32)
+        offset = fo[1, rows, :].astype(jnp.int32)
         wx, rx = axis_tables(offset >> 4, fo[0, rows, :], 4.0)
         for j in range(6):
             for copy in range(4):
                 sw[pl.ds((j * 4 + copy) * 8, 8), :] = wx[j]
                 sw[pl.ds((24 + j * 4 + copy) * 8, 8), :] = rx[j]
-        wy, ry = axis_tables((offset >> 2) & 3, fo[1, rows, :], 4.0)
-        wz, rz = axis_tables(offset & 3, fo[2, rows, :], 4.0)
-        for jz in range(6):
-            for jy in range(6):
-                r = jz * 6 + jy
-                sb[pl.ds(r * 8, 8), :] = wy[jy] * wz[jz]
-                sb[pl.ds((40 + r) * 8, 8), :] = ry[jy] * wz[jz]
-                sb[pl.ds((80 + r) * 8, 8), :] = wy[jy] * rz[jz]
-
-    def work(g, sb, sw):
+
+    def work(g, shaped, first, sw):
         for j in range(8):
             slot = g * 8 + j
             home = jnp.minimum(slot, 127)
@@ -647,11 +687,7 @@
             live = jnp.where(brick >= 0, 1.0, 0.0).astype(f32)
             spot = pl.ds(pl.multiple_of(jnp.maximum(brick, 0) * 24, 8), 24)
             left = lu[spot, :].astype(bf16)
-            right = jnp.concatenate(
-                [sb[pl.ds(n * 320 + j, 40, stride=8), :] for n in range(3)], axis=1
-            )
-            high, low = split_two(right)
-            right = jnp.concatenate([high, high, low, jnp.zeros((8, 384), f32)], axis=0).astype(bf16)
+            right = shaped[pl.ds(pl.multiple_of((slot - first) * 128, 128), 128), :]
             both = jnp.dot(left, right, preferred_element_type=f32)
             plain = sw[pl.ds(j, 24, stride=8), :]
             tilt = sw[pl.ds(192 + j, 24, stride=8), :]
@@ -670,15 +706,19 @@
                 for a in range(3):
                     grad_ref[a * 3 + k : a * 3 + k + 1, lanes] = part[a : a + 1]
 
-    def pair(i, carry):
-        build(2 * i + 1, sb2, sw2)
-        work(2 * i, sb, sw)
-        build(jnp.minimum(2 * i + 2, 31), sb, sw)
-        work(2 * i + 1, sb2, sw2)
-        return carry
-
-    build(0, sb, sw)
-    lax.fori_loop(0, 16, pair, 0)
+    for shaped, first in ((own_shape, 0), (new_shape, 128)):
+        last = first // 8 + 15
+
+        def pair(i, carry, shaped=shaped, first=first, last=last):
+            g = first // 8 + 2 * i
+            build(g + 1, sw2)
+            work(g, shaped, first, sw)
+            build(jnp.minimum(g + 2, last), sw)
+            work(g + 1, shaped, first, sw2)
+            return carry
+
+        build(first // 8, sw)
+        lax.fori_loop(0, 8, pair, 0)
 
 
 def neighbor(value, dx, dy):
@@ -696,7 +736,7 @@
 
 
 def call(
-    kernel, name, inputs, scalars, outputs, scratch, left_there=0, limit=50, flops=1e8, listed=0
+    kernel, name, inputs, scalars, outputs, scratch, left_there=0, limit=24, flops=1e8, listed=0
 ):
     in_specs = (
         [pl.BlockSpec(memory_space=pltpu.SMEM)] * scalars
@@ -878,6 +918,13 @@
         ],
         [vmem(tiles * 128, 128), vmem(4, 184, 128)],
     )
+    shape_scratch = [vmem(3, 128, 128), vmem(120 * 8, 128), vmem(120 * 8, 128)]
+    shape_out = [((128 * 128, 384), bf16)]
+    frac, ml, mb, md = lax.optimization_barrier((frac, ml, mb, md))
+    (own_shape,) = call(
+        shape_own_kernel, "shape_own", (frac, offset), 0, shape_out, shape_scratch, flops=4e9
+    )
+    region, own_shape = lax.optimization_barrier((region, own_shape))
     hl, hb, hd, ko = call(
         update_kernel,
         "update",
@@ -890,6 +937,10 @@
             ((4, 88, 128), f32),
         ],
         [vmem(2, 4, 40, 128), vmem(5, 4, 16, 128)],
+    )
+    came_from, hl, hb, hd = lax.optimization_barrier(((rsxp, rsxm, rsyp, rsym), hl, hb, hd))
+    (new_shape,) = call(
+        shape_new_kernel, "shape_new", came_from, 0, shape_out, shape_scratch, flops=4e9
     )
     move, grad, warm, gvel, gtemp = call(
         collect_kernel,
@@ -909,6 +960,8 @@
             rsxm,
             rsyp,
             rsym,
+            own_shape,
+            new_shape,
         ),
         3,
         [
@@ -926,10 +979,8 @@
             vmem(4, 6, 40, 128),
             vmem(2, 128, 128),
             vmem(128 * 24, 128),
-            vmem(4, 256, 128),
-            vmem(120 * 8, 128),
+            vmem(2, 256, 128),
             vmem(48 * 8, 128),
-            vmem(120 * 8, 128),
             vmem(48 * 8, 128),
         ],
     )

time: 67 us -> 65.4 us (0.976)
  waiting for transfers between devices: 17.7 us -> 13.2 us
  Pallas kernels: 28.1 us -> 30.7 us
  starting transfers between devices: 19.9 us -> 21 us
    ppermute x2, waiting for transfers between devices: 14.2 us -> 7.08 us  [neighbor(): return lax.ppermute(value, ('gx', 'gy'), pairs)]
    pallas_call x8 -> x10, Pallas kernels: 28.1 us -> 30.7 us  [call(): pl.pallas_call(kernel, name=name, out_shape=[jax.ShapeDtypeStruct(shape,...]
    ppermute x2, starting transfers between devices: 0.08 us -> 2.04 us  [neighbor(): return lax.ppermute(value, ('gx', 'gy'), pairs)]
    ppermute x6, waiting for transfers between devices: 0.83 us -> 2.35 us  [neighbor(): lax.ppermute(value, 'gy', [(i, (i + dy) % size_y) for i in range(size_y)])]
    ppermute x6, waiting for transfers between devices: 2.66 us -> 3.72 us  [neighbor(): lax.ppermute(value, 'gx', [(i, (i + dx) % size_x) for i in range(size_x)])]
    ppermute x6, starting transfers between devices: 7.74 us -> 6.79 us  [neighbor(): lax.ppermute(value, 'gx', [(i, (i + dx) % size_x) for i in range(size_x)])]
  transfers between devices with their start and end apart: 14 -> 14, of which waited for: 4 -> 3; matrix products, arithmetic and copies ran while one was open for 0% -> 0% of each run, Pallas kernels for 19% -> 24%
where the time goes in v3:
time: 65.4 us; the launch traced here: 65.7 us
  Pallas kernels  30.7 us (47%)
  starting transfers between devices  21 us (32%)
  waiting for transfers between devices  13.2 us (20%)
  between operations  0.85 us (1%)
    pallas_call x10, Pallas kernels, call(): pl.pallas_call(kernel, name=name, out_shape=[jax.ShapeDtypeStruct(shape,...  30.7 us
    ppermute x6, starting transfers between devices, neighbor(): lax.ppermute(value, 'gy', [(i, (i + dy) % size_y) for i in range(size_y)])  12.1 us
    ppermute x2, waiting for transfers between devices, neighbor(): return lax.ppermute(value, ('gx', 'gy'), pairs)  7.08 us
    ppermute x6, starting transfers between devices, neighbor(): lax.ppermute(value, 'gx', [(i, (i + dx) % size_x) for i in range(size_x)])  6.79 us
    ppermute x6, waiting for transfers between devices, neighbor(): lax.ppermute(value, 'gx', [(i, (i + dx) % size_x) for i in range(size_x)])  3.72 us
    ppermute x6, waiting for transfers between devices, neighbor(): lax.ppermute(value, 'gy', [(i, (i + dy) % size_y) for i in range(size_y)])  2.35 us
    ppermute x2, starting transfers between devices, neighbor(): return lax.ppermute(value, ('gx', 'gy'), pairs)  2.04 us
  transfers between devices with their start and end apart: 14, of which 3 were waited for; matrix products, arithmetic and copies ran while one was open for 0% of the time, Pallas kernels for 24%

profile of v3, /device:TPU:0, one launch (start us, length us, event | category | flops | bytes accessed | tf_op | source)
XLA Modules:
  0.0 65.7 jit_solution(13240909546865423189)
XLA Ops:
  0.6 3.9 %prepare.1 = (s32[768]{0:T(1024)S(1)}, f32[6,96,128]{2,1,0:T(8,128)S(1)}, f32[352,128]{1,0:T(8,128)S(1)}, f32[224,128]{1,0:T(8,128)S(1)}, f32[3,16384]{1,0:T(4,1...) custom-call(f32[3,64]{1,0:T(4,128)} %table_hbm.1, ...), custom_call_target="tpu_custom_call" | custom-call | flops 2000000000 | bytes 6666666 | tf_op jit(solution)/shard_map/prepare/pallas_call | solution.py:746
  4.6 2.3 %collective-permute-start.1 = (f32[224,128]{1,0:T(8,128)S(1)}, f32[224,128]{1,0:T(8,128)S(1)}, u32[]{:S(2)}, u32[]{:S(2)}) collective-permute-start(f32[224,128]{1,0:T(8,128)S(1)} %get-tuple-element.73), channel_id=1, source_target_pairs={{0,112},{16,0},{32,16},{48,32},{64,48},{80,64},{96,80},{112,96},{1... | collective-permute-start | bytes 344072 | tf_op jit(solution)/shard_map/ppermute | solution.py:727
  6.8 0.0 collective-permute-start
  6.8 2.4 %outgoing.1 = (f32[432,128]{1,0:T(8,128)S(1)}, f32[144,128]{1,0:T(8,128)S(1)}, f32[144,128]{1,0:T(8,128)S(1)}, f32[432,128]{1,0:T(8,128)S(1)}) custom-call(s32[768]{0:T(1024)S(1)} %get-tuple-element.78.info_s, f32[3,16384]{1,0:T(4,128)S(1)} %get-tuple-element.63.f_ref, f32[3,16384]{1,0:T(4,128)S(1)} %get-tuple-element.64.v_ref, ...), custom_call_target="tpu_custom_call" | custom-call | flops 6000000000 | bytes 20000000 | tf_op jit(solution)/shard_map/outgoing/pallas_call | solution.py:746
  9.3 3.7 %collective-permute-done.left.rxp = f32[352,128]{1,0:T(8,128)S(1)} collective-permute-done((f32[352,128]{1,0:T(8,128)S(1)}, f32[352,128]{1,0:T(8,128)S(1)}, u32[]{:S(2)}, u32[]{:S(2)}) %collective-permute-start) | collective-permute-done | bytes 180256 | tf_op jit(solution)/shard_map/ppermute | solution.py:727
  13.0 0.0 collective-permute-start.2
  13.0 3.0 %collective-permute-start.3 = (f32[432,128]{1,0:T(8,128)S(1)}, f32[432,128]{1,0:T(8,128)S(1)}, u32[]{:S(2)}, u32[]{:S(2)}) collective-permute-start(f32[432,128]{1,0:T(8,128)S(1)} %get-tuple-element.76), channel_id=1, source_target_pairs={{0,112},{16,0},{32,16},{48,32},{64,48},{80,64},{96,80},{112,96},{1... | collective-permute-start | bytes 663560 | tf_op jit(solution)/shard_map/ppermute | solution.py:727
  15.9 0.1 relay.1
  16.0 6.6 %collective-permute-start.10 = (f32[288,128]{1,0:T(8,128)S(1)}, f32[288,128]{1,0:T(8,128)S(1)}, u32[]{:S(2)}, u32[]{:S(2)}) collective-permute-start(f32[288,128]{1,0:T(8,128)S(1)} %get-tuple-element.95), channel_id=1, source_target_pairs={{0,15},{1,0},{2,1},{3,2},{4,3},{5,4},{6,5},{7,6},{8,7},{9,8},{10,9... | collective-permute-start | bytes 442376 | tf_op jit(solution)/shard_map/ppermute | solution.py:729
  22.7 0.0 copy-start
  22.7 0.1 collective-permute-start.4
  22.8 5.4 %collective-permute-start.5 = (f32[432,128]{1,0:T(8,128)S(1)}, f32[432,128]{1,0:T(8,128)S(1)}, u32[]{:S(2)}, u32[]{:S(2)}) collective-permute-start(f32[432,128]{1,0:T(8,128)S(1)} %get-tuple-element.81), channel_id=1, source_target_pairs={{0,15},{1,0},{2,1},{3,2},{4,3},{5,4},{6,5},{7,6},{8,7},{9,8},{10,9... | collective-permute-start | bytes 663560 | tf_op jit(solution)/shard_map/ppermute | solution.py:729
  28.2 9.0 %staying.1 = (f32[9,128,128]{2,1,0:T(8,128)S(1)}, f32[3,128,128]{2,1,0:T(8,128)S(1)}) custom-call(s32[768]{0:T(1024)S(1)} %get-tuple-element.78.info_s, f32[3,16384]{1,0:T(4,128)S(1)} %get-tuple-element.63.f_ref, f32[3,16384]{1,0:T(4,128)S(1)} %get-tuple-element.64.v_ref, f32[9,16384]{1,0:T(8,128)S(1)} %get-tuple-element.65.c_ref, ...), custom_call_target="tpu_custom_call" | custom-call | flops 10000000000 | bytes 33333332 | tf_op jit(solution)/shard_map/staying/pallas_call | solution.py:746
  37.1 0.0 collective-permute-done.10.above.rym
  37.2 0.1 assemble.1
  37.3 0.0 collective-permute-done.4.ryp
  37.3 0.7 %total.1 = (f32[4,56,128]{2,1,0:T(8,128)S(1)}, f32[4,56,128]{2,1,0:T(8,128)S(1)}, f32[4,48,128]{2,1,0:T(8,128)S(1)}, f32[4,80,128]{2,1,0:T(8,128)S(1)}, s32[1,128]{1,0:T(1,128)S(1)}) custom-call(f32[9,128,128]{2,1,0:T(8,128)S(1)} %get-tuple-element.79.own_ref, f32[432,128]{1,0:T(8,128)S(1)} %collective-permute-done.2.rxp, ...), custom_call_target="tpu_custom_call" | custom-call | flops 100000000 | bytes 333333 | tf_op jit(solution)/shard_map/total/pallas_call | solution.py:746
  38.0 0.0 copy-start.1
  38.1 0.0 copy-start.2
  38.1 0.1 collective-permute-start.8
  38.1 0.0 collective-permute-start.6
  38.2 0.1 collective-permute-start.7
  38.3 2.3 %shape_own.1.own_shape = bf16[16384,384]{1,0:T(8,128)(2,1)S(1)} custom-call(f32[3,128,128]{2,1,0:T(8,128)S(1)} %get-tuple-element.97.frac, s32[128,128]{1,0:T(8,128)S(1)} %bitcast.5), custom_call_target="tpu_custom_call" | custom-call | flops 4000000000 | bytes 13333333 | tf_op jit(solution)/shard_map/shape_own/pallas_call | solution.py:746
  40.5 7.1 %collective-permute-done.8.rd = f32[4,48,128]{2,1,0:T(8,128)S(1)} collective-permute-done((f32[4,48,128]{2,1,0:T(8,128)S(1)}, f32[4,48,128]{2,1,0:T(8,128)S(1)}, u32[]{:S(2)}, u32[]{:S(2)}) %collective-permute-start.8) | collective-permute-done | bytes 98336 | tf_op jit(solution)/shard_map/ppermute | solution.py:735
  47.6 0.3 update.1
  47.9 2.0 %collective-permute-start.13 = (f32[4,32,128]{2,1,0:T(8,128)S(1)}, f32[4,32,128]{2,1,0:T(8,128)S(1)}, u32[]{:S(2)}, u32[]{:S(2)}) collective-permute-start(f32[4,32,128]{2,1,0:T(8,128)S(1)} %get-tuple-element.107), channel_id=1, source_target_pairs={{0,127},{1,112},{2,113},{3,114},{4,115},{5,116},{6,117},{7,118},{8... | collective-permute-start | bytes 196616 | tf_op jit(solution)/shard_map/ppermute | solution.py:735
  49.9 1.5 %collective-permute-start.11 = (f32[4,48,128]{2,1,0:T(8,128)S(1)}, f32[4,48,128]{2,1,0:T(8,128)S(1)}, u32[]{:S(2)}, u32[]{:S(2)}) collective-permute-start(f32[4,48,128]{2,1,0:T(8,128)S(1)} %get-tuple-element.105), channel_id=1, source_target_pairs={{0,112},{16,0},{32,16},{48,32},{64,48},{80,64},{96,80},{112,96},{1... | collective-permute-start | bytes 294920 | tf_op jit(solution)/shard_map/ppermute | solution.py:727
  51.4 0.0 collective-permute-start.12
  51.4 2.2 %shape_new.1.new_shape = bf16[16384,384]{1,0:T(8,128)(2,1)S(1)} custom-call(f32[352,128]{1,0:T(8,128)S(1)} %collective-permute-done.left.rxp, f32[224,128]{1,0:T(8,128)S(1)} %collective-permute-done.1.right.rxm, f32[448,128]{1,0:T(8,128)S(1)} %collective-permute-done.9.below.ryp, f32[288,128]{1,0:T(8,128)S(1)} %collective-permute-done.10.above.rym), custom_call_target="tpu_custom_call" | custom-call | flops 4000000000 | bytes 13333333 | tf_op jit(solution)/shard_map/shape_new/pallas_call | solution.py:746
  53.7 0.0 collective-permute-done.11.rl
  53.7 2.3 %collective-permute-done.12.rb = f32[4,48,128]{2,1,0:T(8,128)S(1)} collective-permute-done((f32[4,48,128]{2,1,0:T(8,128)S(1)}, f32[4,48,128]{2,1,0:T(8,128)S(1)}, u32[]{:S(2)}, u32[]{:S(2)}) %collective-permute-start.12) | collective-permute-done | bytes 98336 | tf_op jit(solution)/shard_map/ppermute | solution.py:729
  56.0 9.7 %collect.1 = (f32[3,32768]{1,0:T(4,128)}, f32[9,32768]{1,0:T(8,128)}, f32[256,128]{1,0:T(8,128)}, f32[3,4,4,512]{3,2,1,0:T(4,128)}, f32[4,4,512]{2,1,0:T(4,128)}) custom-call(s32[128]{0:T(128)S(1)} %copy-done.1, s32[128]{0:T(128)S(1)} %copy-done.2, s32[1,128]{1,0:T(1,128)S(1)} %get-tuple-element.82.came_s, f32[4,88,128]{2,1,0:T(8,128)S(1)} %get-tuple-element.101.ko, ...), custom_call_target="tpu_custom_call" | custom-call | flops 100000000 | bytes 333333 | tf_op jit(solution)/shard_map/collect/pallas_call | solution.py:746
  (15 shorter events, 0.1 us)
Async XLA Ops:
  4.6 4.7 %collective-permute-start.1 = (f32[224,128]{1,0:T(8,128)S(1)}, f32[224,128]{1,0:T(8,128)S(1)}, u32[]{:S(2)}, u32[]{:S(2)}) collective-permute-start(f32[224,128]{1,0:T(8,128)S(1)} %get-tuple-element.73), channel_id=1, source_target_pairs={{0,112},{16,0},{32,16},{48,32},{64,48},{80,64},{96,80},{112,96},{1... | collective-permute-start | bytes 344072 | tf_op jit(solution)/shard_map/ppermute | solution.py:727
  6.8 6.1 %collective-permute-start = (f32[352,128]{1,0:T(8,128)S(1)}, f32[352,128]{1,0:T(8,128)S(1)}, u32[]{:S(2)}, u32[]{:S(2)}) collective-permute-start(f32[352,128]{1,0:T(8,128)S(1)} %get-tuple-element.72), channel_id=1, source_target_pairs={{0,16},{16,32},{32,48},{48,64},{64,80},{80,96},{96,112},{112,0},{1... | collective-permute-start | bytes 540680 | tf_op jit(solution)/shard_map/ppermute | solution.py:727
  13.0 9.6 %collective-permute-start.2 = (f32[432,128]{1,0:T(8,128)S(1)}, f32[432,128]{1,0:T(8,128)S(1)}, u32[]{:S(2)}, u32[]{:S(2)}) collective-permute-start(f32[432,128]{1,0:T(8,128)S(1)} %get-tuple-element.74), channel_id=1, source_target_pairs={{0,16},{16,32},{32,48},{48,64},{64,80},{80,96},{96,112},{112,0},{1... | collective-permute-start | bytes 663560 | tf_op jit(solution)/shard_map/ppermute | solution.py:727
  13.0 9.6 %collective-permute-start.3 = (f32[432,128]{1,0:T(8,128)S(1)}, f32[432,128]{1,0:T(8,128)S(1)}, u32[]{:S(2)}, u32[]{:S(2)}) collective-permute-start(f32[432,128]{1,0:T(8,128)S(1)} %get-tuple-element.76), channel_id=1, source_target_pairs={{0,112},{16,0},{32,16},{48,32},{64,48},{80,64},{96,80},{112,96},{1... | collective-permute-start | bytes 663560 | tf_op jit(solution)/shard_map/ppermute | solution.py:727
  16.0 21.1 %collective-permute-start.10 = (f32[288,128]{1,0:T(8,128)S(1)}, f32[288,128]{1,0:T(8,128)S(1)}, u32[]{:S(2)}, u32[]{:S(2)}) collective-permute-start(f32[288,128]{1,0:T(8,128)S(1)} %get-tuple-element.95), channel_id=1, source_target_pairs={{0,15},{1,0},{2,1},{3,2},{4,3},{5,4},{6,5},{7,6},{8,7},{9,8},{10,9... | collective-permute-start | bytes 442376 | tf_op jit(solution)/shard_map/ppermute | solution.py:729
  22.6 14.6 %collective-permute-start.9 = (f32[448,128]{1,0:T(8,128)S(1)}, f32[448,128]{1,0:T(8,128)S(1)}, u32[]{:S(2)}, u32[]{:S(2)}) collective-permute-start(f32[448,128]{1,0:T(8,128)S(1)} %get-tuple-element.94), channel_id=1, source_target_pairs={{0,1},{1,2},{2,3},{3,4},{4,5},{5,6},{6,7},{7,8},{8,9},{9,10},{10,1... | collective-permute-start | bytes 688136 | tf_op jit(solution)/shard_map/ppermute | solution.py:729
  22.7 15.6 %copy-start = (s32[16384]{0:T(1024)S(1)}, s32[16384]{0:T(1024)}, u32[]{:S(2)}) copy-start(s32[16384]{0:T(1024)} %param.20) | copy-start | bytes 196612
  22.7 14.6 %collective-permute-start.4 = (f32[432,128]{1,0:T(8,128)S(1)}, f32[432,128]{1,0:T(8,128)S(1)}, u32[]{:S(2)}, u32[]{:S(2)}) collective-permute-start(f32[432,128]{1,0:T(8,128)S(1)} %get-tuple-element.80), channel_id=1, source_target_pairs={{0,1},{1,2},{2,3},{3,4},{4,5},{5,6},{6,7},{7,8},{8,9},{9,10},{10,1... | collective-permute-start | bytes 663560 | tf_op jit(solution)/shard_map/ppermute | solution.py:729
  22.8 14.5 %collective-permute-start.5 = (f32[432,128]{1,0:T(8,128)S(1)}, f32[432,128]{1,0:T(8,128)S(1)}, u32[]{:S(2)}, u32[]{:S(2)}) collective-permute-start(f32[432,128]{1,0:T(8,128)S(1)} %get-tuple-element.81), channel_id=1, source_target_pairs={{0,15},{1,0},{2,1},{3,2},{4,3},{5,4},{6,5},{7,6},{8,7},{9,8},{10,9... | collective-permute-start | bytes 663560 | tf_op jit(solution)/shard_map/ppermute | solution.py:729
  38.0 18.0 %copy-start.1 = (s32[128]{0:T(128)S(1)}, s32[128]{0:T(128)}, u32[]{:S(2)}) copy-start(s32[128]{0:T(128)} %code_s.1) | copy-start | bytes 1540
  38.1 18.0 %copy-start.2 = (s32[128]{0:T(128)S(1)}, s32[128]{0:T(128)}, u32[]{:S(2)}) copy-start(s32[128]{0:T(128)} %brick_s.1) | copy-start | bytes 1540
  38.1 9.5 %collective-permute-start.8 = (f32[4,48,128]{2,1,0:T(8,128)S(1)}, f32[4,48,128]{2,1,0:T(8,128)S(1)}, u32[]{:S(2)}, u32[]{:S(2)}) collective-permute-start(f32[4,48,128]{2,1,0:T(8,128)S(1)} %get-tuple-element.90), channel_id=1, source_target_pairs={{0,17},{1,18},{2,19},{3,20},{4,21},{5,22},{6,23},{7,24},{8,25},{9,... | collective-permute-start | bytes 294920 | tf_op jit(solution)/shard_map/ppermute | solution.py:735
  38.1 9.5 %collective-permute-start.6 = (f32[4,56,128]{2,1,0:T(8,128)S(1)}, f32[4,56,128]{2,1,0:T(8,128)S(1)}, u32[]{:S(2)}, u32[]{:S(2)}) collective-permute-start(f32[4,56,128]{2,1,0:T(8,128)S(1)} %get-tuple-element.88), channel_id=1, source_target_pairs={{0,16},{16,32},{32,48},{48,64},{64,80},{80,96},{96,112},{112,0},{1... | collective-permute-start | bytes 344072 | tf_op jit(solution)/shard_map/ppermute | solution.py:727
  38.2 9.4 %collective-permute-start.7 = (f32[4,56,128]{2,1,0:T(8,128)S(1)}, f32[4,56,128]{2,1,0:T(8,128)S(1)}, u32[]{:S(2)}, u32[]{:S(2)}) collective-permute-start(f32[4,56,128]{2,1,0:T(8,128)S(1)} %get-tuple-element.89), channel_id=1, source_target_pairs={{0,1},{1,2},{2,3},{3,4},{4,5},{5,6},{6,7},{7,8},{8,9},{9,10},{10,1... | collective-permute-start | bytes 344072 | tf_op jit(solution)/shard_map/ppermute | solution.py:729
  47.9 5.8 %collective-permute-start.13 = (f32[4,32,128]{2,1,0:T(8,128)S(1)}, f32[4,32,128]{2,1,0:T(8,128)S(1)}, u32[]{:S(2)}, u32[]{:S(2)}) collective-permute-start(f32[4,32,128]{2,1,0:T(8,128)S(1)} %get-tuple-element.107), channel_id=1, source_target_pairs={{0,127},{1,112},{2,113},{3,114},{4,115},{5,116},{6,117},{7,118},{8... | collective-permute-start | bytes 196616 | tf_op jit(solution)/shard_map/ppermute | solution.py:735
  49.9 3.8 %collective-permute-start.11 = (f32[4,48,128]{2,1,0:T(8,128)S(1)}, f32[4,48,128]{2,1,0:T(8,128)S(1)}, u32[]{:S(2)}, u32[]{:S(2)}) collective-permute-start(f32[4,48,128]{2,1,0:T(8,128)S(1)} %get-tuple-element.105), channel_id=1, source_target_pairs={{0,112},{16,0},{32,16},{48,32},{64,48},{80,64},{96,80},{112,96},{1... | collective-permute-start | bytes 294920 | tf_op jit(solution)/shard_map/ppermute | solution.py:727
  51.4 4.6 %collective-permute-start.12 = (f32[4,48,128]{2,1,0:T(8,128)S(1)}, f32[4,48,128]{2,1,0:T(8,128)S(1)}, u32[]{:S(2)}, u32[]{:S(2)}) collective-permute-start(f32[4,48,128]{2,1,0:T(8,128)S(1)} %get-tuple-element.106), channel_id=1, source_target_pairs={{0,15},{1,0},{2,1},{3,2},{4,3},{5,4},{6,5},{7,6},{8,7},{9,8},{10,9... | collective-permute-start | bytes 294920 | tf_op jit(solution)/shard_map/ppermute | solution.py:729

commit v4 on v3

--- a/solution.py
+++ b/solution.py
@@ -860,7 +860,6 @@
         limit=24,
         flops=6e9,
     )
-    xm, xp, rsxp, rsxm = lax.optimization_barrier((xm, xp, rsxp, rsxm))
     rxp = neighbor(xp, 1, 0)
     rxm = neighbor(xm, -1, 0)
     up, down = call(

time: 65.4 us -> 64.7 us (0.989)
  starting transfers between devices: 21 us -> 19.5 us
    ppermute x6, waiting for transfers between devices: 2.35 us -> 4.26 us  [neighbor(): lax.ppermute(value, 'gy', [(i, (i + dy) % size_y) for i in range(size_y)])]
    ppermute x6, waiting for transfers between devices: 3.72 us -> 1.89 us  [neighbor(): lax.ppermute(value, 'gx', [(i, (i + dx) % size_x) for i in range(size_x)])]
    ppermute x6, starting transfers between devices: 6.79 us -> 5.1 us  [neighbor(): lax.ppermute(value, 'gx', [(i, (i + dx) % size_x) for i in range(size_x)])]
    ppermute x6, starting transfers between devices: 12.1 us -> 12.9 us  [neighbor(): lax.ppermute(value, 'gy', [(i, (i + dy) % size_y) for i in range(size_y)])]
  transfers between devices with their start and end apart: 14 -> 14, of which waited for: 3 -> 5; matrix products, arithmetic and copies ran while one was open for 0% -> 0% of each run, Pallas kernels for 24% -> 25%
where the time goes in v4:
time: 64.7 us; the launch traced here: 64.6 us
  Pallas kernels  30.9 us (48%)
  starting transfers between devices  19.5 us (30%)
  waiting for transfers between devices  13.3 us (21%)
  between operations  0.83 us (1%)
    pallas_call x10, Pallas kernels, call(): pl.pallas_call(kernel, name=name, out_shape=[jax.ShapeDtypeStruct(shape,...  30.9 us
    ppermute x6, starting transfers between devices, neighbor(): lax.ppermute(value, 'gy', [(i, (i + dy) % size_y) for i in range(size_y)])  12.9 us
    ppermute x2, waiting for transfers between devices, neighbor(): return lax.ppermute(value, ('gx', 'gy'), pairs)  7.18 us
    ppermute x6, starting transfers between devices, neighbor(): lax.ppermute(value, 'gx', [(i, (i + dx) % size_x) for i in range(size_x)])  5.1 us
    ppermute x6, waiting for transfers between devices, neighbor(): lax.ppermute(value, 'gy', [(i, (i + dy) % size_y) for i in range(size_y)])  4.26 us
    ppermute x6, waiting for transfers between devices, neighbor(): lax.ppermute(value, 'gx', [(i, (i + dx) % size_x) for i in range(size_x)])  1.89 us
    ppermute x2, starting transfers between devices, neighbor(): return lax.ppermute(value, ('gx', 'gy'), pairs)  1.5 us
  transfers between devices with their start and end apart: 14, of which 5 were waited for; matrix products, arithmetic and copies ran while one was open for 0% of the time, Pallas kernels for 25%

profile of v4, /device:TPU:0, one launch (start us, length us, event | category | flops | bytes accessed | tf_op | source)
XLA Modules:
  0.0 64.6 jit_solution(10534707887895820382)
XLA Ops:
  0.6 3.9 %prepare.1 = (s32[768]{0:T(1024)S(1)}, f32[6,96,128]{2,1,0:T(8,128)S(1)}, f32[352,128]{1,0:T(8,128)S(1)}, f32[224,128]{1,0:T(8,128)S(1)}, f32[3,16384]{1,0:T(4,1...) custom-call(f32[3,64]{1,0:T(4,128)} %table_hbm.1, ...), custom_call_target="tpu_custom_call" | custom-call | flops 2000000000 | bytes 6666666 | tf_op jit(solution)/shard_map/prepare/pallas_call | solution.py:746
  4.6 0.0 collective-permute-start.7
  4.6 3.4 %outgoing.1 = (f32[432,128]{1,0:T(8,128)S(1)}, f32[144,128]{1,0:T(8,128)S(1)}, f32[144,128]{1,0:T(8,128)S(1)}, f32[432,128]{1,0:T(8,128)S(1)}) custom-call(s32[768]{0:T(1024)S(1)} %get-tuple-element.70.info_s, f32[3,16384]{1,0:T(4,128)S(1)} %get-tuple-element.59.f_ref, f32[3,16384]{1,0:T(4,128)S(1)} %get-tuple-element.60.v_ref, ...), custom_call_target="tpu_custom_call" | custom-call | flops 6000000000 | bytes 20000000 | tf_op jit(solution)/shard_map/outgoing/pallas_call | solution.py:746
  8.0 1.8 %collective-permute-start = (f32[432,128]{1,0:T(8,128)S(1)}, f32[432,128]{1,0:T(8,128)S(1)}, u32[]{:S(2)}, u32[]{:S(2)}) collective-permute-start(f32[432,128]{1,0:T(8,128)S(1)} %get-tuple-element.66), channel_id=1, source_target_pairs={{0,16},{16,32},{32,48},{48,64},{64,80},{80,96},{96,112},{112,0},{1... | collective-permute-start | bytes 663560 | tf_op jit(solution)/shard_map/ppermute | solution.py:727
  9.7 1.3 %collective-permute-start.8 = (f32[224,128]{1,0:T(8,128)S(1)}, f32[224,128]{1,0:T(8,128)S(1)}, u32[]{:S(2)}, u32[]{:S(2)}) collective-permute-start(f32[224,128]{1,0:T(8,128)S(1)} %get-tuple-element.85), channel_id=1, source_target_pairs={{0,112},{16,0},{32,16},{48,32},{64,48},{80,64},{96,80},{112,96},{1... | collective-permute-start | bytes 344072 | tf_op jit(solution)/shard_map/ppermute | solution.py:727
  11.0 0.5 collective-permute-start.1
  11.5 1.9 %collective-permute-done.8.right.rxm = f32[224,128]{1,0:T(8,128)S(1)} collective-permute-done((f32[224,128]{1,0:T(8,128)S(1)}, f32[224,128]{1,0:T(8,128)S(1)}, u32[]{:S(2)}, u32[]{:S(2)}) %collective-permute-start.8) | collective-permute-done | bytes 114720 | tf_op jit(solution)/shard_map/ppermute | solution.py:727
  13.4 0.1 relay.1
  13.5 7.3 %collective-permute-start.10 = (f32[288,128]{1,0:T(8,128)S(1)}, f32[288,128]{1,0:T(8,128)S(1)}, u32[]{:S(2)}, u32[]{:S(2)}) collective-permute-start(f32[288,128]{1,0:T(8,128)S(1)} %get-tuple-element.87), channel_id=1, source_target_pairs={{0,15},{1,0},{2,1},{3,2},{4,3},{5,4},{6,5},{7,6},{8,7},{9,8},{10,9... | collective-permute-start | bytes 442376 | tf_op jit(solution)/shard_map/ppermute | solution.py:729
  20.9 0.0 copy-start
  20.9 0.1 collective-permute-start.2
  21.0 5.4 %collective-permute-start.3 = (f32[432,128]{1,0:T(8,128)S(1)}, f32[432,128]{1,0:T(8,128)S(1)}, u32[]{:S(2)}, u32[]{:S(2)}) collective-permute-start(f32[432,128]{1,0:T(8,128)S(1)} %get-tuple-element.73), channel_id=1, source_target_pairs={{0,15},{1,0},{2,1},{3,2},{4,3},{5,4},{6,5},{7,6},{8,7},{9,8},{10,9... | collective-permute-start | bytes 663560 | tf_op jit(solution)/shard_map/ppermute | solution.py:729
  26.4 8.2 %staying.1 = (f32[9,128,128]{2,1,0:T(8,128)S(1)}, f32[3,128,128]{2,1,0:T(8,128)S(1)}) custom-call(s32[768]{0:T(1024)S(1)} %get-tuple-element.70.info_s, f32[3,16384]{1,0:T(4,128)S(1)} %get-tuple-element.59.f_ref, f32[3,16384]{1,0:T(4,128)S(1)} %get-tuple-element.60.v_ref, f32[9,16384]{1,0:T(8,128)S(1)} %get-tuple-element.61.c_ref, ...), custom_call_target="tpu_custom_call" | custom-call | flops 10000000000 | bytes 33333332 | tf_op jit(solution)/shard_map/staying/pallas_call | solution.py:746
  34.6 0.0 collective-permute-done.10.above.rym
  34.6 0.1 assemble.1
  34.7 1.5 %collective-permute-done.2.ryp = f32[432,128]{1,0:T(8,128)S(1)} collective-permute-done((f32[432,128]{1,0:T(8,128)S(1)}, f32[432,128]{1,0:T(8,128)S(1)}, u32[]{:S(2)}, u32[]{:S(2)}) %collective-permute-start.2) | collective-permute-done | bytes 221216 | tf_op jit(solution)/shard_map/ppermute | solution.py:729
  36.2 0.7 %total.1 = (f32[4,56,128]{2,1,0:T(8,128)S(1)}, f32[4,56,128]{2,1,0:T(8,128)S(1)}, f32[4,48,128]{2,1,0:T(8,128)S(1)}, f32[4,80,128]{2,1,0:T(8,128)S(1)}, s32[1,128]{1,0:T(1,128)S(1)}) custom-call(f32[9,128,128]{2,1,0:T(8,128)S(1)} %get-tuple-element.71.own_ref, f32[432,128]{1,0:T(8,128)S(1)} %collective-permute-done.rxp, ...), custom_call_target="tpu_custom_call" | custom-call | flops 100000000 | bytes 333333 | tf_op jit(solution)/shard_map/total/pallas_call | solution.py:746
  36.9 0.0 copy-start.1
  36.9 0.0 copy-start.2
  37.0 0.1 collective-permute-start.6
  37.0 0.0 collective-permute-start.4
  37.1 0.1 collective-permute-start.5
  37.2 2.3 %shape_own.1.own_shape = bf16[16384,384]{1,0:T(8,128)(2,1)S(1)} custom-call(f32[3,128,128]{2,1,0:T(8,128)S(1)} %get-tuple-element.89.frac, s32[128,128]{1,0:T(8,128)S(1)} %bitcast.5), custom_call_target="tpu_custom_call" | custom-call | flops 4000000000 | bytes 13333333 | tf_op jit(solution)/shard_map/shape_own/pallas_call | solution.py:746
  39.4 7.2 %collective-permute-done.6.rd = f32[4,48,128]{2,1,0:T(8,128)S(1)} collective-permute-done((f32[4,48,128]{2,1,0:T(8,128)S(1)}, f32[4,48,128]{2,1,0:T(8,128)S(1)}, u32[]{:S(2)}, u32[]{:S(2)}) %collective-permute-start.6) | collective-permute-done | bytes 98336 | tf_op jit(solution)/shard_map/ppermute | solution.py:735
  46.6 0.0 collective-permute-done.4.rl
  46.6 0.4 collective-permute-done.5.rb
  47.1 0.3 update.1
  47.3 1.4 %collective-permute-start.13 = (f32[4,32,128]{2,1,0:T(8,128)S(1)}, f32[4,32,128]{2,1,0:T(8,128)S(1)}, u32[]{:S(2)}, u32[]{:S(2)}) collective-permute-start(f32[4,32,128]{2,1,0:T(8,128)S(1)} %get-tuple-element.99), channel_id=1, source_target_pairs={{0,127},{1,112},{2,113},{3,114},{4,115},{5,116},{6,117},{7,118},{8... | collective-permute-start | bytes 196616 | tf_op jit(solution)/shard_map/ppermute | solution.py:735
  48.8 1.5 %collective-permute-start.11 = (f32[4,48,128]{2,1,0:T(8,128)S(1)}, f32[4,48,128]{2,1,0:T(8,128)S(1)}, u32[]{:S(2)}, u32[]{:S(2)}) collective-permute-start(f32[4,48,128]{2,1,0:T(8,128)S(1)} %get-tuple-element.97), channel_id=1, source_target_pairs={{0,112},{16,0},{32,16},{48,32},{64,48},{80,64},{96,80},{112,96},{1... | collective-permute-start | bytes 294920 | tf_op jit(solution)/shard_map/ppermute | solution.py:727
  50.3 2.2 %shape_new.1.new_shape = bf16[16384,384]{1,0:T(8,128)(2,1)S(1)} custom-call(f32[352,128]{1,0:T(8,128)S(1)} %collective-permute-done.7.left.rxp, f32[224,128]{1,0:T(8,128)S(1)} %collective-permute-done.8.right.rxm, f32[448,128]{1,0:T(8,128)S(1)} %collective-permute-done.9.below.ryp, f32[288,128]{1,0:T(8,128)S(1)} %collective-permute-done.10.above.rym), custom_call_target="tpu_custom_call" | custom-call | flops 4000000000 | bytes 13333333 | tf_op jit(solution)/shard_map/shape_new/pallas_call | solution.py:746
  52.6 2.3 %collective-permute-done.12.rb = f32[4,48,128]{2,1,0:T(8,128)S(1)} collective-permute-done((f32[4,48,128]{2,1,0:T(8,128)S(1)}, f32[4,48,128]{2,1,0:T(8,128)S(1)}, u32[]{:S(2)}, u32[]{:S(2)}) %collective-permute-start.12) | collective-permute-done | bytes 98336 | tf_op jit(solution)/shard_map/ppermute | solution.py:729
  54.9 9.7 %collect.1 = (f32[3,32768]{1,0:T(4,128)}, f32[9,32768]{1,0:T(8,128)}, f32[256,128]{1,0:T(8,128)}, f32[3,4,4,512]{3,2,1,0:T(4,128)}, f32[4,4,512]{2,1,0:T(4,128)}) custom-call(s32[128]{0:T(128)S(1)} %copy-done.1, s32[128]{0:T(128)S(1)} %copy-done.2, s32[1,128]{1,0:T(1,128)S(1)} %get-tuple-element.74.came_s, f32[4,88,128]{2,1,0:T(8,128)S(1)} %get-tuple-element.93.ko, ...), custom_call_target="tpu_custom_call" | custom-call | flops 100000000 | bytes 333333 | tf_op jit(solution)/shard_map/collect/pallas_call | solution.py:746
  (15 shorter events, 0.1 us)
Async XLA Ops:
  4.6 8.8 %collective-permute-start.7 = (f32[352,128]{1,0:T(8,128)S(1)}, f32[352,128]{1,0:T(8,128)S(1)}, u32[]{:S(2)}, u32[]{:S(2)}) collective-permute-start(f32[352,128]{1,0:T(8,128)S(1)} %get-tuple-element.84), channel_id=1, source_target_pairs={{0,16},{16,32},{32,48},{48,64},{64,80},{80,96},{96,112},{112,0},{1... | collective-permute-start | bytes 540680 | tf_op jit(solution)/shard_map/ppermute | solution.py:727
  8.0 12.8 %collective-permute-start = (f32[432,128]{1,0:T(8,128)S(1)}, f32[432,128]{1,0:T(8,128)S(1)}, u32[]{:S(2)}, u32[]{:S(2)}) collective-permute-start(f32[432,128]{1,0:T(8,128)S(1)} %get-tuple-element.66), channel_id=1, source_target_pairs={{0,16},{16,32},{32,48},{48,64},{64,80},{80,96},{96,112},{112,0},{1... | collective-permute-start | bytes 663560 | tf_op jit(solution)/shard_map/ppermute | solution.py:727
  9.7 3.7 %collective-permute-start.8 = (f32[224,128]{1,0:T(8,128)S(1)}, f32[224,128]{1,0:T(8,128)S(1)}, u32[]{:S(2)}, u32[]{:S(2)}) collective-permute-start(f32[224,128]{1,0:T(8,128)S(1)} %get-tuple-element.85), channel_id=1, source_target_pairs={{0,112},{16,0},{32,16},{48,32},{64,48},{80,64},{96,80},{112,96},{1... | collective-permute-start | bytes 344072 | tf_op jit(solution)/shard_map/ppermute | solution.py:727
  11.0 9.8 %collective-permute-start.1 = (f32[432,128]{1,0:T(8,128)S(1)}, f32[432,128]{1,0:T(8,128)S(1)}, u32[]{:S(2)}, u32[]{:S(2)}) collective-permute-start(f32[432,128]{1,0:T(8,128)S(1)} %get-tuple-element.68), channel_id=1, source_target_pairs={{0,112},{16,0},{32,16},{48,32},{64,48},{80,64},{96,80},{112,96},{1... | collective-permute-start | bytes 663560 | tf_op jit(solution)/shard_map/ppermute | solution.py:727
  13.5 21.1 %collective-permute-start.10 = (f32[288,128]{1,0:T(8,128)S(1)}, f32[288,128]{1,0:T(8,128)S(1)}, u32[]{:S(2)}, u32[]{:S(2)}) collective-permute-start(f32[288,128]{1,0:T(8,128)S(1)} %get-tuple-element.87), channel_id=1, source_target_pairs={{0,15},{1,0},{2,1},{3,2},{4,3},{5,4},{6,5},{7,6},{8,7},{9,8},{10,9... | collective-permute-start | bytes 442376 | tf_op jit(solution)/shard_map/ppermute | solution.py:729
  20.8 13.8 %collective-permute-start.9 = (f32[448,128]{1,0:T(8,128)S(1)}, f32[448,128]{1,0:T(8,128)S(1)}, u32[]{:S(2)}, u32[]{:S(2)}) collective-permute-start(f32[448,128]{1,0:T(8,128)S(1)} %get-tuple-element.86), channel_id=1, source_target_pairs={{0,1},{1,2},{2,3},{3,4},{4,5},{5,6},{6,7},{7,8},{8,9},{9,10},{10,1... | collective-permute-start | bytes 688136 | tf_op jit(solution)/shard_map/ppermute | solution.py:729
  20.9 16.3 %copy-start = (s32[16384]{0:T(1024)S(1)}, s32[16384]{0:T(1024)}, u32[]{:S(2)}) copy-start(s32[16384]{0:T(1024)} %param.20) | copy-start | bytes 196612
  20.9 15.3 %collective-permute-start.2 = (f32[432,128]{1,0:T(8,128)S(1)}, f32[432,128]{1,0:T(8,128)S(1)}, u32[]{:S(2)}, u32[]{:S(2)}) collective-permute-start(f32[432,128]{1,0:T(8,128)S(1)} %get-tuple-element.72), channel_id=1, source_target_pairs={{0,1},{1,2},{2,3},{3,4},{4,5},{5,6},{6,7},{7,8},{8,9},{9,10},{10,1... | collective-permute-start | bytes 663560 | tf_op jit(solution)/shard_map/ppermute | solution.py:729
  21.0 15.2 %collective-permute-start.3 = (f32[432,128]{1,0:T(8,128)S(1)}, f32[432,128]{1,0:T(8,128)S(1)}, u32[]{:S(2)}, u32[]{:S(2)}) collective-permute-start(f32[432,128]{1,0:T(8,128)S(1)} %get-tuple-element.73), channel_id=1, source_target_pairs={{0,15},{1,0},{2,1},{3,2},{4,3},{5,4},{6,5},{7,6},{8,7},{9,8},{10,9... | collective-permute-start | bytes 663560 | tf_op jit(solution)/shard_map/ppermute | solution.py:729
  36.9 18.0 %copy-start.1 = (s32[128]{0:T(128)S(1)}, s32[128]{0:T(128)}, u32[]{:S(2)}) copy-start(s32[128]{0:T(128)} %code_s.1) | copy-start | bytes 1540
  36.9 18.0 %copy-start.2 = (s32[128]{0:T(128)S(1)}, s32[128]{0:T(128)}, u32[]{:S(2)}) copy-start(s32[128]{0:T(128)} %brick_s.1) | copy-start | bytes 1540
  37.0 9.6 %collective-permute-start.6 = (f32[4,48,128]{2,1,0:T(8,128)S(1)}, f32[4,48,128]{2,1,0:T(8,128)S(1)}, u32[]{:S(2)}, u32[]{:S(2)}) collective-permute-start(f32[4,48,128]{2,1,0:T(8,128)S(1)} %get-tuple-element.82), channel_id=1, source_target_pairs={{0,17},{1,18},{2,19},{3,20},{4,21},{5,22},{6,23},{7,24},{8,25},{9,... | collective-permute-start | bytes 294920 | tf_op jit(solution)/shard_map/ppermute | solution.py:735
  37.0 9.6 %collective-permute-start.4 = (f32[4,56,128]{2,1,0:T(8,128)S(1)}, f32[4,56,128]{2,1,0:T(8,128)S(1)}, u32[]{:S(2)}, u32[]{:S(2)}) collective-permute-start(f32[4,56,128]{2,1,0:T(8,128)S(1)} %get-tuple-element.80), channel_id=1, source_target_pairs={{0,16},{16,32},{32,48},{48,64},{64,80},{80,96},{96,112},{112,0},{1... | collective-permute-start | bytes 344072 | tf_op jit(solution)/shard_map/ppermute | solution.py:727
  37.1 10.0 %collective-permute-start.5 = (f32[4,56,128]{2,1,0:T(8,128)S(1)}, f32[4,56,128]{2,1,0:T(8,128)S(1)}, u32[]{:S(2)}, u32[]{:S(2)}) collective-permute-start(f32[4,56,128]{2,1,0:T(8,128)S(1)} %get-tuple-element.81), channel_id=1, source_target_pairs={{0,1},{1,2},{2,3},{3,4},{4,5},{5,6},{6,7},{7,8},{8,9},{9,10},{10,1... | collective-permute-start | bytes 344072 | tf_op jit(solution)/shard_map/ppermute | solution.py:729
  47.3 5.2 %collective-permute-start.13 = (f32[4,32,128]{2,1,0:T(8,128)S(1)}, f32[4,32,128]{2,1,0:T(8,128)S(1)}, u32[]{:S(2)}, u32[]{:S(2)}) collective-permute-start(f32[4,32,128]{2,1,0:T(8,128)S(1)} %get-tuple-element.99), channel_id=1, source_target_pairs={{0,127},{1,112},{2,113},{3,114},{4,115},{5,116},{6,117},{7,118},{8... | collective-permute-start | bytes 196616 | tf_op jit(solution)/shard_map/ppermute | solution.py:735
  48.8 3.8 %collective-permute-start.11 = (f32[4,48,128]{2,1,0:T(8,128)S(1)}, f32[4,48,128]{2,1,0:T(8,128)S(1)}, u32[]{:S(2)}, u32[]{:S(2)}) collective-permute-start(f32[4,48,128]{2,1,0:T(8,128)S(1)} %get-tuple-element.97), channel_id=1, source_target_pairs={{0,112},{16,0},{32,16},{48,32},{64,48},{80,64},{96,80},{112,96},{1... | collective-permute-start | bytes 294920 | tf_op jit(solution)/shard_map/ppermute | solution.py:727
  50.3 4.6 %collective-permute-start.12 = (f32[4,48,128]{2,1,0:T(8,128)S(1)}, f32[4,48,128]{2,1,0:T(8,128)S(1)}, u32[]{:S(2)}, u32[]{:S(2)}) collective-permute-start(f32[4,48,128]{2,1,0:T(8,128)S(1)} %get-tuple-element.98), channel_id=1, source_target_pairs={{0,15},{1,0},{2,1},{3,2},{4,3},{5,4},{6,5},{7,6},{8,7},{9,8},{10,9... | collective-permute-start | bytes 294920 | tf_op jit(solution)/shard_map/ppermute | solution.py:729
